TPU v7x, 256 devices: a whole 4x4x8 slice. The times are simulated.
256 devices in a mesh: ctx: 32 (over z, x_hi, core), head: 8 (over y, x_lo).
Axes of the slice: x: 4 (x_hi: 2, x_lo: 2; x = x_hi * 2 + x_lo), y: 4, z: 8, core: 2. Of those that a mesh axis runs over, the one named last changes fastest.
Arguments:
- inputs: bfloat16 [4096, 4096], P('ctx', 'head'), may hold values from -60 to 60
- out_grad: bfloat16 [4096, 4096], P('ctx', 'head'), may hold values from -6 to 6
- norm_gain: float32 [4096], replicated, may hold values from 0.5 to 1.5
- w_query: bfloat16 [4096, 4096], P(None, 'head'), may hold values from -2 to 2
- w_key: bfloat16 [4096, 1024], P(None, 'head'), may hold values from -2 to 2
- w_value: bfloat16 [4096, 1024], P(None, 'head'), may hold values from -0.09375 to 0.09375
- w_out: bfloat16 [4096, 4096], P('head'), may hold values from -0.09375 to 0.09375
- record_lengths: int32 [8], replicated, may hold values from 1 to 2048, 4096 in all
- block_order: int32 [64], replicated, may hold values from 0 to 63, each once
Outputs:
- input_grad: bfloat16 [4096, 4096], P('ctx', 'head')
- saliency: float32 [4096], P('ctx')
Inputs may be any that keep to these rules, and one draw needn't show every extreme that they name: `record_lengths`: record lengths sum to 4096. `block_order`: each number once.
All inputs are finite; a program needn't handle non-finite values.
Results may differ from a plain program's by a relative error of at most 0.007.
Values may be sent and summed in bfloat16 or wider, within the bound.
No kernel may reach another device: no remote copies, remote signals or barrier semaphores. Data moves between devices by JAX's collectives and lax.ppermute only.
A program may use at most 128 MiB of HBM per device.

v0:
```python
import functools

import jax
import jax.numpy as jnp
from jax import lax
from jax.experimental import pallas as pl
from jax.experimental.pallas import tpu as pltpu
from jax.sharding import PartitionSpec as P

D = 4096
HEAD_DIM = 128
BLOCK = 64
ROWS = 128
SHARE = 512
HEADS = 4
GROUPS = 8
RECORDS = 8
KEYS = 1024
WIDE = 2 * HEAD_DIM
EPS = 1e-05
SCALE = HEAD_DIM ** (-0.5)
LOG2E = 1.4426950408889634
NEG = -1e30
KS = (0, 7, 6, 3, 5, 4, 2, 1)
BACK = (1, 2, 4, 5, 3, 6, 7)
EXTRA = 16
QUAD, RING = 4, 8
SIDE = 3

f32, bf16 = jnp.float32, jnp.bfloat16
NT = (((1,), (1,)), ((), ()))
NN = (((1,), (0,)), ((), ()))
TT = (((0,), (1,)), ((), ()))


def mm(a, b, dims=NN):
    return lax.dot_general(a, b, dims, preferred_element_type=f32)


def tree(parts):
    while len(parts) > 1:
        parts = [parts[i] + parts[i + 1] for i in range(0, len(parts), 2)]
    return parts[0]


def vmem(n):
    return [pl.BlockSpec(memory_space=pltpu.VMEM)] * n


def smem(n):
    return [pl.BlockSpec(memory_space=pltpu.SMEM)] * n


def call(body, scalars, arrays, outs, mib, flops=0, moved=0, exps=0, scratch=(), name=None):
    return pl.pallas_call(
        body,
        out_shape=outs,
        in_specs=smem(len(scalars)) + vmem(len(arrays)),
        out_specs=jax.tree.map(lambda _: pl.BlockSpec(memory_space=pltpu.VMEM), outs),
        scratch_shapes=list(scratch),
        compiler_params=pltpu.CompilerParams(vmem_limit_bytes=mib << 20),
        cost_estimate=pl.CostEstimate(flops=flops, bytes_accessed=moved, transcendentals=exps),
        name=name,
    )(*scalars, *arrays)


def shape(dims, dtype):
    return jax.ShapeDtypeStruct(dims, dtype)


def spot(head, k):
    return pl.multiple_of(lax.bitwise_xor(head, k) * SHARE, SHARE)


def in_order(ks, refs):
    return [ref for _, ref in sorted(zip(ks, refs), key=lambda pair: pair[0])]


def as_row(column):
    return jnp.transpose(jnp.broadcast_to(column, (ROWS, ROWS)))[:8]


def touch_kernel(*refs):
    refs[-1][...] = jnp.zeros((8, ROWS), f32)


def hold_kernel(own, other, *refs):
    both = refs[-1]
    both[:ROWS, :] = own[...]
    both[ROWS:, :] = other[...]


def norm_kernel(ids, *refs):
    xs = in_order(KS, refs[:GROUPS])
    gain, w_key, w_value, _, kv, normed, mean, mean_row = refs[GROUPS:]
    head = ids[1]
    squares = []
    for x in xs:
        wide = x[...].astype(f32)
        squares.append(jnp.sum(wide * wide, axis=1, keepdims=True))
    average = tree(squares) * (1.0 / D)
    mean[...] = jnp.broadcast_to(average, (ROWS, ROWS))
    mean_row[...] = as_row(average)
    inverse = 1.0 / jnp.sqrt(average + EPS)
    for k, x in enumerate(xs):
        at = pl.ds(spot(head, k), SHARE)
        normed[:, at] = (x[...].astype(f32) * inverse * gain[:, at]).astype(bf16)
    kv[:, :HEAD_DIM] = mm(normed[...], w_key[...]).astype(bf16)
    kv[:, HEAD_DIM:] = mm(normed[...], w_value[...]).astype(bf16)


def project_kernel(ids, *refs):
    xs, dys, (w_out, normed, w_query) = in_order(KS, refs[:GROUPS]), refs[GROUPS : GROUPS + 4], refs[GROUPS + 4 : GROUPS + 7]
    both, dot_row = refs[-2:]
    head = ids[1]
    total = jnp.zeros((ROWS, SHARE), f32)
    parts = []
    for k, x in enumerate(xs):
        dy = dys[k // 2][(k % 2) * ROWS : (k % 2 + 1) * ROWS, :]
        total = total + mm(dy, w_out[:, pl.ds(spot(head, k), SHARE)], NT)
        parts.append(jnp.sum(x[...].astype(f32) * dy.astype(f32), axis=1, keepdims=True))
    both[:ROWS, :] = mm(normed[...], w_query[...]).astype(bf16)
    both[ROWS:, :] = total.astype(bf16)
    dot_row[...] = as_row(tree(parts))


def group(n):
    return slice(n * ROWS, (n + 1) * ROWS)


def lanes(x, op):
    return functools.reduce(op, [x[:, group(n)] for n in range(x.shape[1] // ROWS)])


def stack(ref, blocks):
    for b, block in enumerate(blocks):
        for h in range(HEADS):
            ref[group(b * HEADS + h), :] = block[:, group(h)]


def slot(core):
    return pl.ds(pl.multiple_of(core * ROWS, ROWS), ROWS)


def join_kernel(ids, mine, other, both):
    core = ids[0] % 2
    both[slot(core), :] = mine[...]
    both[slot(1 - core), :] = other[...]


def sort_kernel(ids, *refs):
    core = ids[0] % 2
    for n, ref in enumerate(refs[:SIDE]):
        refs[-1][group(n), :] = ref[slot(1 - core), :]


def softmax_kernel(ids, order, lengths, *refs):
    projections, (kv, across, *near, others) = refs[:QUAD], refs[QUAD : QUAD + SIDE + 3]
    powers, stats, key, value, stacked = refs[QUAD + SIDE + 3 :]
    ctx = ids[0]
    z, place_in_quad, core = ctx // QUAD, ctx % QUAD, ctx % 2
    lane = lax.broadcasted_iota(jnp.int32, (1, ROWS), 1)
    row = lax.broadcasted_iota(jnp.int32, (ROWS, 1), 0)

    def places(owner, i):
        first, second = order[2 * owner] * BLOCK, order[2 * owner + 1] * BLOCK - BLOCK
        return jnp.where(i < BLOCK, first + i, second + i)

    sign = 1 - 2 * core
    blocks = [(kv[...], 0), (across[...], RING // 2)]
    blocks += [(ref[slot(core), :], sign * (n + 1)) for n, ref in enumerate(near)]
    blocks += [(others[group(n), :], -sign * (n + 1)) for n in range(SIDE)]
    found = []
    for n, (block, hop) in enumerate(blocks):
        key[group(n), :] = block[:, :HEAD_DIM]
        value[group(n), :] = block[:, HEAD_DIM:]
        found.append(places(((z + RING - hop) % RING) * QUAD + place_in_quad, lane))
    place = jnp.concatenate(found, axis=1)
    stack(stacked, [p.at[:ROWS, :] for p in projections])
    packed = jnp.zeros((ROWS, ROWS), f32)
    spots = lax.broadcasted_iota(jnp.int32, (ROWS, ROWS), 1)
    for b in range(QUAD):
        mine = places(lax.bitwise_xor(ctx, b), row)
        low = jnp.zeros((ROWS, 1), jnp.int32)
        start = 0
        for r in range(RECORDS):
            low = jnp.where(mine >= start, start, low)
            start = start + lengths[r]
        seen = (place <= mine) & (place >= low)
        scores = mm(stacked[b * SHARE : (b + 1) * SHARE, :], key[...], NT)
        for h in range(HEADS):
            n = b * HEADS + h
            masked = jnp.where(seen, scores[group(h)], NEG)
            shift = jnp.max(lanes(masked, jnp.maximum), axis=1, keepdims=True) * (SCALE * LOG2E)
            power = jnp.exp2(masked * (SCALE * LOG2E) - shift)
            total = jnp.sum(lanes(power, jnp.add), axis=1, keepdims=True)
            half = power.astype(bf16)
            powers[group(n), :] = half
            mixed = mm(half, value[...])
            dot = jnp.sum(projections[b][ROWS:, group(h)].astype(f32) * mixed, axis=1, keepdims=True)
            for m, column in enumerate((shift, total, dot)):
                packed = jnp.where(spots == QUAD * HEADS * m + n, column, packed)
    stats[...] = packed


def gradient_kernel(*refs):
    projections, (key, value, powers), parts = refs[:QUAD], refs[QUAD : QUAD + 3], refs[QUAD + 3 : 2 * QUAD + 3]
    queries, dirs = [p.at[:ROWS, :] for p in projections], [p.at[ROWS:, :] for p in projections]
    own, across, near, others, dq_own, dq_send, grad, query_t, dirs_n, dirs_t = refs[2 * QUAD + 3 :]
    outs = [own, across] + [near.at[n] for n in range(SIDE)] + [others.at[n] for n in range(SIDE)]
    lane = lax.broadcasted_iota(jnp.int32, (ROWS, ROWS), 1)
    groups = QUAD * HEADS

    def toward(x, n):
        return pltpu.roll(x, (ROWS - n) % ROWS, 1)

    def swap(x, n):
        return jnp.where(lane & n == 0, toward(x, n), toward(x, -n))

    same = []
    for r in range(QUAD):
        x = parts[r][...]
        for bit in (1, 2):
            if r & bit:
                x = swap(x, bit * HEADS)
        same.append(x)
    top = functools.reduce(jnp.maximum, same)
    weights = [jnp.exp2(jnp.where(lane < groups, x - top, 0.0)) for x in same]
    total = functools.reduce(jnp.add, [w * toward(x, groups) for w, x in zip(weights, same)])
    total = jnp.where(lane < groups, total, 1.0)
    dot = functools.reduce(jnp.add, [w * toward(x, 2 * groups) for w, x in zip(weights, same)])
    factors = weights[0] / total
    shifts = dot / total * factors
    shifted = []
    for b in range(QUAD):
        for h in range(HEADS):
            n = b * HEADS + h
            shifted.append(shifts[:, n : n + 1])
            scaled = dirs[b][:, group(h)].astype(f32) * factors[:, n : n + 1]
            dirs_n[group(n), :] = scaled.astype(bf16)
            dirs_t[:, group(n)] = jnp.transpose(scaled).astype(bf16)
            query_t[:, group(n)] = jnp.transpose(queries[b][:, group(h)].astype(f32)).astype(bf16)
    for b in (1, 3, 0, 2):
        rows = slice(b * SHARE, (b + 1) * SHARE)
        slope = mm(dirs_n[rows, :], value[...], NT)
        for h in range(HEADS):
            n = b * HEADS + h
            grad[group(n), :] = (powers[group(n), :].astype(f32) * (slope[group(h)] - shifted[n])).astype(bf16)
        query_grad = mm(grad[rows, :], key[...]) * SCALE
        for h in range(HEADS):
            if b % 2:
                dq_send[group(b // 2), group(h)] = query_grad[group(h)].astype(bf16)
            else:
                dq_own[group(b // 2), group(h)] = query_grad[group(h)]
    for t in range(2):
        at = slice(t * SHARE, (t + 1) * SHARE)
        key_part = mm(query_t[...], grad[:, at]) * SCALE
        value_part = mm(dirs_t[...], powers[:, at])
        for n in range(SHARE // ROWS):
            out = outs[t * (SHARE // ROWS) + n]
            out[:HEAD_DIM, :] = key_part[:, group(n)].astype(bf16)
            out[HEAD_DIM:, :] = value_part[:, group(n)].astype(bf16)


def pair_kernel(ids, near, got, *sends):
    core = ids[0] % 2
    for n, send in enumerate(sends):
        send[core] = near[n]
        send[1 - core] = got[n]


def sum_kernel(ids, *refs):
    core = ids[0] % 2
    parts, (own, across, keep, send) = refs[:SIDE], refs[SIDE:]
    mine = functools.reduce(jnp.add, [p[core].astype(f32) for p in parts])
    keep[...] = own[...].astype(f32) + across[...].astype(f32) + mine
    send[...] = functools.reduce(jnp.add, [p[1 - core].astype(f32) for p in parts]).astype(bf16)


def add_kernel(own, got, stay, send):
    stay[...] = own[:ROWS, :] + got[:ROWS, :].astype(f32)
    send[...] = (own[ROWS:, :] + got[ROWS:, :].astype(f32)).astype(bf16)


def back_query_kernel(stay, got, w_query, hidden):
    query_grad = (stay[...] + got[...].astype(f32)).astype(bf16)
    for k in range(GROUPS):
        at = slice(k * SHARE, (k + 1) * SHARE)
        hidden[:, at] = mm(query_grad, w_query[at, :], NT)


def back_kernel(ids, *refs):
    grads, xs = refs[:2], in_order(KS, refs[2 : 2 + GROUPS])
    gain, hidden, w_key, w_value, own, own_row, *sends = refs[2 + GROUPS :]
    head = ids[1]
    both = functools.reduce(lambda a, b: a + b, [g[...].astype(f32) for g in grads]).astype(bf16)
    key_grad, value_grad = both[:HEAD_DIM], both[HEAD_DIM:]
    inner = []
    for k, x in enumerate(xs):
        at = pl.ds(spot(head, k), SHARE)
        block = hidden[:, at] + mm(key_grad, w_key[at, :], TT) + mm(value_grad, w_value[at, :], TT)
        inner.append(jnp.sum(x[...].astype(f32) * gain[:, at] * block, axis=1, keepdims=True))
        if k == 0:
            own[...] = block
        else:
            sends[k - 1][:ROWS, :] = block.astype(bf16)
    row = jnp.transpose(jnp.broadcast_to(tree(inner), (ROWS, ROWS)))[:EXTRA]
    high = row.astype(bf16)
    lower = (row - high.astype(f32)).astype(bf16)
    own_row[:, :ROWS] = high
    own_row[:, ROWS:] = lower
    for send in sends:
        send[ROWS:, :] = jnp.zeros((EXTRA, SHARE), bf16)
        send[ROWS:, :ROWS] = high
        send[ROWS:, ROWS : 2 * ROWS] = lower


def last_kernel(ids, own, own_row, *refs):
    got = in_order(BACK, refs[: GROUPS - 1])
    x, dy, gain, mean, mean_row, dot_row, input_grad, saliency = refs[GROUPS - 1 :]
    head = ids[1]
    hidden = functools.reduce(lambda a, b: a + b, [g[:ROWS, :].astype(f32) for g in got], own[...])

    def term(ref, at):
        return ref[at : at + EXTRA, :ROWS].astype(f32) + ref[at : at + EXTRA, ROWS : 2 * ROWS].astype(f32)

    total_row = tree([term(own_row, 0)] + [term(g, ROWS) for g in got])[:8]
    root_row = jnp.sqrt(mean_row[...] + EPS)
    inner_row = total_row / (root_row * D)
    sums = dot_row[...] + (total_row - inner_row * (mean_row[...] * D) / root_row) / root_row
    saliency[...] = sums[:1]
    inner = jnp.transpose(jnp.broadcast_to(inner_row[:1], (ROWS, ROWS)))
    inverse = 1.0 / jnp.sqrt(mean[...] + EPS)
    for n in range(SHARE // ROWS):
        at = slice(n * ROWS, (n + 1) * ROWS)
        unit = x[:, at].astype(f32) * inverse
        scaled = hidden[:, at] * gain[:, pl.ds(pl.multiple_of(head * SHARE + n * ROWS, ROWS), ROWS)]
        input_grad[:, at] = (dy[:, at].astype(f32) + (scaled - unit * inner) * inverse).astype(bf16)


def xor_head(a, k):
    return lax.ppermute(a, "head", [(i, i ^ k) for i in range(GROUPS)])


def xor_ctx(a, k):
    return lax.ppermute(a, "ctx", [(i, i ^ k) for i in range(32)])


def touch(arrays):
    return call(touch_kernel, [], arrays, shape((8, ROWS), f32), 16, moved=6 << 20, name="touch")


def turn(a, k):
    return lax.ppermute(a, "ctx", [(i, (i + 4 * k) % 32) for i in range(32)])


def apart(a, k):
    return lax.ppermute(a, "ctx", [(i, (i + 4 * k * (1 - 2 * (i % 2))) % 32) for i in range(32)])


def spread(a):
    across = xor_ctx(a, 2)
    return [a, xor_ctx(a, 1), across, xor_ctx(across, 1)]


def local(inputs, out_grad, norm_gain, w_query, w_key, w_value, w_out, record_lengths, block_order):
    ids = jnp.stack([lax.axis_index("ctx"), lax.axis_index("head")]).astype(jnp.int32)
    gain = norm_gain.reshape(1, D)
    xs = [xor_head(inputs, k) if k else inputs for k in KS]
    ready = touch([w_key, w_value, gain])
    kv, normed, mean, mean_row = call(
        norm_kernel,
        [ids],
        [*xs, gain, w_key, w_value, ready],
        [
            shape((ROWS, WIDE), bf16),
            shape((ROWS, D), bf16),
            shape((ROWS, ROWS), f32),
            shape((8, ROWS), f32),
        ],
        16,
        flops=2 * ROWS * D * WIDE,
        moved=5 << 20,
        name="norm_kv",
    )
    both = call(join_kernel, [ids], [kv, xor_ctx(kv, 1)], shape((2 * ROWS, WIDE), bf16), 4, moved=1 << 18, name="join")
    near = [apart(both, n) for n in range(1, SIDE + 1)]
    kvs = [kv, turn(kv, RING // 2), *near]
    given = call(sort_kernel, [ids], [*near, kvs[1]], shape((SIDE * ROWS, WIDE), bf16), 4, moved=1 << 19, name="sort")
    kvs.append(xor_ctx(given, 1))
    held = call(
        hold_kernel,
        [],
        [out_grad, xor_head(out_grad, 1), kv],
        shape((2 * ROWS, SHARE), bf16),
        4,
        moved=1 << 19,
        name="hold",
    )
    dys = [held] + [xor_head(held, k) for k in (2, 4, 6)]
    ready_out = touch([w_out, w_query, normed])
    projected, dot_row = call(
        project_kernel,
        [ids],
        [*xs, *dys, w_out, normed, w_query, ready_out, kvs[1], near[2]],
        [shape((2 * ROWS, SHARE), bf16), shape((8, ROWS), f32)],
        24,
        flops=4 * ROWS * D * SHARE,
        moved=10 << 20,
        name="project",
    )
    projections = spread(projected)
    tall = QUAD * HEADS * ROWS
    powers, stats, key, value = call(
        softmax_kernel,
        [ids, block_order, record_lengths],
        [*projections, *kvs],
        [
            shape((tall, KEYS), bf16),
            shape((ROWS, ROWS), f32),
            shape((KEYS, HEAD_DIM), bf16),
            shape((KEYS, HEAD_DIM), bf16),
        ],
        24,
        flops=4 * tall * KEYS * HEAD_DIM,
        moved=6 << 20,
        exps=tall * KEYS,
        scratch=[pltpu.VMEM((tall, HEAD_DIM), bf16)],
        name="softmax",
    )
    parts = spread(stats)
    part = shape((WIDE, HEAD_DIM), bf16)
    side = shape((SIDE, WIDE, HEAD_DIM), bf16)
    own, across, near, others, dq_own, dq_send = call(
        gradient_kernel,
        [],
        [*projections, key, value, powers, *parts],
        [part, part, side, side, shape((2 * ROWS, SHARE), f32), shape((2 * ROWS, SHARE), bf16)],
        32,
        flops=8 * tall * KEYS * HEAD_DIM,
        moved=6 << 20,
        scratch=[
            pltpu.VMEM((tall, KEYS), bf16),
            pltpu.VMEM((HEAD_DIM, tall), bf16),
            pltpu.VMEM((tall, HEAD_DIM), bf16),
            pltpu.VMEM((HEAD_DIM, tall), bf16),
        ],
        name="gradient",
    )
    sends = call(
        pair_kernel,
        [ids],
        [near, xor_ctx(others, 1)],
        [shape((2, WIDE, HEAD_DIM), bf16)] * SIDE,
        8,
        moved=1 << 20,
        name="pair",
    )
    keep, give = call(
        sum_kernel,
        [ids],
        [*[apart(a, -n) for n, a in enumerate(sends, 1)], own, turn(across, RING // 2)],
        [shape((WIDE, HEAD_DIM), f32), part],
        8,
        moved=1 << 20,
        name="sum",
    )
    grads = [keep, xor_ctx(give, 1)]
    stay, dq_far = call(
        add_kernel,
        [],
        [dq_own, xor_ctx(dq_send, 1)],
        [shape((ROWS, SHARE), f32), shape((ROWS, SHARE), bf16)],
        16,
        flops=4 * ROWS * SHARE,
        moved=2 << 20,
        name="add",
    )
    hidden = call(
        back_query_kernel,
        [],
        [stay, xor_ctx(dq_far, 2), w_query],
        shape((ROWS, D), f32),
        16,
        flops=2 * ROWS * D * SHARE,
        moved=6 << 20,
        name="back_query",
    )
    own, own_row, *sends = call(
        back_kernel,
        [ids],
        [*grads, *xs, gain, hidden, w_key, w_value],
        [shape((ROWS, SHARE), f32), shape((EXTRA, WIDE), bf16)]
        + [shape((ROWS + EXTRA, SHARE), bf16)] * (GROUPS - 1),
        24,
        flops=2 * ROWS * D * WIDE,
        moved=7 << 20,
        name="back_kv",
    )
    home = [xor_head(sends[k - 1], k) for k in BACK]
    input_grad, saliency = call(
        last_kernel,
        [ids],
        [own, own_row, *home, inputs, out_grad, gain, mean, mean_row, dot_row],
        [shape((ROWS, SHARE), bf16), shape((1, ROWS), f32)],
        16,
        flops=10 * ROWS * SHARE,
        moved=3 << 20,
        name="last",
    )
    return (input_grad, saliency.reshape(ROWS))


def solution(mesh):
    placed = (
        P("ctx", "head"),
        P("ctx", "head"),
        P(),
        P(None, "head"),
        P(None, "head"),
        P(None, "head"),
        P("head", None),
        P(),
        P(),
    )
    return jax.shard_map(
        local, mesh=mesh, in_specs=placed, out_specs=(P("ctx", "head"), P("ctx")), check_vma=False
    )
```

profile of v0, /device:TPU:32, one launch (start us, length us, event | category | flops | bytes accessed | tf_op | source)
XLA Modules:
  0.0 124.1 jit_solution(12075542934206806097)
XLA Ops:
  0.6 1.6 %collective-permute-start.6 = (bf16[128,512]{1,0:T(8,128)(2,1)}, bf16[128,512]{1,0:T(8,128)(2,1)S(1)}, u32[]{:S(2)}, u32[]{:S(2)}) collective-permute-start(bf16[128,512]{1,0:T(8,128)(2,1)} %refs_7_.1), channel_id=1, source_target_pairs={{0,1},{1,0},{2,3},{3,2},{4,5},{5,4},{6,7},{7,6},{8,9},{9,8},{10,11... | collective-permute-start | bytes 393224 | tf_op jit(solution)/shard_map/ppermute | solution.py:342
  2.2 1.6 %collective-permute-start.5 = (bf16[128,512]{1,0:T(8,128)(2,1)}, bf16[128,512]{1,0:T(8,128)(2,1)S(1)}, u32[]{:S(2)}, u32[]{:S(2)}) collective-permute-start(bf16[128,512]{1,0:T(8,128)(2,1)} %refs_7_.1), channel_id=1, source_target_pairs={{0,2},{1,3},{2,0},{3,1},{4,6},{5,7},{6,4},{7,5},{8,10},{9,11},{10,... | collective-permute-start | bytes 393224 | tf_op jit(solution)/shard_map/ppermute | solution.py:342
  3.8 2.9 %collective-permute-start.4 = (bf16[128,512]{1,0:T(8,128)(2,1)}, bf16[128,512]{1,0:T(8,128)(2,1)S(1)}, u32[]{:S(2)}, u32[]{:S(2)}) collective-permute-start(bf16[128,512]{1,0:T(8,128)(2,1)} %refs_7_.1), channel_id=1, source_target_pairs={{0,4},{1,5},{2,6},{3,7},{4,0},{5,1},{6,2},{7,3},{8,12},{9,13},{10,... | collective-permute-start | bytes 393224 | tf_op jit(solution)/shard_map/ppermute | solution.py:342
  6.7 0.6 collective-permute-start.3
  7.3 1.4 %collective-permute-start.2 = (bf16[128,512]{1,0:T(8,128)(2,1)}, bf16[128,512]{1,0:T(8,128)(2,1)S(1)}, u32[]{:S(2)}, u32[]{:S(2)}) collective-permute-start(bf16[128,512]{1,0:T(8,128)(2,1)} %refs_7_.1), channel_id=1, source_target_pairs={{0,3},{1,2},{2,1},{3,0},{4,7},{5,6},{6,5},{7,4},{8,11},{9,10},{10,... | collective-permute-start | bytes 393224 | tf_op jit(solution)/shard_map/ppermute | solution.py:342
  8.7 3.0 %collective-permute-start.1 = (bf16[128,512]{1,0:T(8,128)(2,1)}, bf16[128,512]{1,0:T(8,128)(2,1)S(1)}, u32[]{:S(2)}, u32[]{:S(2)}) collective-permute-start(bf16[128,512]{1,0:T(8,128)(2,1)} %refs_7_.1), channel_id=1, source_target_pairs={{0,6},{1,7},{2,4},{3,5},{4,2},{5,3},{6,0},{7,1},{8,14},{9,15},{10,... | collective-permute-start | bytes 393224 | tf_op jit(solution)/shard_map/ppermute | solution.py:342
  11.7 4.0 %collective-permute-start = (bf16[128,512]{1,0:T(8,128)(2,1)}, bf16[128,512]{1,0:T(8,128)(2,1)S(1)}, u32[]{:S(2)}, u32[]{:S(2)}) collective-permute-start(bf16[128,512]{1,0:T(8,128)(2,1)} %refs_7_.1), channel_id=1, source_target_pairs={{0,7},{1,6},{2,5},{3,4},{4,3},{5,2},{6,1},{7,0},{8,15},{9,14},{10,... | collective-permute-start | bytes 393224 | tf_op jit(solution)/shard_map/ppermute | solution.py:342
  15.7 1.4 %copy-done.3 = bf16[4096,128]{1,0:T(8,128)(2,1)S(1)} copy-done((bf16[4096,128]{1,0:T(8,128)(2,1)S(1)}, bf16[4096,128]{1,0:T(8,128)(2,1)}, u32[]{:S(2)}) %copy-start.3) | copy-done | bytes 1048600
  17.1 1.4 %copy-done.5 = bf16[4096,128]{1,0:T(8,128)(2,1)S(1)} copy-done((bf16[4096,128]{1,0:T(8,128)(2,1)S(1)}, bf16[4096,128]{1,0:T(8,128)(2,1)}, u32[]{:S(2)}) %copy-start.5) | copy-done | bytes 1048600
  18.5 0.7 copy-done.11
  19.2 1.5 %collective-permute-start.7 = (bf16[128,512]{1,0:T(8,128)(2,1)}, bf16[128,512]{1,0:T(8,128)(2,1)S(1)}, u32[]{:S(2)}, u32[]{:S(2)}) collective-permute-start(bf16[128,512]{1,0:T(8,128)(2,1)} %refs_8_.1), channel_id=1, source_target_pairs={{0,1},{1,0},{2,3},{3,2},{4,5},{5,4},{6,7},{7,6},{8,9},{9,8},{10,11... | collective-permute-start | bytes 393224 | tf_op jit(solution)/shard_map/ppermute | solution.py:342
  20.8 0.1 collective-permute-done.1.refs_2_.refs_4_
  20.9 0.9 copy-done.7
  21.8 1.8 %norm_kv.1 = (bf16[128,256]{1,0:T(8,128)(2,1)S(1)}, bf16[128,4096]{1,0:T(8,128)(2,1)S(1)}, f32[128,128]{1,0:T(8,128)S(1)}, f32[8,128]{1,0:T(8,128)S(1)}) custom-call(s32[2]{0:T(128)S(1)} %pad_add_fusion.ids, bf16[128,512]{1,0:T(8,128)(2,1)S(1)} %copy-done.7, bf16[128,512]{1,0:T(8,128)(2,1)S(1)} %collective-permute-done.refs_1_.refs_3_, ...), custom_call_target="tpu_custom_call" | custom-call | flops 268435456 | bytes 5242880 | tf_op jit(solution)/shard_map/norm_kv/pallas_call | solution.py:55
  23.6 0.7 collective-permute-done.7.other
  24.4 0.9 copy-done.9
  25.3 1.9 %collective-permute-start.10 = (bf16[256,512]{1,0:T(8,128)(2,1)S(1)}, bf16[256,512]{1,0:T(8,128)(2,1)S(1)}, u32[]{:S(2)}, u32[]{:S(2)}) collective-permute-start(bf16[256,512]{1,0:T(8,128)(2,1)S(1)} %hold.1.refs_8_), channel_id=1, source_target_pairs={{0,6},{1,7},{2,4},{3,5},{4,2},{5,3},{6,0},{7,1},{8,14},{9,15},{10,... | collective-permute-start | bytes 786440 | tf_op jit(solution)/shard_map/ppermute | solution.py:342
  27.2 0.9 collective-permute-start.9
  28.1 1.4 %collective-permute-start.8 = (bf16[256,512]{1,0:T(8,128)(2,1)S(1)}, bf16[256,512]{1,0:T(8,128)(2,1)S(1)}, u32[]{:S(2)}, u32[]{:S(2)}) collective-permute-start(bf16[256,512]{1,0:T(8,128)(2,1)S(1)} %hold.1.refs_8_), channel_id=1, source_target_pairs={{0,2},{1,3},{2,0},{3,1},{4,6},{5,7},{6,4},{7,5},{8,10},{9,11},{10,... | collective-permute-start | bytes 786440 | tf_op jit(solution)/shard_map/ppermute | solution.py:342
  29.5 1.3 %collective-permute-done.12.other = bf16[128,256]{1,0:T(8,128)(2,1)S(1)} collective-permute-done((bf16[128,256]{1,0:T(8,128)(2,1)S(1)}, bf16[128,256]{1,0:T(8,128)(2,1)S(1)}, u32[]{:S(2)}, u32[]{:S(2)}) %collective-permute-start.12) | collective-permute-done | bytes 65568 | tf_op jit(solution)/shard_map/ppermute | solution.py:346
  30.8 0.6 join.1
  31.3 5.9 %collective-permute-start.13 = (bf16[256,256]{1,0:T(8,128)(2,1)S(1)}, bf16[256,256]{1,0:T(8,128)(2,1)S(1)}, u32[]{:S(2)}, u32[]{:S(2)}) collective-permute-start(bf16[256,256]{1,0:T(8,128)(2,1)S(1)} %join.1), channel_id=1, source_target_pairs={{0,96},{8,168},{16,112},{24,184},{32,128},{40,200},{48,144},{56,21... | collective-permute-start | bytes 393224 | tf_op jit(solution)/shard_map/ppermute | solution.py:358
  37.2 0.6 collective-permute-start.11
  37.8 2.2 %copy-done.1 = bf16[512,4096]{1,0:T(8,128)(2,1)S(1)} copy-done((bf16[512,4096]{1,0:T(8,128)(2,1)S(1)}, bf16[512,4096]{1,0:T(8,128)(2,1)}, u32[]{:S(2)}) %copy-start.1) | copy-done | bytes 4194328
  40.0 5.4 %collective-permute-done.11.refs_16_.refs_3_.refs_5_ = bf16[128,256]{1,0:T(8,128)(2,1)S(1)} collective-permute-done((bf16[128,256]{1,0:T(8,128)(2,1)S(1)}, bf16[128,256]{1,0:T(8,128)(2,1)S(1)}, u32[]{:S(2)}, u32[]{:S(2)}) %collective-permute-start.11) | collective-permute-done | bytes 65568 | tf_op jit(solution)/shard_map/ppermute | solution.py:354
  45.4 2.8 %project.1 = (bf16[256,512]{1,0:T(8,128)(2,1)S(1)}, f32[8,128]{1,0:T(8,128)S(1)}) custom-call(s32[2]{0:T(128)S(1)} %pad_add_fusion.ids, bf16[128,512]{1,0:T(8,128)(2,1)S(1)} %copy-done.8, bf16[128,512]{1,0:T(8,128)(2,1)S(1)} %collective-permute-done.refs_1_.refs_3_, bf16[128,512]{1,0:T(8,128)(2,1)S(1)} %collective-permute-done.1.refs_2_.refs_4_, ...), custom_call_target="tpu_custom_call" | custom-call | flops 1073741824 | bytes 10485760 | tf_op jit(solution)/shard_map/project/pallas_call | solution.py:55
  48.2 3.1 %collective-permute-start.15 = (bf16[256,512]{1,0:T(8,128)(2,1)S(1)}, bf16[256,512]{1,0:T(8,128)(2,1)S(1)}, u32[]{:S(2)}, u32[]{:S(2)}) collective-permute-start(bf16[256,512]{1,0:T(8,128)(2,1)S(1)} %get-tuple-element.38.refs_0_), channel_id=1, source_target_pairs={{0,16},{8,24},{16,0},{24,8},{32,48},{40,56},{48,32},{56,40},{64,80... | collective-permute-start | bytes 786440 | tf_op jit(solution)/shard_map/ppermute | solution.py:346
  51.4 1.5 %collective-permute-start.18 = (bf16[256,256]{1,0:T(8,128)(2,1)S(1)}, bf16[256,256]{1,0:T(8,128)(2,1)S(1)}, u32[]{:S(2)}, u32[]{:S(2)}) collective-permute-start(bf16[256,256]{1,0:T(8,128)(2,1)S(1)} %join.1), channel_id=1, source_target_pairs={{0,64},{8,200},{16,80},{24,216},{32,96},{40,232},{48,112},{56,248}... | collective-permute-start | bytes 393224 | tf_op jit(solution)/shard_map/ppermute | solution.py:358
  52.9 2.8 %collective-permute-start.17 = (bf16[256,256]{1,0:T(8,128)(2,1)S(1)}, bf16[256,256]{1,0:T(8,128)(2,1)S(1)}, u32[]{:S(2)}, u32[]{:S(2)}) collective-permute-start(bf16[256,256]{1,0:T(8,128)(2,1)S(1)} %join.1), channel_id=1, source_target_pairs={{0,32},{8,232},{16,48},{24,248},{32,64},{40,8},{48,80},{56,24},{64... | collective-permute-start | bytes 393224 | tf_op jit(solution)/shard_map/ppermute | solution.py:358
  55.6 1.5 %collective-permute-done.15.refs_2_ = bf16[256,512]{1,0:T(8,128)(2,1)S(1)} collective-permute-done((bf16[256,512]{1,0:T(8,128)(2,1)S(1)}, bf16[256,512]{1,0:T(8,128)(2,1)S(1)}, u32[]{:S(2)}, u32[]{:S(2)}) %collective-permute-start.15) | collective-permute-done | bytes 262176 | tf_op jit(solution)/shard_map/ppermute | solution.py:346
  57.2 1.4 %collective-permute-done.18.refs_1_.refs_7_ = bf16[256,256]{1,0:T(8,128)(2,1)S(1)} collective-permute-done((bf16[256,256]{1,0:T(8,128)(2,1)S(1)}, bf16[256,256]{1,0:T(8,128)(2,1)S(1)}, u32[]{:S(2)}, u32[]{:S(2)}) %collective-permute-start.18) | collective-permute-done | bytes 131104 | tf_op jit(solution)/shard_map/ppermute | solution.py:358
  58.5 2.1 %collective-permute-done.17.refs_0_.refs_6_ = bf16[256,256]{1,0:T(8,128)(2,1)S(1)} collective-permute-done((bf16[256,256]{1,0:T(8,128)(2,1)S(1)}, bf16[256,256]{1,0:T(8,128)(2,1)S(1)}, u32[]{:S(2)}, u32[]{:S(2)}) %collective-permute-start.17) | collective-permute-done | bytes 131104 | tf_op jit(solution)/shard_map/ppermute | solution.py:358
  60.7 0.6 sort.1
  61.2 0.1 collective-permute-start.19
  61.3 1.4 %collective-permute-done.19.refs_9_ = bf16[384,256]{1,0:T(8,128)(2,1)S(1)} collective-permute-done((bf16[384,256]{1,0:T(8,128)(2,1)S(1)}, bf16[384,256]{1,0:T(8,128)(2,1)S(1)}, u32[]{:S(2)}, u32[]{:S(2)}) %collective-permute-start.19) | collective-permute-done | bytes 196640 | tf_op jit(solution)/shard_map/ppermute | solution.py:346
  62.8 4.7 %softmax.1 = (bf16[2048,1024]{1,0:T(8,128)(2,1)S(1)}, f32[128,128]{1,0:T(8,128)S(1)}, bf16[1024,128]{1,0:T(8,128)(2,1)S(1)}, bf16[1024,128]{1,0:T(8,128)(2,1)S(1)}) custom-call(s32[2]{0:T(128)S(1)} %pad_add_fusion.ids, s32[64]{0:T(128)S(1)} %copy-done.13, s32[8]{0:T(128)S(1)} %copy-done.14, bf16[256,512]{1,0:T(8,128)(2,1)S(1)} %get-tuple-element.38.refs_0_, ...), custom_call_target="tpu_custom_call" | custom-call | flops 1073741824 | bytes 6291456 | tf_op jit(solution)/shard_map/softmax/pallas_call | solution.py:55
  67.5 0.6 collective-permute-start.21
  68.1 5.3 %collective-permute-done.21.refs_9_ = f32[128,128]{1,0:T(8,128)S(1)} collective-permute-done((f32[128,128]{1,0:T(8,128)S(1)}, f32[128,128]{1,0:T(8,128)S(1)}, u32[]{:S(2)}, u32[]{:S(2)}) %collective-permute-start.21) | collective-permute-done | bytes 65568 | tf_op jit(solution)/shard_map/ppermute | solution.py:346
  73.4 1.2 %collective-permute-done.22.refs_10_ = f32[128,128]{1,0:T(8,128)S(1)} collective-permute-done((f32[128,128]{1,0:T(8,128)S(1)}, f32[128,128]{1,0:T(8,128)S(1)}, u32[]{:S(2)}, u32[]{:S(2)}) %collective-permute-start.22) | collective-permute-done | bytes 65568 | tf_op jit(solution)/shard_map/ppermute | solution.py:346
  74.6 4.1 %gradient.1 = (bf16[256,128]{1,0:T(8,128)(2,1)S(1)}, bf16[256,128]{1,0:T(8,128)(2,1)S(1)}, bf16[3,256,128]{2,1,0:T(8,128)(2,1)S(1)}, bf16[3,256,128]{2,1,0:T(8,1...) custom-call(bf16[256,512]{1,0:T(8,128)(2,1)S(1)} %get-tuple-element.38.refs_0_, ...), custom_call_target="tpu_custom_call" | custom-call | flops 2147483648 | bytes 6291456 | tf_op jit(solution)/shard_map/gradient/pallas_call | solution.py:55
  78.7 0.5 collective-permute-start.29
  79.2 0.4 collective-permute-start.23
  79.5 1.3 %collective-permute-done.23.got = bf16[3,256,128]{2,1,0:T(8,128)(2,1)S(1)} collective-permute-done((bf16[3,256,128]{2,1,0:T(8,128)(2,1)S(1)}, bf16[3,256,128]{2,1,0:T(8,128)(2,1)S(1)}, u32[]{:S(2)}, u32[]{:S(2)}) %collective-permute-start.23) | collective-permute-done | bytes 196640 | tf_op jit(solution)/shard_map/ppermute | solution.py:346
  80.8 0.6 pair.1
  81.4 1.2 collective-permute-start.24
  82.6 2.0 %collective-permute-start.25 = (bf16[2,256,128]{2,1,0:T(8,128)(2,1)S(1)}, bf16[2,256,128]{2,1,0:T(8,128)(2,1)S(1)}, u32[]{:S(2)}, u32[]{:S(2)}) collective-permute-start(bf16[2,256,128]{2,1,0:T(8,128)(2,1)S(1)} %get-tuple-element.46), channel_id=1, source_target_pairs={{0,192},{8,72},{16,208},{24,88},{32,224},{40,104},{48,240},{56,120... | collective-permute-start | bytes 393224 | tf_op jit(solution)/shard_map/ppermute | solution.py:358
  84.6 2.1 %collective-permute-start.26 = (bf16[2,256,128]{2,1,0:T(8,128)(2,1)S(1)}, bf16[2,256,128]{2,1,0:T(8,128)(2,1)S(1)}, u32[]{:S(2)}, u32[]{:S(2)}) collective-permute-start(bf16[2,256,128]{2,1,0:T(8,128)(2,1)S(1)} %get-tuple-element.47), channel_id=1, source_target_pairs={{0,160},{8,104},{16,176},{24,120},{32,192},{40,136},{48,208},{56,1... | collective-permute-start | bytes 393224 | tf_op jit(solution)/shard_map/ppermute | solution.py:358
  86.8 0.9 collective-permute-start.30
  87.7 2.2 %collective-permute-start.27 = (bf16[256,128]{1,0:T(8,128)(2,1)S(1)}, bf16[256,128]{1,0:T(8,128)(2,1)S(1)}, u32[]{:S(2)}, u32[]{:S(2)}) collective-permute-start(bf16[256,128]{1,0:T(8,128)(2,1)S(1)} %get-tuple-element.49), channel_id=1, source_target_pairs={{0,128},{8,136},{16,144},{24,152},{32,160},{40,168},{48,176},{56,1... | collective-permute-start | bytes 196616 | tf_op jit(solution)/shard_map/ppermute | solution.py:354
  90.0 8.9 %collective-permute-done.27.refs_4_ = bf16[256,128]{1,0:T(8,128)(2,1)S(1)} collective-permute-done((bf16[256,128]{1,0:T(8,128)(2,1)S(1)}, bf16[256,128]{1,0:T(8,128)(2,1)S(1)}, u32[]{:S(2)}, u32[]{:S(2)}) %collective-permute-start.27) | collective-permute-done | bytes 65568 | tf_op jit(solution)/shard_map/ppermute | solution.py:354
  98.9 0.6 sum.1
  99.5 0.1 collective-permute-start.28
  99.6 1.5 %back_query.1.refs_11_ = f32[128,4096]{1,0:T(8,128)S(1)} custom-call(f32[128,512]{1,0:T(8,128)S(1)} %get-tuple-element.54.stay, bf16[128,512]{1,0:T(8,128)(2,1)S(1)} %collective-permute-done.30.got, bf16[4096,512]{1,0:T(8,128)(2,1)S(1)} %copy-done), custom_call_target="tpu_custom_call" | custom-call | flops 536870912 | bytes 6291456 | tf_op jit(solution)/shard_map/back_query/pallas_call | solution.py:55
  101.1 1.5 %back_kv.1 = (f32[128,512]{1,0:T(8,128)S(1)}, bf16[16,256]{1,0:T(8,128)(2,1)S(1)}, bf16[144,512]{1,0:T(8,128)(2,1)S(1)}, bf16[144,512]{1,0:T(8,128)(2,1)S(1)}, b...) custom-call(s32[2]{0:T(128)S(1)} %pad_add_fusion.ids, ...), custom_call_target="tpu_custom_call" | custom-call | flops 268435456 | bytes 7340032 | tf_op jit(solution)/shard_map/back_kv/pallas_call | solution.py:55
  102.6 0.6 collective-permute-start.31
  103.2 1.1 collective-permute-start.32
  104.3 1.5 %collective-permute-start.33 = (bf16[144,512]{1,0:T(8,128)(2,1)S(1)}, bf16[144,512]{1,0:T(8,128)(2,1)S(1)}, u32[]{:S(2)}, u32[]{:S(2)}) collective-permute-start(bf16[144,512]{1,0:T(8,128)(2,1)S(1)} %get-tuple-element.60), channel_id=1, source_target_pairs={{0,4},{1,5},{2,6},{3,7},{4,0},{5,1},{6,2},{7,3},{8,12},{9,13},{10,... | collective-permute-start | bytes 442376 | tf_op jit(solution)/shard_map/ppermute | solution.py:342
  105.9 2.6 %collective-permute-start.34 = (bf16[144,512]{1,0:T(8,128)(2,1)S(1)}, bf16[144,512]{1,0:T(8,128)(2,1)S(1)}, u32[]{:S(2)}, u32[]{:S(2)}) collective-permute-start(bf16[144,512]{1,0:T(8,128)(2,1)S(1)} %get-tuple-element.61), channel_id=1, source_target_pairs={{0,5},{1,4},{2,7},{3,6},{4,1},{5,0},{6,3},{7,2},{8,13},{9,12},{10,... | collective-permute-start | bytes 442376 | tf_op jit(solution)/shard_map/ppermute | solution.py:342
  108.4 1.3 %collective-permute-start.35 = (bf16[144,512]{1,0:T(8,128)(2,1)S(1)}, bf16[144,512]{1,0:T(8,128)(2,1)S(1)}, u32[]{:S(2)}, u32[]{:S(2)}) collective-permute-start(bf16[144,512]{1,0:T(8,128)(2,1)S(1)} %get-tuple-element.62), channel_id=1, source_target_pairs={{0,3},{1,2},{2,1},{3,0},{4,7},{5,6},{6,5},{7,4},{8,11},{9,10},{10,... | collective-permute-start | bytes 442376 | tf_op jit(solution)/shard_map/ppermute | solution.py:342
  109.7 1.2 collective-permute-start.36
  110.9 3.0 %collective-permute-start.37 = (bf16[144,512]{1,0:T(8,128)(2,1)S(1)}, bf16[144,512]{1,0:T(8,128)(2,1)S(1)}, u32[]{:S(2)}, u32[]{:S(2)}) collective-permute-start(bf16[144,512]{1,0:T(8,128)(2,1)S(1)} %get-tuple-element.64), channel_id=1, source_target_pairs={{0,7},{1,6},{2,5},{3,4},{4,3},{5,2},{6,1},{7,0},{8,15},{9,14},{10,... | collective-permute-start | bytes 442376 | tf_op jit(solution)/shard_map/ppermute | solution.py:342
  113.8 7.3 %collective-permute-done.33.refs_2_ = bf16[144,512]{1,0:T(8,128)(2,1)S(1)} collective-permute-done((bf16[144,512]{1,0:T(8,128)(2,1)S(1)}, bf16[144,512]{1,0:T(8,128)(2,1)S(1)}, u32[]{:S(2)}, u32[]{:S(2)}) %collective-permute-start.33) | collective-permute-done | bytes 147488 | tf_op jit(solution)/shard_map/ppermute | solution.py:342
  121.1 1.5 %collective-permute-done.36.refs_5_ = bf16[144,512]{1,0:T(8,128)(2,1)S(1)} collective-permute-done((bf16[144,512]{1,0:T(8,128)(2,1)S(1)}, bf16[144,512]{1,0:T(8,128)(2,1)S(1)}, u32[]{:S(2)}, u32[]{:S(2)}) %collective-permute-start.36) | collective-permute-done | bytes 147488 | tf_op jit(solution)/shard_map/ppermute | solution.py:342
  122.6 1.5 %last.1 = (bf16[128,512]{1,0:T(8,128)(2,1)}, f32[1,128]{1,0:T(1,128)}) custom-call(s32[2]{0:T(128)S(1)} %pad_add_fusion.ids, f32[128,512]{1,0:T(8,128)S(1)} %get-tuple-element.56.own, bf16[16,256]{1,0:T(8,128)(2,1)S(1)} %get-tuple-element.57.own_row, bf16[144,512]{1,0:T(8,128)(2,1)S(1)} %collective-permute-done.31.refs_0_, ...), custom_call_target="tpu_custom_call" | custom-call | flops 655360 | bytes 3145728 | tf_op jit(solution)/shard_map/last/pallas_call | solution.py:55
  (58 shorter events, 0.3 us)
Async XLA Ops:
  0.6 8.0 %collective-permute-start.6 = (bf16[128,512]{1,0:T(8,128)(2,1)}, bf16[128,512]{1,0:T(8,128)(2,1)S(1)}, u32[]{:S(2)}, u32[]{:S(2)}) collective-permute-start(bf16[128,512]{1,0:T(8,128)(2,1)} %refs_7_.1), channel_id=1, source_target_pairs={{0,1},{1,0},{2,3},{3,2},{4,5},{5,4},{6,7},{7,6},{8,9},{9,8},{10,11... | collective-permute-start | bytes 393224 | tf_op jit(solution)/shard_map/ppermute | solution.py:342
  2.2 9.5 %collective-permute-start.5 = (bf16[128,512]{1,0:T(8,128)(2,1)}, bf16[128,512]{1,0:T(8,128)(2,1)S(1)}, u32[]{:S(2)}, u32[]{:S(2)}) collective-permute-start(bf16[128,512]{1,0:T(8,128)(2,1)} %refs_7_.1), channel_id=1, source_target_pairs={{0,2},{1,3},{2,0},{3,1},{4,6},{5,7},{6,4},{7,5},{8,10},{9,11},{10,... | collective-permute-start | bytes 393224 | tf_op jit(solution)/shard_map/ppermute | solution.py:342
  3.8 15.4 %collective-permute-start.4 = (bf16[128,512]{1,0:T(8,128)(2,1)}, bf16[128,512]{1,0:T(8,128)(2,1)S(1)}, u32[]{:S(2)}, u32[]{:S(2)}) collective-permute-start(bf16[128,512]{1,0:T(8,128)(2,1)} %refs_7_.1), channel_id=1, source_target_pairs={{0,4},{1,5},{2,6},{3,7},{4,0},{5,1},{6,2},{7,3},{8,12},{9,13},{10,... | collective-permute-start | bytes 393224 | tf_op jit(solution)/shard_map/ppermute | solution.py:342
  6.7 14.1 %collective-permute-start.3 = (bf16[128,512]{1,0:T(8,128)(2,1)}, bf16[128,512]{1,0:T(8,128)(2,1)S(1)}, u32[]{:S(2)}, u32[]{:S(2)}) collective-permute-start(bf16[128,512]{1,0:T(8,128)(2,1)} %refs_7_.1), channel_id=1, source_target_pairs={{0,5},{1,4},{2,7},{3,6},{4,1},{5,0},{6,3},{7,2},{8,13},{9,12},{10,... | collective-permute-start | bytes 393224 | tf_op jit(solution)/shard_map/ppermute | solution.py:342
  7.3 13.5 %collective-permute-start.2 = (bf16[128,512]{1,0:T(8,128)(2,1)}, bf16[128,512]{1,0:T(8,128)(2,1)S(1)}, u32[]{:S(2)}, u32[]{:S(2)}) collective-permute-start(bf16[128,512]{1,0:T(8,128)(2,1)} %refs_7_.1), channel_id=1, source_target_pairs={{0,3},{1,2},{2,1},{3,0},{4,7},{5,6},{6,5},{7,4},{8,11},{9,10},{10,... | collective-permute-start | bytes 393224 | tf_op jit(solution)/shard_map/ppermute | solution.py:342
  8.7 12.2 %collective-permute-start.1 = (bf16[128,512]{1,0:T(8,128)(2,1)}, bf16[128,512]{1,0:T(8,128)(2,1)S(1)}, u32[]{:S(2)}, u32[]{:S(2)}) collective-permute-start(bf16[128,512]{1,0:T(8,128)(2,1)} %refs_7_.1), channel_id=1, source_target_pairs={{0,6},{1,7},{2,4},{3,5},{4,2},{5,3},{6,0},{7,1},{8,14},{9,15},{10,... | collective-permute-start | bytes 393224 | tf_op jit(solution)/shard_map/ppermute | solution.py:342
  11.7 9.2 %collective-permute-start = (bf16[128,512]{1,0:T(8,128)(2,1)}, bf16[128,512]{1,0:T(8,128)(2,1)S(1)}, u32[]{:S(2)}, u32[]{:S(2)}) collective-permute-start(bf16[128,512]{1,0:T(8,128)(2,1)} %refs_7_.1), channel_id=1, source_target_pairs={{0,7},{1,6},{2,5},{3,4},{4,3},{5,2},{6,1},{7,0},{8,15},{9,14},{10,... | collective-permute-start | bytes 393224 | tf_op jit(solution)/shard_map/ppermute | solution.py:342
  15.7 22.1 %copy-start = (bf16[4096,512]{1,0:T(8,128)(2,1)S(1)}, bf16[4096,512]{1,0:T(8,128)(2,1)}, u32[]{:S(2)}) copy-start(bf16[4096,512]{1,0:T(8,128)(2,1)} %w_query.1) | copy-start | bytes 12582916
  15.7 1.4 %copy-start.3 = (bf16[4096,128]{1,0:T(8,128)(2,1)S(1)}, bf16[4096,128]{1,0:T(8,128)(2,1)}, u32[]{:S(2)}) copy-start(bf16[4096,128]{1,0:T(8,128)(2,1)} %refs_12_.3) | copy-start | bytes 3145732
  17.1 1.4 %copy-start.5 = (bf16[4096,128]{1,0:T(8,128)(2,1)S(1)}, bf16[4096,128]{1,0:T(8,128)(2,1)}, u32[]{:S(2)}) copy-start(bf16[4096,128]{1,0:T(8,128)(2,1)} %refs_13_.1) | copy-start | bytes 3145732
  18.5 0.7 copy-start.11
  19.2 5.2 %collective-permute-start.7 = (bf16[128,512]{1,0:T(8,128)(2,1)}, bf16[128,512]{1,0:T(8,128)(2,1)S(1)}, u32[]{:S(2)}, u32[]{:S(2)}) collective-permute-start(bf16[128,512]{1,0:T(8,128)(2,1)} %refs_8_.1), channel_id=1, source_target_pairs={{0,1},{1,0},{2,3},{3,2},{4,5},{5,4},{6,7},{7,6},{8,9},{9,8},{10,11... | collective-permute-start | bytes 393224 | tf_op jit(solution)/shard_map/ppermute | solution.py:342
  20.9 0.9 copy-start.7
  24.4 0.9 copy-start.9
  25.3 20.1 %collective-permute-start.10 = (bf16[256,512]{1,0:T(8,128)(2,1)S(1)}, bf16[256,512]{1,0:T(8,128)(2,1)S(1)}, u32[]{:S(2)}, u32[]{:S(2)}) collective-permute-start(bf16[256,512]{1,0:T(8,128)(2,1)S(1)} %hold.1.refs_8_), channel_id=1, source_target_pairs={{0,6},{1,7},{2,4},{3,5},{4,2},{5,3},{6,0},{7,1},{8,14},{9,15},{10,... | collective-permute-start | bytes 786440 | tf_op jit(solution)/shard_map/ppermute | solution.py:342
  27.2 18.2 %collective-permute-start.9 = (bf16[256,512]{1,0:T(8,128)(2,1)S(1)}, bf16[256,512]{1,0:T(8,128)(2,1)S(1)}, u32[]{:S(2)}, u32[]{:S(2)}) collective-permute-start(bf16[256,512]{1,0:T(8,128)(2,1)S(1)} %hold.1.refs_8_), channel_id=1, source_target_pairs={{0,4},{1,5},{2,6},{3,7},{4,0},{5,1},{6,2},{7,3},{8,12},{9,13},{10,... | collective-permute-start | bytes 786440 | tf_op jit(solution)/shard_map/ppermute | solution.py:342
  28.1 17.4 %collective-permute-start.8 = (bf16[256,512]{1,0:T(8,128)(2,1)S(1)}, bf16[256,512]{1,0:T(8,128)(2,1)S(1)}, u32[]{:S(2)}, u32[]{:S(2)}) collective-permute-start(bf16[256,512]{1,0:T(8,128)(2,1)S(1)} %hold.1.refs_8_), channel_id=1, source_target_pairs={{0,2},{1,3},{2,0},{3,1},{4,6},{5,7},{6,4},{7,5},{8,10},{9,11},{10,... | collective-permute-start | bytes 786440 | tf_op jit(solution)/shard_map/ppermute | solution.py:342
  29.5 1.3 %collective-permute-start.12 = (bf16[128,256]{1,0:T(8,128)(2,1)S(1)}, bf16[128,256]{1,0:T(8,128)(2,1)S(1)}, u32[]{:S(2)}, u32[]{:S(2)}) collective-permute-start(bf16[128,256]{1,0:T(8,128)(2,1)S(1)} %get-tuple-element.36.refs_0_.mine.refs_4_), channel_id=1, source_target_pairs={{0,8},{8,0},{16,24},{24,16},{32,40},{40,32},{48,56},{56,48},{64,72... | collective-permute-start | bytes 196616 | tf_op jit(solution)/shard_map/ppermute | solution.py:346
  31.3 14.1 %collective-permute-start.13 = (bf16[256,256]{1,0:T(8,128)(2,1)S(1)}, bf16[256,256]{1,0:T(8,128)(2,1)S(1)}, u32[]{:S(2)}, u32[]{:S(2)}) collective-permute-start(bf16[256,256]{1,0:T(8,128)(2,1)S(1)} %join.1), channel_id=1, source_target_pairs={{0,96},{8,168},{16,112},{24,184},{32,128},{40,200},{48,144},{56,21... | collective-permute-start | bytes 393224 | tf_op jit(solution)/shard_map/ppermute | solution.py:358
  37.2 8.2 %collective-permute-start.11 = (bf16[128,256]{1,0:T(8,128)(2,1)S(1)}, bf16[128,256]{1,0:T(8,128)(2,1)S(1)}, u32[]{:S(2)}, u32[]{:S(2)}) collective-permute-start(bf16[128,256]{1,0:T(8,128)(2,1)S(1)} %get-tuple-element.36.refs_0_.mine.refs_4_), channel_id=1, source_target_pairs={{0,128},{8,136},{16,144},{24,152},{32,160},{40,168},{48,176},{56,1... | collective-permute-start | bytes 196616 | tf_op jit(solution)/shard_map/ppermute | solution.py:354
  37.8 2.2 %copy-start.1 = (bf16[512,4096]{1,0:T(8,128)(2,1)S(1)}, bf16[512,4096]{1,0:T(8,128)(2,1)}, u32[]{:S(2)}) copy-start(bf16[512,4096]{1,0:T(8,128)(2,1)} %refs_12_.2) | copy-start | bytes 12582916
  40.0 5.5 %copy-start.2 = (bf16[512,4096]{1,0:T(8,128)(2,1)S(1)}, bf16[512,4096]{1,0:T(8,128)(2,1)}, u32[]{:S(2)}) copy-start(bf16[512,4096]{1,0:T(8,128)(2,1)} %refs_12_.2) | copy-start | bytes 12582916
  40.0 5.5 %copy-start.8 = (bf16[128,512]{1,0:T(8,128)(2,1)S(1)}, bf16[128,512]{1,0:T(8,128)(2,1)}, u32[]{:S(2)}) copy-start(bf16[128,512]{1,0:T(8,128)(2,1)} %refs_7_.1) | copy-start | bytes 393220
  40.0 22.8 %copy-start.13 = (s32[64]{0:T(128)S(1)}, s32[64]{0:T(128)}, u32[]{:S(2)}) copy-start(s32[64]{0:T(128)} %order.1) | copy-start | bytes 772
  40.0 22.8 %copy-start.14 = (s32[8]{0:T(128)S(1)}, s32[8]{0:T(128)}, u32[]{:S(2)}) copy-start(s32[8]{0:T(128)} %lengths.1) | copy-start | bytes 100
  48.2 8.9 %collective-permute-start.15 = (bf16[256,512]{1,0:T(8,128)(2,1)S(1)}, bf16[256,512]{1,0:T(8,128)(2,1)S(1)}, u32[]{:S(2)}, u32[]{:S(2)}) collective-permute-start(bf16[256,512]{1,0:T(8,128)(2,1)S(1)} %get-tuple-element.38.refs_0_), channel_id=1, source_target_pairs={{0,16},{8,24},{16,0},{24,8},{32,48},{40,56},{48,32},{56,40},{64,80... | collective-permute-start | bytes 786440 | tf_op jit(solution)/shard_map/ppermute | solution.py:346
  51.4 7.2 %collective-permute-start.18 = (bf16[256,256]{1,0:T(8,128)(2,1)S(1)}, bf16[256,256]{1,0:T(8,128)(2,1)S(1)}, u32[]{:S(2)}, u32[]{:S(2)}) collective-permute-start(bf16[256,256]{1,0:T(8,128)(2,1)S(1)} %join.1), channel_id=1, source_target_pairs={{0,64},{8,200},{16,80},{24,216},{32,96},{40,232},{48,112},{56,248}... | collective-permute-start | bytes 393224 | tf_op jit(solution)/shard_map/ppermute | solution.py:358
  52.9 7.8 %collective-permute-start.17 = (bf16[256,256]{1,0:T(8,128)(2,1)S(1)}, bf16[256,256]{1,0:T(8,128)(2,1)S(1)}, u32[]{:S(2)}, u32[]{:S(2)}) collective-permute-start(bf16[256,256]{1,0:T(8,128)(2,1)S(1)} %join.1), channel_id=1, source_target_pairs={{0,32},{8,232},{16,48},{24,248},{32,64},{40,8},{48,80},{56,24},{64... | collective-permute-start | bytes 393224 | tf_op jit(solution)/shard_map/ppermute | solution.py:358
  55.6 7.1 %collective-permute-start.14 = (bf16[256,512]{1,0:T(8,128)(2,1)S(1)}, bf16[256,512]{1,0:T(8,128)(2,1)S(1)}, u32[]{:S(2)}, u32[]{:S(2)}) collective-permute-start(bf16[256,512]{1,0:T(8,128)(2,1)S(1)} %get-tuple-element.38.refs_0_), channel_id=1, source_target_pairs={{0,8},{8,0},{16,24},{24,16},{32,40},{40,32},{48,56},{56,48},{64,72... | collective-permute-start | bytes 786440 | tf_op jit(solution)/shard_map/ppermute | solution.py:346
  57.2 5.6 %collective-permute-start.16 = (bf16[256,512]{1,0:T(8,128)(2,1)S(1)}, bf16[256,512]{1,0:T(8,128)(2,1)S(1)}, u32[]{:S(2)}, u32[]{:S(2)}) collective-permute-start(bf16[256,512]{1,0:T(8,128)(2,1)S(1)} %collective-permute-done.15.refs_2_), channel_id=1, source_target_pairs={{0,8},{8,0},{16,24},{24,16},{32,40},{40,32},{48,56},{56,48},{64,72... | collective-permute-start | bytes 786440 | tf_op jit(solution)/shard_map/ppermute | solution.py:346
  61.2 1.5 %collective-permute-start.19 = (bf16[384,256]{1,0:T(8,128)(2,1)S(1)}, bf16[384,256]{1,0:T(8,128)(2,1)S(1)}, u32[]{:S(2)}, u32[]{:S(2)}) collective-permute-start(bf16[384,256]{1,0:T(8,128)(2,1)S(1)} %sort.1), channel_id=1, source_target_pairs={{0,8},{8,0},{16,24},{24,16},{32,40},{40,32},{48,56},{56,48},{64,72... | collective-permute-start | bytes 589832 | tf_op jit(solution)/shard_map/ppermute | solution.py:346
  67.5 5.8 %collective-permute-start.21 = (f32[128,128]{1,0:T(8,128)S(1)}, f32[128,128]{1,0:T(8,128)S(1)}, u32[]{:S(2)}, u32[]{:S(2)}) collective-permute-start(f32[128,128]{1,0:T(8,128)S(1)} %get-tuple-element.42.refs_7_), channel_id=1, source_target_pairs={{0,16},{8,24},{16,0},{24,8},{32,48},{40,56},{48,32},{56,40},{64,80... | collective-permute-start | bytes 196616 | tf_op jit(solution)/shard_map/ppermute | solution.py:346
  68.1 5.3 %collective-permute-start.20 = (f32[128,128]{1,0:T(8,128)S(1)}, f32[128,128]{1,0:T(8,128)S(1)}, u32[]{:S(2)}, u32[]{:S(2)}) collective-permute-start(f32[128,128]{1,0:T(8,128)S(1)} %get-tuple-element.42.refs_7_), channel_id=1, source_target_pairs={{0,8},{8,0},{16,24},{24,16},{32,40},{40,32},{48,56},{56,48},{64,72... | collective-permute-start | bytes 196616 | tf_op jit(solution)/shard_map/ppermute | solution.py:346
  73.4 1.3 %collective-permute-start.22 = (f32[128,128]{1,0:T(8,128)S(1)}, f32[128,128]{1,0:T(8,128)S(1)}, u32[]{:S(2)}, u32[]{:S(2)}) collective-permute-start(f32[128,128]{1,0:T(8,128)S(1)} %collective-permute-done.21.refs_9_), channel_id=1, source_target_pairs={{0,8},{8,0},{16,24},{24,16},{32,40},{40,32},{48,56},{56,48},{64,72... | collective-permute-start | bytes 196616 | tf_op jit(solution)/shard_map/ppermute | solution.py:346
  78.7 8.1 %collective-permute-start.29 = (bf16[256,512]{1,0:T(8,128)(2,1)S(1)}, bf16[256,512]{1,0:T(8,128)(2,1)S(1)}, u32[]{:S(2)}, u32[]{:S(2)}) collective-permute-start(bf16[256,512]{1,0:T(8,128)(2,1)S(1)} %get-tuple-element.53), channel_id=1, source_target_pairs={{0,8},{8,0},{16,24},{24,16},{32,40},{40,32},{48,56},{56,48},{64,72... | collective-permute-start | bytes 786440 | tf_op jit(solution)/shard_map/ppermute | solution.py:346
  79.2 1.7 %collective-permute-start.23 = (bf16[3,256,128]{2,1,0:T(8,128)(2,1)S(1)}, bf16[3,256,128]{2,1,0:T(8,128)(2,1)S(1)}, u32[]{:S(2)}, u32[]{:S(2)}) collective-permute-start(bf16[3,256,128]{2,1,0:T(8,128)(2,1)S(1)} %get-tuple-element.44), channel_id=1, source_target_pairs={{0,8},{8,0},{16,24},{24,16},{32,40},{40,32},{48,56},{56,48},{64,72... | collective-permute-start | bytes 589832 | tf_op jit(solution)/shard_map/ppermute | solution.py:346
  80.8 20.3 %copy-start.4 = (bf16[4096,128]{1,0:T(8,128)(2,1)S(1)}, bf16[4096,128]{1,0:T(8,128)(2,1)}, u32[]{:S(2)}) copy-start(bf16[4096,128]{1,0:T(8,128)(2,1)} %refs_12_.3) | copy-start | bytes 3145732
  80.8 20.3 %copy-start.6 = (bf16[4096,128]{1,0:T(8,128)(2,1)S(1)}, bf16[4096,128]{1,0:T(8,128)(2,1)}, u32[]{:S(2)}) copy-start(bf16[4096,128]{1,0:T(8,128)(2,1)} %refs_13_.1) | copy-start | bytes 3145732
  80.8 20.3 %copy-start.12 = (f32[4096]{0:T(1024)S(1)}, f32[4096]{0:T(1024)}, u32[]{:S(2)}) copy-start(f32[4096]{0:T(1024)} %param.11) | copy-start | bytes 49156
  81.4 17.4 %collective-permute-start.24 = (bf16[2,256,128]{2,1,0:T(8,128)(2,1)S(1)}, bf16[2,256,128]{2,1,0:T(8,128)(2,1)S(1)}, u32[]{:S(2)}, u32[]{:S(2)}) collective-permute-start(bf16[2,256,128]{2,1,0:T(8,128)(2,1)S(1)} %get-tuple-element.45), channel_id=1, source_target_pairs={{0,224},{8,40},{16,240},{24,56},{32,0},{40,72},{48,16},{56,88},{64... | collective-permute-start | bytes 393224 | tf_op jit(solution)/shard_map/ppermute | solution.py:358
  82.6 16.2 %collective-permute-start.25 = (bf16[2,256,128]{2,1,0:T(8,128)(2,1)S(1)}, bf16[2,256,128]{2,1,0:T(8,128)(2,1)S(1)}, u32[]{:S(2)}, u32[]{:S(2)}) collective-permute-start(bf16[2,256,128]{2,1,0:T(8,128)(2,1)S(1)} %get-tuple-element.46), channel_id=1, source_target_pairs={{0,192},{8,72},{16,208},{24,88},{32,224},{40,104},{48,240},{56,120... | collective-permute-start | bytes 393224 | tf_op jit(solution)/shard_map/ppermute | solution.py:358
  84.6 14.2 %collective-permute-start.26 = (bf16[2,256,128]{2,1,0:T(8,128)(2,1)S(1)}, bf16[2,256,128]{2,1,0:T(8,128)(2,1)S(1)}, u32[]{:S(2)}, u32[]{:S(2)}) collective-permute-start(bf16[2,256,128]{2,1,0:T(8,128)(2,1)S(1)} %get-tuple-element.47), channel_id=1, source_target_pairs={{0,160},{8,104},{16,176},{24,120},{32,192},{40,136},{48,208},{56,1... | collective-permute-start | bytes 393224 | tf_op jit(solution)/shard_map/ppermute | solution.py:358
  86.8 12.8 %collective-permute-start.30 = (bf16[128,512]{1,0:T(8,128)(2,1)S(1)}, bf16[128,512]{1,0:T(8,128)(2,1)S(1)}, u32[]{:S(2)}, u32[]{:S(2)}) collective-permute-start(bf16[128,512]{1,0:T(8,128)(2,1)S(1)} %get-tuple-element.55), channel_id=1, source_target_pairs={{0,16},{8,24},{16,0},{24,8},{32,48},{40,56},{48,32},{56,40},{64,80... | collective-permute-start | bytes 393224 | tf_op jit(solution)/shard_map/ppermute | solution.py:346
  87.7 11.1 %collective-permute-start.27 = (bf16[256,128]{1,0:T(8,128)(2,1)S(1)}, bf16[256,128]{1,0:T(8,128)(2,1)S(1)}, u32[]{:S(2)}, u32[]{:S(2)}) collective-permute-start(bf16[256,128]{1,0:T(8,128)(2,1)S(1)} %get-tuple-element.49), channel_id=1, source_target_pairs={{0,128},{8,136},{16,144},{24,152},{32,160},{40,168},{48,176},{56,1... | collective-permute-start | bytes 196616 | tf_op jit(solution)/shard_map/ppermute | solution.py:354
  99.5 1.6 %collective-permute-start.28 = (bf16[256,128]{1,0:T(8,128)(2,1)S(1)}, bf16[256,128]{1,0:T(8,128)(2,1)S(1)}, u32[]{:S(2)}, u32[]{:S(2)}) collective-permute-start(bf16[256,128]{1,0:T(8,128)(2,1)S(1)} %get-tuple-element.51), channel_id=1, source_target_pairs={{0,8},{8,0},{16,24},{24,16},{32,40},{40,32},{48,56},{56,48},{64,72... | collective-permute-start | bytes 196616 | tf_op jit(solution)/shard_map/ppermute | solution.py:346
  101.1 21.5 %copy-start.10 = (bf16[128,512]{1,0:T(8,128)(2,1)S(1)}, bf16[128,512]{1,0:T(8,128)(2,1)}, u32[]{:S(2)}) copy-start(bf16[128,512]{1,0:T(8,128)(2,1)} %refs_8_.1) | copy-start | bytes 393220
  102.6 7.1 %collective-permute-start.31 = (bf16[144,512]{1,0:T(8,128)(2,1)S(1)}, bf16[144,512]{1,0:T(8,128)(2,1)S(1)}, u32[]{:S(2)}, u32[]{:S(2)}) collective-permute-start(bf16[144,512]{1,0:T(8,128)(2,1)S(1)} %get-tuple-element.58), channel_id=1, source_target_pairs={{0,1},{1,0},{2,3},{3,2},{4,5},{5,4},{6,7},{7,6},{8,9},{9,8},{10,11... | collective-permute-start | bytes 442376 | tf_op jit(solution)/shard_map/ppermute | solution.py:342
  103.2 7.6 %collective-permute-start.32 = (bf16[144,512]{1,0:T(8,128)(2,1)S(1)}, bf16[144,512]{1,0:T(8,128)(2,1)S(1)}, u32[]{:S(2)}, u32[]{:S(2)}) collective-permute-start(bf16[144,512]{1,0:T(8,128)(2,1)S(1)} %get-tuple-element.59), channel_id=1, source_target_pairs={{0,2},{1,3},{2,0},{3,1},{4,6},{5,7},{6,4},{7,5},{8,10},{9,11},{10,... | collective-permute-start | bytes 442376 | tf_op jit(solution)/shard_map/ppermute | solution.py:342
  104.3 16.8 %collective-permute-start.33 = (bf16[144,512]{1,0:T(8,128)(2,1)S(1)}, bf16[144,512]{1,0:T(8,128)(2,1)S(1)}, u32[]{:S(2)}, u32[]{:S(2)}) collective-permute-start(bf16[144,512]{1,0:T(8,128)(2,1)S(1)} %get-tuple-element.60), channel_id=1, source_target_pairs={{0,4},{1,5},{2,6},{3,7},{4,0},{5,1},{6,2},{7,3},{8,12},{9,13},{10,... | collective-permute-start | bytes 442376 | tf_op jit(solution)/shard_map/ppermute | solution.py:342
  105.9 15.2 %collective-permute-start.34 = (bf16[144,512]{1,0:T(8,128)(2,1)S(1)}, bf16[144,512]{1,0:T(8,128)(2,1)S(1)}, u32[]{:S(2)}, u32[]{:S(2)}) collective-permute-start(bf16[144,512]{1,0:T(8,128)(2,1)S(1)} %get-tuple-element.61), channel_id=1, source_target_pairs={{0,5},{1,4},{2,7},{3,6},{4,1},{5,0},{6,3},{7,2},{8,13},{9,12},{10,... | collective-permute-start | bytes 442376 | tf_op jit(solution)/shard_map/ppermute | solution.py:342
  108.4 12.7 %collective-permute-start.35 = (bf16[144,512]{1,0:T(8,128)(2,1)S(1)}, bf16[144,512]{1,0:T(8,128)(2,1)S(1)}, u32[]{:S(2)}, u32[]{:S(2)}) collective-permute-start(bf16[144,512]{1,0:T(8,128)(2,1)S(1)} %get-tuple-element.62), channel_id=1, source_target_pairs={{0,3},{1,2},{2,1},{3,0},{4,7},{5,6},{6,5},{7,4},{8,11},{9,10},{10,... | collective-permute-start | bytes 442376 | tf_op jit(solution)/shard_map/ppermute | solution.py:342
  109.7 12.9 %collective-permute-start.36 = (bf16[144,512]{1,0:T(8,128)(2,1)S(1)}, bf16[144,512]{1,0:T(8,128)(2,1)S(1)}, u32[]{:S(2)}, u32[]{:S(2)}) collective-permute-start(bf16[144,512]{1,0:T(8,128)(2,1)S(1)} %get-tuple-element.63), channel_id=1, source_target_pairs={{0,6},{1,7},{2,4},{3,5},{4,2},{5,3},{6,0},{7,1},{8,14},{9,15},{10,... | collective-permute-start | bytes 442376 | tf_op jit(solution)/shard_map/ppermute | solution.py:342
  110.9 11.7 %collective-permute-start.37 = (bf16[144,512]{1,0:T(8,128)(2,1)S(1)}, bf16[144,512]{1,0:T(8,128)(2,1)S(1)}, u32[]{:S(2)}, u32[]{:S(2)}) collective-permute-start(bf16[144,512]{1,0:T(8,128)(2,1)S(1)} %get-tuple-element.64), channel_id=1, source_target_pairs={{0,7},{1,6},{2,5},{3,4},{4,3},{5,2},{6,1},{7,0},{8,15},{9,14},{10,... | collective-permute-start | bytes 442376 | tf_op jit(solution)/shard_map/ppermute | solution.py:342
where the time goes:
time: 125 us; the launch traced here: 124 us
  starting transfers between devices  55.9 us (45%)
  waiting for transfers between devices  39.5 us (32%)
  Pallas kernels  20.2 us (16%)
  local copies, waits for them, and re-layouts  7.55 us (6%)
    ppermute x18, starting transfers between devices, xor_head(): return lax.ppermute(a, 'head', [(i, i ^ k) for i in range(GROUPS)])  31.9 us
    pallas_call x15, Pallas kernels, call(): pl.pallas_call(body, out_shape=outs, in_specs=smem(len(scalars)) + vmem(l...  20.2 us
    ppermute x6, starting transfers between devices, apart(): lax.ppermute(a, 'ctx', [(i, (i + 4 * k * (1 - 2 * (i % 2))) % 32) for i i...  15.6 us
    ppermute x2, waiting for transfers between devices, turn(): return lax.ppermute(a, 'ctx', [(i, (i + 4 * k) % 32) for i in range(32)])  14.3 us
    ppermute x12, waiting for transfers between devices, xor_ctx(): return lax.ppermute(a, 'ctx', [(i, i ^ k) for i in range(32)])  12 us
    ppermute x18, waiting for transfers between devices, xor_head(): return lax.ppermute(a, 'head', [(i, i ^ k) for i in range(GROUPS)])  9.63 us
    unnamed x30, local copies, waits for them, and re-layouts  7.55 us
    ppermute x12, starting transfers between devices, xor_ctx(): return lax.ppermute(a, 'ctx', [(i, i ^ k) for i in range(32)])  5.59 us
  transfers between devices with their start and end apart: 38, of which 14 were waited for; matrix products, arithmetic and copies ran while one was open for 0% of the time, Pallas kernels for 5%

commit v1 on v0

--- a/solution.py
+++ b/solution.py
@@ -271,13 +271,14 @@
 
 def sum_kernel(ids, *refs):
     core = ids[0] % 2
-    parts, (own, across, keep, send) = refs[:SIDE], refs[SIDE:]
+    across, *parts = refs[: 1 + SIDE]
+    own, keep, send = refs[1 + SIDE :]
     mine = functools.reduce(jnp.add, [p[core].astype(f32) for p in parts])
     keep[...] = own[...].astype(f32) + across[...].astype(f32) + mine
     send[...] = functools.reduce(jnp.add, [p[1 - core].astype(f32) for p in parts]).astype(bf16)
 
 
-def add_kernel(own, got, stay, send):
+def add_kernel(own, got, _, stay, send):
     stay[...] = own[:ROWS, :] + got[:ROWS, :].astype(f32)
     send[...] = (own[ROWS:, :] + got[ROWS:, :].astype(f32)).astype(bf16)
 
@@ -367,7 +368,7 @@
     ids = jnp.stack([lax.axis_index("ctx"), lax.axis_index("head")]).astype(jnp.int32)
     gain = norm_gain.reshape(1, D)
     xs = [xor_head(inputs, k) if k else inputs for k in KS]
-    ready = touch([w_key, w_value, gain])
+    ready = touch([w_key, w_value, gain, inputs, out_grad])
     kv, normed, mean, mean_row = call(
         norm_kernel,
         [ids],
@@ -402,7 +403,7 @@
     projected, dot_row = call(
         project_kernel,
         [ids],
-        [*xs, *dys, w_out, normed, w_query, ready_out, kvs[1], near[2]],
+        [*xs, *dys, w_out, normed, w_query, ready_out, near[1], near[2]],
         [shape((2 * ROWS, SHARE), bf16), shape((8, ROWS), f32)],
         24,
         flops=4 * ROWS * D * SHARE,
@@ -447,6 +448,7 @@
         ],
         name="gradient",
     )
+    far_part = turn(across, RING // 2)
     sends = call(
         pair_kernel,
         [ids],
@@ -459,7 +461,7 @@
     keep, give = call(
         sum_kernel,
         [ids],
-        [*[apart(a, -n) for n, a in enumerate(sends, 1)], own, turn(across, RING // 2)],
+        [far_part, *[apart(a, -n) for n, a in enumerate(sends, 1)], own],
         [shape((WIDE, HEAD_DIM), f32), part],
         8,
         moved=1 << 20,
@@ -469,7 +471,7 @@
     stay, dq_far = call(
         add_kernel,
         [],
-        [dq_own, xor_ctx(dq_send, 1)],
+        [dq_own, xor_ctx(dq_send, 1), far_part],
         [shape((ROWS, SHARE), f32), shape((ROWS, SHARE), bf16)],
         16,
         flops=4 * ROWS * SHARE,

time: 125 us -> 127 us (1.016)
  Pallas kernels: 20.2 us -> 22.4 us
  waiting for transfers between devices: 39.5 us -> 41.1 us
    ppermute x2, waiting for transfers between devices: 14.3 us -> 3.48 us  [turn(): return lax.ppermute(a, 'ctx', [(i, (i + 4 * k) % 32) for i in range(32)])]
    ppermute x6, waiting for transfers between devices: 3.52 us -> 13.7 us  [apart(): lax.ppermute(a, 'ctx', [(i, (i + 4 * k * (1 - 2 * (i % 2))) % 32) for i i...]
    ppermute x2, starting transfers between devices: 2.8 us -> 9.22 us  [turn(): return lax.ppermute(a, 'ctx', [(i, (i + 4 * k) % 32) for i in range(32)])]
    ppermute x18, waiting for transfers between devices: 9.63 us -> 14.2 us  [xor_head(): return lax.ppermute(a, 'head', [(i, i ^ k) for i in range(GROUPS)])]
    ppermute x18, starting transfers between devices: 31.9 us -> 27.9 us  [xor_head(): return lax.ppermute(a, 'head', [(i, i ^ k) for i in range(GROUPS)])]
    ppermute x6, starting transfers between devices: 15.6 us -> 11.9 us  [apart(): lax.ppermute(a, 'ctx', [(i, (i + 4 * k * (1 - 2 * (i % 2))) % 32) for i i...]
    ppermute x12, waiting for transfers between devices: 12 us -> 9.75 us  [xor_ctx(): return lax.ppermute(a, 'ctx', [(i, i ^ k) for i in range(32)])]
    pallas_call x15, Pallas kernels: 20.2 us -> 22.4 us  [call(): pl.pallas_call(body, out_shape=outs, in_specs=smem(len(scalars)) + vmem(l...]
  transfers between devices with their start and end apart: 38 -> 38, of which waited for: 14 -> 15; matrix products, arithmetic and copies ran while one was open for 0% -> 0% of each run, Pallas kernels for 5% -> 5%
where the time goes in v1:
time: 127 us; the launch traced here: 126 us
  starting transfers between devices  55 us (43%)
  waiting for transfers between devices  41.1 us (32%)
  Pallas kernels  22.4 us (18%)
  local copies, waits for them, and re-layouts  6.64 us (5%)
    ppermute x18, starting transfers between devices, xor_head(): return lax.ppermute(a, 'head', [(i, i ^ k) for i in range(GROUPS)])  27.9 us
    pallas_call x15, Pallas kernels, call(): pl.pallas_call(body, out_shape=outs, in_specs=smem(len(scalars)) + vmem(l...  22.4 us
    ppermute x18, waiting for transfers between devices, xor_head(): return lax.ppermute(a, 'head', [(i, i ^ k) for i in range(GROUPS)])  14.2 us
    ppermute x6, waiting for transfers between devices, apart(): lax.ppermute(a, 'ctx', [(i, (i + 4 * k * (1 - 2 * (i % 2))) % 32) for i i...  13.7 us
    ppermute x6, starting transfers between devices, apart(): lax.ppermute(a, 'ctx', [(i, (i + 4 * k * (1 - 2 * (i % 2))) % 32) for i i...  11.9 us
    ppermute x12, waiting for transfers between devices, xor_ctx(): return lax.ppermute(a, 'ctx', [(i, i ^ k) for i in range(32)])  9.75 us
    ppermute x2, starting transfers between devices, turn(): return lax.ppermute(a, 'ctx', [(i, (i + 4 * k) % 32) for i in range(32)])  9.22 us
    unnamed x26, local copies, waits for them, and re-layouts  6.64 us
  transfers between devices with their start and end apart: 38, of which 15 were waited for; matrix products, arithmetic and copies ran while one was open for 0% of the time, Pallas kernels for 5%

profile of v1, /device:TPU:32, one launch (start us, length us, event | category | flops | bytes accessed | tf_op | source)
XLA Modules:
  0.0 126.1 jit_solution(10546513877628124103)
XLA Ops:
  0.6 1.6 %collective-permute-start.6 = (bf16[128,512]{1,0:T(8,128)(2,1)}, bf16[128,512]{1,0:T(8,128)(2,1)S(1)}, u32[]{:S(2)}, u32[]{:S(2)}) collective-permute-start(bf16[128,512]{1,0:T(8,128)(2,1)} %refs_7_.1), channel_id=1, source_target_pairs={{0,1},{1,0},{2,3},{3,2},{4,5},{5,4},{6,7},{7,6},{8,9},{9,8},{10,11... | collective-permute-start | bytes 393224 | tf_op jit(solution)/shard_map/ppermute | solution.py:343
  2.2 1.6 %collective-permute-start.5 = (bf16[128,512]{1,0:T(8,128)(2,1)}, bf16[128,512]{1,0:T(8,128)(2,1)S(1)}, u32[]{:S(2)}, u32[]{:S(2)}) collective-permute-start(bf16[128,512]{1,0:T(8,128)(2,1)} %refs_7_.1), channel_id=1, source_target_pairs={{0,2},{1,3},{2,0},{3,1},{4,6},{5,7},{6,4},{7,5},{8,10},{9,11},{10,... | collective-permute-start | bytes 393224 | tf_op jit(solution)/shard_map/ppermute | solution.py:343
  3.8 2.9 %collective-permute-start.4 = (bf16[128,512]{1,0:T(8,128)(2,1)}, bf16[128,512]{1,0:T(8,128)(2,1)S(1)}, u32[]{:S(2)}, u32[]{:S(2)}) collective-permute-start(bf16[128,512]{1,0:T(8,128)(2,1)} %refs_7_.1), channel_id=1, source_target_pairs={{0,4},{1,5},{2,6},{3,7},{4,0},{5,1},{6,2},{7,3},{8,12},{9,13},{10,... | collective-permute-start | bytes 393224 | tf_op jit(solution)/shard_map/ppermute | solution.py:343
  6.7 0.6 collective-permute-start.3
  7.3 1.4 %collective-permute-start.2 = (bf16[128,512]{1,0:T(8,128)(2,1)}, bf16[128,512]{1,0:T(8,128)(2,1)S(1)}, u32[]{:S(2)}, u32[]{:S(2)}) collective-permute-start(bf16[128,512]{1,0:T(8,128)(2,1)} %refs_7_.1), channel_id=1, source_target_pairs={{0,3},{1,2},{2,1},{3,0},{4,7},{5,6},{6,5},{7,4},{8,11},{9,10},{10,... | collective-permute-start | bytes 393224 | tf_op jit(solution)/shard_map/ppermute | solution.py:343
  8.7 3.0 %collective-permute-start.1 = (bf16[128,512]{1,0:T(8,128)(2,1)}, bf16[128,512]{1,0:T(8,128)(2,1)S(1)}, u32[]{:S(2)}, u32[]{:S(2)}) collective-permute-start(bf16[128,512]{1,0:T(8,128)(2,1)} %refs_7_.1), channel_id=1, source_target_pairs={{0,6},{1,7},{2,4},{3,5},{4,2},{5,3},{6,0},{7,1},{8,14},{9,15},{10,... | collective-permute-start | bytes 393224 | tf_op jit(solution)/shard_map/ppermute | solution.py:343
  11.7 4.0 %collective-permute-start = (bf16[128,512]{1,0:T(8,128)(2,1)}, bf16[128,512]{1,0:T(8,128)(2,1)S(1)}, u32[]{:S(2)}, u32[]{:S(2)}) collective-permute-start(bf16[128,512]{1,0:T(8,128)(2,1)} %refs_7_.1), channel_id=1, source_target_pairs={{0,7},{1,6},{2,5},{3,4},{4,3},{5,2},{6,1},{7,0},{8,15},{9,14},{10,... | collective-permute-start | bytes 393224 | tf_op jit(solution)/shard_map/ppermute | solution.py:343
  15.7 1.4 %copy-done.3 = bf16[4096,128]{1,0:T(8,128)(2,1)S(1)} copy-done((bf16[4096,128]{1,0:T(8,128)(2,1)S(1)}, bf16[4096,128]{1,0:T(8,128)(2,1)}, u32[]{:S(2)}) %copy-start.3) | copy-done | bytes 1048600
  17.1 1.4 %copy-done.5 = bf16[4096,128]{1,0:T(8,128)(2,1)S(1)} copy-done((bf16[4096,128]{1,0:T(8,128)(2,1)S(1)}, bf16[4096,128]{1,0:T(8,128)(2,1)}, u32[]{:S(2)}) %copy-start.5) | copy-done | bytes 1048600
  18.5 0.9 copy-done.7
  19.4 0.7 copy-done.9
  20.1 0.9 touch.2.refs_11_
  21.0 1.5 %collective-permute-start.7 = (bf16[128,512]{1,0:T(8,128)(2,1)}, bf16[128,512]{1,0:T(8,128)(2,1)S(1)}, u32[]{:S(2)}, u32[]{:S(2)}) collective-permute-start(bf16[128,512]{1,0:T(8,128)(2,1)} %refs_8_.1), channel_id=1, source_target_pairs={{0,1},{1,0},{2,3},{3,2},{4,5},{5,4},{6,7},{7,6},{8,9},{9,8},{10,11... | collective-permute-start | bytes 393224 | tf_op jit(solution)/shard_map/ppermute | solution.py:343
  22.6 1.8 %norm_kv.1 = (bf16[128,256]{1,0:T(8,128)(2,1)S(1)}, bf16[128,4096]{1,0:T(8,128)(2,1)S(1)}, f32[128,128]{1,0:T(8,128)S(1)}, f32[8,128]{1,0:T(8,128)S(1)}) custom-call(s32[2]{0:T(128)S(1)} %pad_add_fusion.ids, bf16[128,512]{1,0:T(8,128)(2,1)S(1)} %copy-done.7, bf16[128,512]{1,0:T(8,128)(2,1)S(1)} %collective-permute-done.refs_1_.refs_3_, ...), custom_call_target="tpu_custom_call" | custom-call | flops 268435456 | bytes 5242880 | tf_op jit(solution)/shard_map/norm_kv/pallas_call | solution.py:55
  24.4 1.7 %collective-permute-done.7.other = bf16[128,512]{1,0:T(8,128)(2,1)S(1)} collective-permute-done((bf16[128,512]{1,0:T(8,128)(2,1)}, bf16[128,512]{1,0:T(8,128)(2,1)S(1)}, u32[]{:S(2)}, u32[]{:S(2)}) %collective-permute-start.7) | collective-permute-done | bytes 131104 | tf_op jit(solution)/shard_map/ppermute | solution.py:343
  26.2 0.9 hold.1.refs_8_
  27.1 0.1 collective-permute-start.10
  27.2 2.6 %collective-permute-start.9 = (bf16[256,512]{1,0:T(8,128)(2,1)S(1)}, bf16[256,512]{1,0:T(8,128)(2,1)S(1)}, u32[]{:S(2)}, u32[]{:S(2)}) collective-permute-start(bf16[256,512]{1,0:T(8,128)(2,1)S(1)} %hold.1.refs_8_), channel_id=1, source_target_pairs={{0,4},{1,5},{2,6},{3,7},{4,0},{5,1},{6,2},{7,3},{8,12},{9,13},{10,... | collective-permute-start | bytes 786440 | tf_op jit(solution)/shard_map/ppermute | solution.py:343
  29.9 1.4 %collective-permute-start.8 = (bf16[256,512]{1,0:T(8,128)(2,1)S(1)}, bf16[256,512]{1,0:T(8,128)(2,1)S(1)}, u32[]{:S(2)}, u32[]{:S(2)}) collective-permute-start(bf16[256,512]{1,0:T(8,128)(2,1)S(1)} %hold.1.refs_8_), channel_id=1, source_target_pairs={{0,2},{1,3},{2,0},{3,1},{4,6},{5,7},{6,4},{7,5},{8,10},{9,11},{10,... | collective-permute-start | bytes 786440 | tf_op jit(solution)/shard_map/ppermute | solution.py:343
  31.3 1.3 collective-permute-done.11.other
  32.6 0.6 join.1
  33.1 5.9 %collective-permute-start.13 = (bf16[256,256]{1,0:T(8,128)(2,1)S(1)}, bf16[256,256]{1,0:T(8,128)(2,1)S(1)}, u32[]{:S(2)}, u32[]{:S(2)}) collective-permute-start(bf16[256,256]{1,0:T(8,128)(2,1)S(1)} %join.1), channel_id=1, source_target_pairs={{0,96},{8,168},{16,112},{24,184},{32,128},{40,200},{48,144},{56,21... | collective-permute-start | bytes 393224 | tf_op jit(solution)/shard_map/ppermute | solution.py:359
  39.0 1.5 %collective-permute-start.12 = (bf16[256,256]{1,0:T(8,128)(2,1)S(1)}, bf16[256,256]{1,0:T(8,128)(2,1)S(1)}, u32[]{:S(2)}, u32[]{:S(2)}) collective-permute-start(bf16[256,256]{1,0:T(8,128)(2,1)S(1)} %join.1), channel_id=1, source_target_pairs={{0,64},{8,200},{16,80},{24,216},{32,96},{40,232},{48,112},{56,248}... | collective-permute-start | bytes 393224 | tf_op jit(solution)/shard_map/ppermute | solution.py:359
  40.5 2.2 %copy-done.1 = bf16[512,4096]{1,0:T(8,128)(2,1)S(1)} copy-done((bf16[512,4096]{1,0:T(8,128)(2,1)S(1)}, bf16[512,4096]{1,0:T(8,128)(2,1)}, u32[]{:S(2)}) %copy-start.1) | copy-done | bytes 4194328
  42.7 3.2 %collective-permute-done.13.refs_17_.refs_2_.refs_8_ = bf16[256,256]{1,0:T(8,128)(2,1)S(1)} collective-permute-done((bf16[256,256]{1,0:T(8,128)(2,1)S(1)}, bf16[256,256]{1,0:T(8,128)(2,1)S(1)}, u32[]{:S(2)}, u32[]{:S(2)}) %collective-permute-start.13) | collective-permute-done | bytes 131104 | tf_op jit(solution)/shard_map/ppermute | solution.py:359
  46.0 2.4 %collective-permute-done.12.refs_16_.refs_1_.refs_7_ = bf16[256,256]{1,0:T(8,128)(2,1)S(1)} collective-permute-done((bf16[256,256]{1,0:T(8,128)(2,1)S(1)}, bf16[256,256]{1,0:T(8,128)(2,1)S(1)}, u32[]{:S(2)}, u32[]{:S(2)}) %collective-permute-start.12) | collective-permute-done | bytes 131104 | tf_op jit(solution)/shard_map/ppermute | solution.py:359
  48.4 2.8 %project.1 = (bf16[256,512]{1,0:T(8,128)(2,1)S(1)}, f32[8,128]{1,0:T(8,128)S(1)}) custom-call(s32[2]{0:T(128)S(1)} %pad_add_fusion.ids, bf16[128,512]{1,0:T(8,128)(2,1)S(1)} %copy-done.8, bf16[128,512]{1,0:T(8,128)(2,1)S(1)} %collective-permute-done.refs_1_.refs_3_, bf16[128,512]{1,0:T(8,128)(2,1)S(1)} %collective-permute-done.1.refs_2_.refs_4_, ...), custom_call_target="tpu_custom_call" | custom-call | flops 1073741824 | bytes 10485760 | tf_op jit(solution)/shard_map/project/pallas_call | solution.py:55
  51.2 3.1 %collective-permute-start.15 = (bf16[256,512]{1,0:T(8,128)(2,1)S(1)}, bf16[256,512]{1,0:T(8,128)(2,1)S(1)}, u32[]{:S(2)}, u32[]{:S(2)}) collective-permute-start(bf16[256,512]{1,0:T(8,128)(2,1)S(1)} %get-tuple-element.38.refs_0_), channel_id=1, source_target_pairs={{0,16},{8,24},{16,0},{24,8},{32,48},{40,56},{48,32},{56,40},{64,80... | collective-permute-start | bytes 786440 | tf_op jit(solution)/shard_map/ppermute | solution.py:347
  54.3 4.3 %collective-permute-start.17 = (bf16[128,256]{1,0:T(8,128)(2,1)S(1)}, bf16[128,256]{1,0:T(8,128)(2,1)S(1)}, u32[]{:S(2)}, u32[]{:S(2)}) collective-permute-start(bf16[128,256]{1,0:T(8,128)(2,1)S(1)} %get-tuple-element.36.refs_0_.mine.refs_4_), channel_id=1, source_target_pairs={{0,128},{8,136},{16,144},{24,152},{32,160},{40,168},{48,176},{56,1... | collective-permute-start | bytes 196616 | tf_op jit(solution)/shard_map/ppermute | solution.py:355
  58.6 0.6 collective-permute-done.15.refs_2_
  59.2 3.5 %collective-permute-done.17.refs_3_.refs_5_ = bf16[128,256]{1,0:T(8,128)(2,1)S(1)} collective-permute-done((bf16[128,256]{1,0:T(8,128)(2,1)S(1)}, bf16[128,256]{1,0:T(8,128)(2,1)S(1)}, u32[]{:S(2)}, u32[]{:S(2)}) %collective-permute-start.17) | collective-permute-done | bytes 65568 | tf_op jit(solution)/shard_map/ppermute | solution.py:355
  62.6 0.6 sort.1
  63.2 0.1 collective-permute-start.19
  63.3 1.4 %collective-permute-done.19.refs_9_ = bf16[384,256]{1,0:T(8,128)(2,1)S(1)} collective-permute-done((bf16[384,256]{1,0:T(8,128)(2,1)S(1)}, bf16[384,256]{1,0:T(8,128)(2,1)S(1)}, u32[]{:S(2)}, u32[]{:S(2)}) %collective-permute-start.19) | collective-permute-done | bytes 196640 | tf_op jit(solution)/shard_map/ppermute | solution.py:347
  64.8 4.7 %softmax.1 = (bf16[2048,1024]{1,0:T(8,128)(2,1)S(1)}, f32[128,128]{1,0:T(8,128)S(1)}, bf16[1024,128]{1,0:T(8,128)(2,1)S(1)}, bf16[1024,128]{1,0:T(8,128)(2,1)S(1)}) custom-call(s32[2]{0:T(128)S(1)} %pad_add_fusion.ids, s32[64]{0:T(128)S(1)} %copy-done.11, s32[8]{0:T(128)S(1)} %copy-done.12, bf16[256,512]{1,0:T(8,128)(2,1)S(1)} %get-tuple-element.38.refs_0_, ...), custom_call_target="tpu_custom_call" | custom-call | flops 1073741824 | bytes 6291456 | tf_op jit(solution)/shard_map/softmax/pallas_call | solution.py:55
  69.5 0.6 collective-permute-start.21
  70.1 5.2 %collective-permute-done.21.refs_9_ = f32[128,128]{1,0:T(8,128)S(1)} collective-permute-done((f32[128,128]{1,0:T(8,128)S(1)}, f32[128,128]{1,0:T(8,128)S(1)}, u32[]{:S(2)}, u32[]{:S(2)}) %collective-permute-start.21) | collective-permute-done | bytes 65568 | tf_op jit(solution)/shard_map/ppermute | solution.py:347
  75.3 1.2 collective-permute-done.22.refs_10_
  76.6 4.1 %gradient.1 = (bf16[256,128]{1,0:T(8,128)(2,1)S(1)}, bf16[256,128]{1,0:T(8,128)(2,1)S(1)}, bf16[3,256,128]{2,1,0:T(8,128)(2,1)S(1)}, bf16[3,256,128]{2,1,0:T(8,1...) custom-call(bf16[256,512]{1,0:T(8,128)(2,1)S(1)} %get-tuple-element.38.refs_0_, ...), custom_call_target="tpu_custom_call" | custom-call | flops 2147483648 | bytes 6291456 | tf_op jit(solution)/shard_map/gradient/pallas_call | solution.py:55
  80.7 0.5 collective-permute-start.29
  81.1 0.3 collective-permute-start.24
  81.5 5.0 %collective-permute-start.23 = (bf16[256,128]{1,0:T(8,128)(2,1)S(1)}, bf16[256,128]{1,0:T(8,128)(2,1)S(1)}, u32[]{:S(2)}, u32[]{:S(2)}) collective-permute-start(bf16[256,128]{1,0:T(8,128)(2,1)S(1)} %get-tuple-element.43), channel_id=1, source_target_pairs={{0,128},{8,136},{16,144},{24,152},{32,160},{40,168},{48,176},{56,1... | collective-permute-start | bytes 196616 | tf_op jit(solution)/shard_map/ppermute | solution.py:355
  86.5 0.6 pair.1
  87.0 1.8 %collective-permute-start.25 = (bf16[2,256,128]{2,1,0:T(8,128)(2,1)S(1)}, bf16[2,256,128]{2,1,0:T(8,128)(2,1)S(1)}, u32[]{:S(2)}, u32[]{:S(2)}) collective-permute-start(bf16[2,256,128]{2,1,0:T(8,128)(2,1)S(1)} %get-tuple-element.46), channel_id=1, source_target_pairs={{0,224},{8,40},{16,240},{24,56},{32,0},{40,72},{48,16},{56,88},{64... | collective-permute-start | bytes 393224 | tf_op jit(solution)/shard_map/ppermute | solution.py:359
  88.8 0.2 collective-permute-start.26
  89.0 2.5 %collective-permute-start.27 = (bf16[2,256,128]{2,1,0:T(8,128)(2,1)S(1)}, bf16[2,256,128]{2,1,0:T(8,128)(2,1)S(1)}, u32[]{:S(2)}, u32[]{:S(2)}) collective-permute-start(bf16[2,256,128]{2,1,0:T(8,128)(2,1)S(1)} %get-tuple-element.48), channel_id=1, source_target_pairs={{0,160},{8,104},{16,176},{24,120},{32,192},{40,136},{48,208},{56,1... | collective-permute-start | bytes 393224 | tf_op jit(solution)/shard_map/ppermute | solution.py:359
  91.6 0.6 collective-permute-start.30
  92.3 2.7 %collective-permute-done.26.refs_2_ = bf16[2,256,128]{2,1,0:T(8,128)(2,1)S(1)} collective-permute-done((bf16[2,256,128]{2,1,0:T(8,128)(2,1)S(1)}, bf16[2,256,128]{2,1,0:T(8,128)(2,1)S(1)}, u32[]{:S(2)}, u32[]{:S(2)}) %collective-permute-start.26) | collective-permute-done | bytes 131104 | tf_op jit(solution)/shard_map/ppermute | solution.py:359
  95.0 5.3 %collective-permute-done.27.refs_3_ = bf16[2,256,128]{2,1,0:T(8,128)(2,1)S(1)} collective-permute-done((bf16[2,256,128]{2,1,0:T(8,128)(2,1)S(1)}, bf16[2,256,128]{2,1,0:T(8,128)(2,1)S(1)}, u32[]{:S(2)}, u32[]{:S(2)}) %collective-permute-start.27) | collective-permute-done | bytes 131104 | tf_op jit(solution)/shard_map/ppermute | solution.py:359
  100.3 0.6 sum.1
  100.9 0.6 collective-permute-start.28
  101.5 1.5 %back_query.1.refs_11_ = f32[128,4096]{1,0:T(8,128)S(1)} custom-call(f32[128,512]{1,0:T(8,128)S(1)} %get-tuple-element.54.stay, bf16[128,512]{1,0:T(8,128)(2,1)S(1)} %collective-permute-done.30.got, bf16[4096,512]{1,0:T(8,128)(2,1)S(1)} %copy-done), custom_call_target="tpu_custom_call" | custom-call | flops 536870912 | bytes 6291456 | tf_op jit(solution)/shard_map/back_query/pallas_call | solution.py:55
  103.0 1.5 %back_kv.1 = (f32[128,512]{1,0:T(8,128)S(1)}, bf16[16,256]{1,0:T(8,128)(2,1)S(1)}, bf16[144,512]{1,0:T(8,128)(2,1)S(1)}, bf16[144,512]{1,0:T(8,128)(2,1)S(1)}, b...) custom-call(s32[2]{0:T(128)S(1)} %pad_add_fusion.ids, ...), custom_call_target="tpu_custom_call" | custom-call | flops 268435456 | bytes 7340032 | tf_op jit(solution)/shard_map/back_kv/pallas_call | solution.py:55
  104.5 0.7 collective-permute-start.31
  105.2 1.1 collective-permute-start.32
  106.3 0.4 collective-permute-start.33
  106.7 3.6 %collective-permute-start.34 = (bf16[144,512]{1,0:T(8,128)(2,1)S(1)}, bf16[144,512]{1,0:T(8,128)(2,1)S(1)}, u32[]{:S(2)}, u32[]{:S(2)}) collective-permute-start(bf16[144,512]{1,0:T(8,128)(2,1)S(1)} %get-tuple-element.61), channel_id=1, source_target_pairs={{0,5},{1,4},{2,7},{3,6},{4,1},{5,0},{6,3},{7,2},{8,13},{9,12},{10,... | collective-permute-start | bytes 442376 | tf_op jit(solution)/shard_map/ppermute | solution.py:343
  110.3 1.3 %collective-permute-start.35 = (bf16[144,512]{1,0:T(8,128)(2,1)S(1)}, bf16[144,512]{1,0:T(8,128)(2,1)S(1)}, u32[]{:S(2)}, u32[]{:S(2)}) collective-permute-start(bf16[144,512]{1,0:T(8,128)(2,1)S(1)} %get-tuple-element.62), channel_id=1, source_target_pairs={{0,3},{1,2},{2,1},{3,0},{4,7},{5,6},{6,5},{7,4},{8,11},{9,10},{10,... | collective-permute-start | bytes 442376 | tf_op jit(solution)/shard_map/ppermute | solution.py:343
  111.6 0.1 collective-permute-start.36
  111.7 5.2 %collective-permute-done.32.refs_1_ = bf16[144,512]{1,0:T(8,128)(2,1)S(1)} collective-permute-done((bf16[144,512]{1,0:T(8,128)(2,1)S(1)}, bf16[144,512]{1,0:T(8,128)(2,1)S(1)}, u32[]{:S(2)}, u32[]{:S(2)}) %collective-permute-start.32) | collective-permute-done | bytes 147488 | tf_op jit(solution)/shard_map/ppermute | solution.py:343
  116.9 2.9 %collective-permute-done.33.refs_2_ = bf16[144,512]{1,0:T(8,128)(2,1)S(1)} collective-permute-done((bf16[144,512]{1,0:T(8,128)(2,1)S(1)}, bf16[144,512]{1,0:T(8,128)(2,1)S(1)}, u32[]{:S(2)}, u32[]{:S(2)}) %collective-permute-start.33) | collective-permute-done | bytes 147488 | tf_op jit(solution)/shard_map/ppermute | solution.py:343
  119.8 2.3 %collective-permute-done.36.refs_5_ = bf16[144,512]{1,0:T(8,128)(2,1)S(1)} collective-permute-done((bf16[144,512]{1,0:T(8,128)(2,1)S(1)}, bf16[144,512]{1,0:T(8,128)(2,1)S(1)}, u32[]{:S(2)}, u32[]{:S(2)}) %collective-permute-start.36) | collective-permute-done | bytes 147488 | tf_op jit(solution)/shard_map/ppermute | solution.py:343
  122.1 2.1 %collective-permute-done.37.refs_6_ = bf16[144,512]{1,0:T(8,128)(2,1)S(1)} collective-permute-done((bf16[144,512]{1,0:T(8,128)(2,1)S(1)}, bf16[144,512]{1,0:T(8,128)(2,1)S(1)}, u32[]{:S(2)}, u32[]{:S(2)}) %collective-permute-start.37) | collective-permute-done | bytes 147488 | tf_op jit(solution)/shard_map/ppermute | solution.py:343
  124.2 1.9 %last.1 = (bf16[128,512]{1,0:T(8,128)(2,1)}, f32[1,128]{1,0:T(1,128)}) custom-call(s32[2]{0:T(128)S(1)} %pad_add_fusion.ids, f32[128,512]{1,0:T(8,128)S(1)} %get-tuple-element.56.own, bf16[16,256]{1,0:T(8,128)(2,1)S(1)} %get-tuple-element.57.own_row, bf16[144,512]{1,0:T(8,128)(2,1)S(1)} %collective-permute-done.31.refs_0_, ...), custom_call_target="tpu_custom_call" | custom-call | flops 655360 | bytes 3145728 | tf_op jit(solution)/shard_map/last/pallas_call | solution.py:55
  (54 shorter events, 0.2 us)
Async XLA Ops:
  0.6 8.0 %collective-permute-start.6 = (bf16[128,512]{1,0:T(8,128)(2,1)}, bf16[128,512]{1,0:T(8,128)(2,1)S(1)}, u32[]{:S(2)}, u32[]{:S(2)}) collective-permute-start(bf16[128,512]{1,0:T(8,128)(2,1)} %refs_7_.1), channel_id=1, source_target_pairs={{0,1},{1,0},{2,3},{3,2},{4,5},{5,4},{6,7},{7,6},{8,9},{9,8},{10,11... | collective-permute-start | bytes 393224 | tf_op jit(solution)/shard_map/ppermute | solution.py:343
  2.2 9.5 %collective-permute-start.5 = (bf16[128,512]{1,0:T(8,128)(2,1)}, bf16[128,512]{1,0:T(8,128)(2,1)S(1)}, u32[]{:S(2)}, u32[]{:S(2)}) collective-permute-start(bf16[128,512]{1,0:T(8,128)(2,1)} %refs_7_.1), channel_id=1, source_target_pairs={{0,2},{1,3},{2,0},{3,1},{4,6},{5,7},{6,4},{7,5},{8,10},{9,11},{10,... | collective-permute-start | bytes 393224 | tf_op jit(solution)/shard_map/ppermute | solution.py:343
  3.8 17.2 %collective-permute-start.4 = (bf16[128,512]{1,0:T(8,128)(2,1)}, bf16[128,512]{1,0:T(8,128)(2,1)S(1)}, u32[]{:S(2)}, u32[]{:S(2)}) collective-permute-start(bf16[128,512]{1,0:T(8,128)(2,1)} %refs_7_.1), channel_id=1, source_target_pairs={{0,4},{1,5},{2,6},{3,7},{4,0},{5,1},{6,2},{7,3},{8,12},{9,13},{10,... | collective-permute-start | bytes 393224 | tf_op jit(solution)/shard_map/ppermute | solution.py:343
  6.7 15.9 %collective-permute-start.3 = (bf16[128,512]{1,0:T(8,128)(2,1)}, bf16[128,512]{1,0:T(8,128)(2,1)S(1)}, u32[]{:S(2)}, u32[]{:S(2)}) collective-permute-start(bf16[128,512]{1,0:T(8,128)(2,1)} %refs_7_.1), channel_id=1, source_target_pairs={{0,5},{1,4},{2,7},{3,6},{4,1},{5,0},{6,3},{7,2},{8,13},{9,12},{10,... | collective-permute-start | bytes 393224 | tf_op jit(solution)/shard_map/ppermute | solution.py:343
  7.3 15.3 %collective-permute-start.2 = (bf16[128,512]{1,0:T(8,128)(2,1)}, bf16[128,512]{1,0:T(8,128)(2,1)S(1)}, u32[]{:S(2)}, u32[]{:S(2)}) collective-permute-start(bf16[128,512]{1,0:T(8,128)(2,1)} %refs_7_.1), channel_id=1, source_target_pairs={{0,3},{1,2},{2,1},{3,0},{4,7},{5,6},{6,5},{7,4},{8,11},{9,10},{10,... | collective-permute-start | bytes 393224 | tf_op jit(solution)/shard_map/ppermute | solution.py:343
  8.7 13.9 %collective-permute-start.1 = (bf16[128,512]{1,0:T(8,128)(2,1)}, bf16[128,512]{1,0:T(8,128)(2,1)S(1)}, u32[]{:S(2)}, u32[]{:S(2)}) collective-permute-start(bf16[128,512]{1,0:T(8,128)(2,1)} %refs_7_.1), channel_id=1, source_target_pairs={{0,6},{1,7},{2,4},{3,5},{4,2},{5,3},{6,0},{7,1},{8,14},{9,15},{10,... | collective-permute-start | bytes 393224 | tf_op jit(solution)/shard_map/ppermute | solution.py:343
  11.7 10.9 %collective-permute-start = (bf16[128,512]{1,0:T(8,128)(2,1)}, bf16[128,512]{1,0:T(8,128)(2,1)S(1)}, u32[]{:S(2)}, u32[]{:S(2)}) collective-permute-start(bf16[128,512]{1,0:T(8,128)(2,1)} %refs_7_.1), channel_id=1, source_target_pairs={{0,7},{1,6},{2,5},{3,4},{4,3},{5,2},{6,1},{7,0},{8,15},{9,14},{10,... | collective-permute-start | bytes 393224 | tf_op jit(solution)/shard_map/ppermute | solution.py:343
  15.7 24.8 %copy-start = (bf16[4096,512]{1,0:T(8,128)(2,1)S(1)}, bf16[4096,512]{1,0:T(8,128)(2,1)}, u32[]{:S(2)}) copy-start(bf16[4096,512]{1,0:T(8,128)(2,1)} %w_query.1) | copy-start | bytes 12582916
  15.7 1.4 %copy-start.3 = (bf16[4096,128]{1,0:T(8,128)(2,1)S(1)}, bf16[4096,128]{1,0:T(8,128)(2,1)}, u32[]{:S(2)}) copy-start(bf16[4096,128]{1,0:T(8,128)(2,1)} %refs_12_.3) | copy-start | bytes 3145732
  17.1 1.4 %copy-start.5 = (bf16[4096,128]{1,0:T(8,128)(2,1)S(1)}, bf16[4096,128]{1,0:T(8,128)(2,1)}, u32[]{:S(2)}) copy-start(bf16[4096,128]{1,0:T(8,128)(2,1)} %refs_13_.1) | copy-start | bytes 3145732
  18.5 0.9 copy-start.7
  19.4 0.7 copy-start.9
  21.0 5.2 %collective-permute-start.7 = (bf16[128,512]{1,0:T(8,128)(2,1)}, bf16[128,512]{1,0:T(8,128)(2,1)S(1)}, u32[]{:S(2)}, u32[]{:S(2)}) collective-permute-start(bf16[128,512]{1,0:T(8,128)(2,1)} %refs_8_.1), channel_id=1, source_target_pairs={{0,1},{1,0},{2,3},{3,2},{4,5},{5,4},{6,7},{7,6},{8,9},{9,8},{10,11... | collective-permute-start | bytes 393224 | tf_op jit(solution)/shard_map/ppermute | solution.py:343
  27.1 21.3 %collective-permute-start.10 = (bf16[256,512]{1,0:T(8,128)(2,1)S(1)}, bf16[256,512]{1,0:T(8,128)(2,1)S(1)}, u32[]{:S(2)}, u32[]{:S(2)}) collective-permute-start(bf16[256,512]{1,0:T(8,128)(2,1)S(1)} %hold.1.refs_8_), channel_id=1, source_target_pairs={{0,6},{1,7},{2,4},{3,5},{4,2},{5,3},{6,0},{7,1},{8,14},{9,15},{10,... | collective-permute-start | bytes 786440 | tf_op jit(solution)/shard_map/ppermute | solution.py:343
  27.2 21.1 %collective-permute-start.9 = (bf16[256,512]{1,0:T(8,128)(2,1)S(1)}, bf16[256,512]{1,0:T(8,128)(2,1)S(1)}, u32[]{:S(2)}, u32[]{:S(2)}) collective-permute-start(bf16[256,512]{1,0:T(8,128)(2,1)S(1)} %hold.1.refs_8_), channel_id=1, source_target_pairs={{0,4},{1,5},{2,6},{3,7},{4,0},{5,1},{6,2},{7,3},{8,12},{9,13},{10,... | collective-permute-start | bytes 786440 | tf_op jit(solution)/shard_map/ppermute | solution.py:343
  29.9 18.5 %collective-permute-start.8 = (bf16[256,512]{1,0:T(8,128)(2,1)S(1)}, bf16[256,512]{1,0:T(8,128)(2,1)S(1)}, u32[]{:S(2)}, u32[]{:S(2)}) collective-permute-start(bf16[256,512]{1,0:T(8,128)(2,1)S(1)} %hold.1.refs_8_), channel_id=1, source_target_pairs={{0,2},{1,3},{2,0},{3,1},{4,6},{5,7},{6,4},{7,5},{8,10},{9,11},{10,... | collective-permute-start | bytes 786440 | tf_op jit(solution)/shard_map/ppermute | solution.py:343
  31.3 1.3 collective-permute-start.11
  33.1 12.8 %collective-permute-start.13 = (bf16[256,256]{1,0:T(8,128)(2,1)S(1)}, bf16[256,256]{1,0:T(8,128)(2,1)S(1)}, u32[]{:S(2)}, u32[]{:S(2)}) collective-permute-start(bf16[256,256]{1,0:T(8,128)(2,1)S(1)} %join.1), channel_id=1, source_target_pairs={{0,96},{8,168},{16,112},{24,184},{32,128},{40,200},{48,144},{56,21... | collective-permute-start | bytes 393224 | tf_op jit(solution)/shard_map/ppermute | solution.py:359
  39.0 9.3 %collective-permute-start.12 = (bf16[256,256]{1,0:T(8,128)(2,1)S(1)}, bf16[256,256]{1,0:T(8,128)(2,1)S(1)}, u32[]{:S(2)}, u32[]{:S(2)}) collective-permute-start(bf16[256,256]{1,0:T(8,128)(2,1)S(1)} %join.1), channel_id=1, source_target_pairs={{0,64},{8,200},{16,80},{24,216},{32,96},{40,232},{48,112},{56,248}... | collective-permute-start | bytes 393224 | tf_op jit(solution)/shard_map/ppermute | solution.py:359
  40.5 2.2 %copy-start.1 = (bf16[512,4096]{1,0:T(8,128)(2,1)S(1)}, bf16[512,4096]{1,0:T(8,128)(2,1)}, u32[]{:S(2)}) copy-start(bf16[512,4096]{1,0:T(8,128)(2,1)} %refs_12_.2) | copy-start | bytes 12582916
  42.7 5.7 %copy-start.2 = (bf16[512,4096]{1,0:T(8,128)(2,1)S(1)}, bf16[512,4096]{1,0:T(8,128)(2,1)}, u32[]{:S(2)}) copy-start(bf16[512,4096]{1,0:T(8,128)(2,1)} %refs_12_.2) | copy-start | bytes 12582916
  42.7 5.7 %copy-start.8 = (bf16[128,512]{1,0:T(8,128)(2,1)S(1)}, bf16[128,512]{1,0:T(8,128)(2,1)}, u32[]{:S(2)}) copy-start(bf16[128,512]{1,0:T(8,128)(2,1)} %refs_7_.1) | copy-start | bytes 393220
  42.7 22.0 %copy-start.11 = (s32[64]{0:T(128)S(1)}, s32[64]{0:T(128)}, u32[]{:S(2)}) copy-start(s32[64]{0:T(128)} %order.1) | copy-start | bytes 772
  42.7 22.0 %copy-start.12 = (s32[8]{0:T(128)S(1)}, s32[8]{0:T(128)}, u32[]{:S(2)}) copy-start(s32[8]{0:T(128)} %lengths.1) | copy-start | bytes 100
  51.2 8.0 %collective-permute-start.15 = (bf16[256,512]{1,0:T(8,128)(2,1)S(1)}, bf16[256,512]{1,0:T(8,128)(2,1)S(1)}, u32[]{:S(2)}, u32[]{:S(2)}) collective-permute-start(bf16[256,512]{1,0:T(8,128)(2,1)S(1)} %get-tuple-element.38.refs_0_), channel_id=1, source_target_pairs={{0,16},{8,24},{16,0},{24,8},{32,48},{40,56},{48,32},{56,40},{64,80... | collective-permute-start | bytes 786440 | tf_op jit(solution)/shard_map/ppermute | solution.py:347
  54.3 8.3 %collective-permute-start.18 = (bf16[256,256]{1,0:T(8,128)(2,1)S(1)}, bf16[256,256]{1,0:T(8,128)(2,1)S(1)}, u32[]{:S(2)}, u32[]{:S(2)}) collective-permute-start(bf16[256,256]{1,0:T(8,128)(2,1)S(1)} %join.1), channel_id=1, source_target_pairs={{0,32},{8,232},{16,48},{24,248},{32,64},{40,8},{48,80},{56,24},{64... | collective-permute-start | bytes 393224 | tf_op jit(solution)/shard_map/ppermute | solution.py:359
  54.3 8.3 %collective-permute-start.17 = (bf16[128,256]{1,0:T(8,128)(2,1)S(1)}, bf16[128,256]{1,0:T(8,128)(2,1)S(1)}, u32[]{:S(2)}, u32[]{:S(2)}) collective-permute-start(bf16[128,256]{1,0:T(8,128)(2,1)S(1)} %get-tuple-element.36.refs_0_.mine.refs_4_), channel_id=1, source_target_pairs={{0,128},{8,136},{16,144},{24,152},{32,160},{40,168},{48,176},{56,1... | collective-permute-start | bytes 196616 | tf_op jit(solution)/shard_map/ppermute | solution.py:355
  58.6 6.2 %collective-permute-start.14 = (bf16[256,512]{1,0:T(8,128)(2,1)S(1)}, bf16[256,512]{1,0:T(8,128)(2,1)S(1)}, u32[]{:S(2)}, u32[]{:S(2)}) collective-permute-start(bf16[256,512]{1,0:T(8,128)(2,1)S(1)} %get-tuple-element.38.refs_0_), channel_id=1, source_target_pairs={{0,8},{8,0},{16,24},{24,16},{32,40},{40,32},{48,56},{56,48},{64,72... | collective-permute-start | bytes 786440 | tf_op jit(solution)/shard_map/ppermute | solution.py:347
  59.2 5.6 %collective-permute-start.16 = (bf16[256,512]{1,0:T(8,128)(2,1)S(1)}, bf16[256,512]{1,0:T(8,128)(2,1)S(1)}, u32[]{:S(2)}, u32[]{:S(2)}) collective-permute-start(bf16[256,512]{1,0:T(8,128)(2,1)S(1)} %collective-permute-done.15.refs_2_), channel_id=1, source_target_pairs={{0,8},{8,0},{16,24},{24,16},{32,40},{40,32},{48,56},{56,48},{64,72... | collective-permute-start | bytes 786440 | tf_op jit(solution)/shard_map/ppermute | solution.py:347
  63.2 1.5 %collective-permute-start.19 = (bf16[384,256]{1,0:T(8,128)(2,1)S(1)}, bf16[384,256]{1,0:T(8,128)(2,1)S(1)}, u32[]{:S(2)}, u32[]{:S(2)}) collective-permute-start(bf16[384,256]{1,0:T(8,128)(2,1)S(1)} %sort.1), channel_id=1, source_target_pairs={{0,8},{8,0},{16,24},{24,16},{32,40},{40,32},{48,56},{56,48},{64,72... | collective-permute-start | bytes 589832 | tf_op jit(solution)/shard_map/ppermute | solution.py:347
  69.5 5.8 %collective-permute-start.21 = (f32[128,128]{1,0:T(8,128)S(1)}, f32[128,128]{1,0:T(8,128)S(1)}, u32[]{:S(2)}, u32[]{:S(2)}) collective-permute-start(f32[128,128]{1,0:T(8,128)S(1)} %get-tuple-element.42.refs_7_), channel_id=1, source_target_pairs={{0,16},{8,24},{16,0},{24,8},{32,48},{40,56},{48,32},{56,40},{64,80... | collective-permute-start | bytes 196616 | tf_op jit(solution)/shard_map/ppermute | solution.py:347
  70.1 5.2 %collective-permute-start.20 = (f32[128,128]{1,0:T(8,128)S(1)}, f32[128,128]{1,0:T(8,128)S(1)}, u32[]{:S(2)}, u32[]{:S(2)}) collective-permute-start(f32[128,128]{1,0:T(8,128)S(1)} %get-tuple-element.42.refs_7_), channel_id=1, source_target_pairs={{0,8},{8,0},{16,24},{24,16},{32,40},{40,32},{48,56},{56,48},{64,72... | collective-permute-start | bytes 196616 | tf_op jit(solution)/shard_map/ppermute | solution.py:347
  75.3 1.3 collective-permute-start.22
  80.7 10.9 %collective-permute-start.29 = (bf16[256,512]{1,0:T(8,128)(2,1)S(1)}, bf16[256,512]{1,0:T(8,128)(2,1)S(1)}, u32[]{:S(2)}, u32[]{:S(2)}) collective-permute-start(bf16[256,512]{1,0:T(8,128)(2,1)S(1)} %get-tuple-element.53), channel_id=1, source_target_pairs={{0,8},{8,0},{16,24},{24,16},{32,40},{40,32},{48,56},{56,48},{64,72... | collective-permute-start | bytes 786440 | tf_op jit(solution)/shard_map/ppermute | solution.py:347
  81.1 5.3 %collective-permute-start.24 = (bf16[3,256,128]{2,1,0:T(8,128)(2,1)S(1)}, bf16[3,256,128]{2,1,0:T(8,128)(2,1)S(1)}, u32[]{:S(2)}, u32[]{:S(2)}) collective-permute-start(bf16[3,256,128]{2,1,0:T(8,128)(2,1)S(1)} %get-tuple-element.45), channel_id=1, source_target_pairs={{0,8},{8,0},{16,24},{24,16},{32,40},{40,32},{48,56},{56,48},{64,72... | collective-permute-start | bytes 589832 | tf_op jit(solution)/shard_map/ppermute | solution.py:347
  81.5 10.1 %collective-permute-start.23 = (bf16[256,128]{1,0:T(8,128)(2,1)S(1)}, bf16[256,128]{1,0:T(8,128)(2,1)S(1)}, u32[]{:S(2)}, u32[]{:S(2)}) collective-permute-start(bf16[256,128]{1,0:T(8,128)(2,1)S(1)} %get-tuple-element.43), channel_id=1, source_target_pairs={{0,128},{8,136},{16,144},{24,152},{32,160},{40,168},{48,176},{56,1... | collective-permute-start | bytes 196616 | tf_op jit(solution)/shard_map/ppermute | solution.py:355
  86.4 16.6 %copy-start.4 = (bf16[4096,128]{1,0:T(8,128)(2,1)S(1)}, bf16[4096,128]{1,0:T(8,128)(2,1)}, u32[]{:S(2)}) copy-start(bf16[4096,128]{1,0:T(8,128)(2,1)} %refs_12_.3) | copy-start | bytes 3145732
  86.4 16.6 %copy-start.6 = (bf16[4096,128]{1,0:T(8,128)(2,1)S(1)}, bf16[4096,128]{1,0:T(8,128)(2,1)}, u32[]{:S(2)}) copy-start(bf16[4096,128]{1,0:T(8,128)(2,1)} %refs_13_.1) | copy-start | bytes 3145732
  86.4 16.6 %copy-start.10 = (f32[4096]{0:T(1024)S(1)}, f32[4096]{0:T(1024)}, u32[]{:S(2)}) copy-start(f32[4096]{0:T(1024)} %param.11) | copy-start | bytes 49156
  87.0 5.2 %collective-permute-start.25 = (bf16[2,256,128]{2,1,0:T(8,128)(2,1)S(1)}, bf16[2,256,128]{2,1,0:T(8,128)(2,1)S(1)}, u32[]{:S(2)}, u32[]{:S(2)}) collective-permute-start(bf16[2,256,128]{2,1,0:T(8,128)(2,1)S(1)} %get-tuple-element.46), channel_id=1, source_target_pairs={{0,224},{8,40},{16,240},{24,56},{32,0},{40,72},{48,16},{56,88},{64... | collective-permute-start | bytes 393224 | tf_op jit(solution)/shard_map/ppermute | solution.py:359
  88.8 6.1 %collective-permute-start.26 = (bf16[2,256,128]{2,1,0:T(8,128)(2,1)S(1)}, bf16[2,256,128]{2,1,0:T(8,128)(2,1)S(1)}, u32[]{:S(2)}, u32[]{:S(2)}) collective-permute-start(bf16[2,256,128]{2,1,0:T(8,128)(2,1)S(1)} %get-tuple-element.47), channel_id=1, source_target_pairs={{0,192},{8,72},{16,208},{24,88},{32,224},{40,104},{48,240},{56,120... | collective-permute-start | bytes 393224 | tf_op jit(solution)/shard_map/ppermute | solution.py:359
  89.0 11.3 %collective-permute-start.27 = (bf16[2,256,128]{2,1,0:T(8,128)(2,1)S(1)}, bf16[2,256,128]{2,1,0:T(8,128)(2,1)S(1)}, u32[]{:S(2)}, u32[]{:S(2)}) collective-permute-start(bf16[2,256,128]{2,1,0:T(8,128)(2,1)S(1)} %get-tuple-element.48), channel_id=1, source_target_pairs={{0,160},{8,104},{16,176},{24,120},{32,192},{40,136},{48,208},{56,1... | collective-permute-start | bytes 393224 | tf_op jit(solution)/shard_map/ppermute | solution.py:359
  91.6 9.9 %collective-permute-start.30 = (bf16[128,512]{1,0:T(8,128)(2,1)S(1)}, bf16[128,512]{1,0:T(8,128)(2,1)S(1)}, u32[]{:S(2)}, u32[]{:S(2)}) collective-permute-start(bf16[128,512]{1,0:T(8,128)(2,1)S(1)} %get-tuple-element.55), channel_id=1, source_target_pairs={{0,16},{8,24},{16,0},{24,8},{32,48},{40,56},{48,32},{56,40},{64,80... | collective-permute-start | bytes 393224 | tf_op jit(solution)/shard_map/ppermute | solution.py:347
  100.9 2.1 %collective-permute-start.28 = (bf16[256,128]{1,0:T(8,128)(2,1)S(1)}, bf16[256,128]{1,0:T(8,128)(2,1)S(1)}, u32[]{:S(2)}, u32[]{:S(2)}) collective-permute-start(bf16[256,128]{1,0:T(8,128)(2,1)S(1)} %get-tuple-element.51), channel_id=1, source_target_pairs={{0,8},{8,0},{16,24},{24,16},{32,40},{40,32},{48,56},{56,48},{64,72... | collective-permute-start | bytes 196616 | tf_op jit(solution)/shard_map/ppermute | solution.py:347
  104.5 7.1 %collective-permute-start.31 = (bf16[144,512]{1,0:T(8,128)(2,1)S(1)}, bf16[144,512]{1,0:T(8,128)(2,1)S(1)}, u32[]{:S(2)}, u32[]{:S(2)}) collective-permute-start(bf16[144,512]{1,0:T(8,128)(2,1)S(1)} %get-tuple-element.58), channel_id=1, source_target_pairs={{0,1},{1,0},{2,3},{3,2},{4,5},{5,4},{6,7},{7,6},{8,9},{9,8},{10,11... | collective-permute-start | bytes 442376 | tf_op jit(solution)/shard_map/ppermute | solution.py:343
  105.2 11.7 %collective-permute-start.32 = (bf16[144,512]{1,0:T(8,128)(2,1)S(1)}, bf16[144,512]{1,0:T(8,128)(2,1)S(1)}, u32[]{:S(2)}, u32[]{:S(2)}) collective-permute-start(bf16[144,512]{1,0:T(8,128)(2,1)S(1)} %get-tuple-element.59), channel_id=1, source_target_pairs={{0,2},{1,3},{2,0},{3,1},{4,6},{5,7},{6,4},{7,5},{8,10},{9,11},{10,... | collective-permute-start | bytes 442376 | tf_op jit(solution)/shard_map/ppermute | solution.py:343
  106.3 13.5 %collective-permute-start.33 = (bf16[144,512]{1,0:T(8,128)(2,1)S(1)}, bf16[144,512]{1,0:T(8,128)(2,1)S(1)}, u32[]{:S(2)}, u32[]{:S(2)}) collective-permute-start(bf16[144,512]{1,0:T(8,128)(2,1)S(1)} %get-tuple-element.60), channel_id=1, source_target_pairs={{0,4},{1,5},{2,6},{3,7},{4,0},{5,1},{6,2},{7,3},{8,12},{9,13},{10,... | collective-permute-start | bytes 442376 | tf_op jit(solution)/shard_map/ppermute | solution.py:343
  106.7 13.1 %collective-permute-start.34 = (bf16[144,512]{1,0:T(8,128)(2,1)S(1)}, bf16[144,512]{1,0:T(8,128)(2,1)S(1)}, u32[]{:S(2)}, u32[]{:S(2)}) collective-permute-start(bf16[144,512]{1,0:T(8,128)(2,1)S(1)} %get-tuple-element.61), channel_id=1, source_target_pairs={{0,5},{1,4},{2,7},{3,6},{4,1},{5,0},{6,3},{7,2},{8,13},{9,12},{10,... | collective-permute-start | bytes 442376 | tf_op jit(solution)/shard_map/ppermute | solution.py:343
  110.3 9.5 %collective-permute-start.35 = (bf16[144,512]{1,0:T(8,128)(2,1)S(1)}, bf16[144,512]{1,0:T(8,128)(2,1)S(1)}, u32[]{:S(2)}, u32[]{:S(2)}) collective-permute-start(bf16[144,512]{1,0:T(8,128)(2,1)S(1)} %get-tuple-element.62), channel_id=1, source_target_pairs={{0,3},{1,2},{2,1},{3,0},{4,7},{5,6},{6,5},{7,4},{8,11},{9,10},{10,... | collective-permute-start | bytes 442376 | tf_op jit(solution)/shard_map/ppermute | solution.py:343
  111.6 10.4 %collective-permute-start.36 = (bf16[144,512]{1,0:T(8,128)(2,1)S(1)}, bf16[144,512]{1,0:T(8,128)(2,1)S(1)}, u32[]{:S(2)}, u32[]{:S(2)}) collective-permute-start(bf16[144,512]{1,0:T(8,128)(2,1)S(1)} %get-tuple-element.63), channel_id=1, source_target_pairs={{0,6},{1,7},{2,4},{3,5},{4,2},{5,3},{6,0},{7,1},{8,14},{9,15},{10,... | collective-permute-start | bytes 442376 | tf_op jit(solution)/shard_map/ppermute | solution.py:343
  116.9 7.3 %collective-permute-start.37 = (bf16[144,512]{1,0:T(8,128)(2,1)S(1)}, bf16[144,512]{1,0:T(8,128)(2,1)S(1)}, u32[]{:S(2)}, u32[]{:S(2)}) collective-permute-start(bf16[144,512]{1,0:T(8,128)(2,1)S(1)} %get-tuple-element.64), channel_id=1, source_target_pairs={{0,7},{1,6},{2,5},{3,4},{4,3},{5,2},{6,1},{7,0},{8,15},{9,14},{10,... | collective-permute-start | bytes 442376 | tf_op jit(solution)/shard_map/ppermute | solution.py:343

commit v2 on v1

--- a/solution.py
+++ b/solution.py
@@ -368,7 +368,7 @@
     ids = jnp.stack([lax.axis_index("ctx"), lax.axis_index("head")]).astype(jnp.int32)
     gain = norm_gain.reshape(1, D)
     xs = [xor_head(inputs, k) if k else inputs for k in KS]
-    ready = touch([w_key, w_value, gain, inputs, out_grad])
+    ready = touch([w_key, w_value, gain, inputs])
     kv, normed, mean, mean_row = call(
         norm_kernel,
         [ids],
@@ -403,7 +403,7 @@
     projected, dot_row = call(
         project_kernel,
         [ids],
-        [*xs, *dys, w_out, normed, w_query, ready_out, near[1], near[2]],
+        [*xs, *dys, w_out, normed, w_query, ready_out, kvs[1], near[2]],
         [shape((2 * ROWS, SHARE), bf16), shape((8, ROWS), f32)],
         24,
         flops=4 * ROWS * D * SHARE,

time: 127 us -> 123 us (0.969)
  Pallas kernels: 22.4 us -> 20.2 us
  waiting for transfers between devices: 41.1 us -> 39.3 us
    ppermute x18, waiting for transfers between devices: 14.2 us -> 10.1 us  [xor_head(): return lax.ppermute(a, 'head', [(i, i ^ k) for i in range(GROUPS)])]
    ppermute x2, starting transfers between devices: 9.22 us -> 5.18 us  [turn(): return lax.ppermute(a, 'ctx', [(i, (i + 4 * k) % 32) for i in range(32)])]
    ppermute x18, starting transfers between devices: 27.9 us -> 31.8 us  [xor_head(): return lax.ppermute(a, 'head', [(i, i ^ k) for i in range(GROUPS)])]
    ppermute x2, waiting for transfers between devices: 3.48 us -> 6.83 us  [turn(): return lax.ppermute(a, 'ctx', [(i, (i + 4 * k) % 32) for i in range(32)])]
    pallas_call x15, Pallas kernels: 22.4 us -> 20.2 us  [call(): pl.pallas_call(body, out_shape=outs, in_specs=smem(len(scalars)) + vmem(l...]
    ppermute x6, waiting for transfers between devices: 13.7 us -> 11.6 us  [apart(): lax.ppermute(a, 'ctx', [(i, (i + 4 * k * (1 - 2 * (i % 2))) % 32) for i i...]
    ppermute x6, starting transfers between devices: 11.9 us -> 13.2 us  [apart(): lax.ppermute(a, 'ctx', [(i, (i + 4 * k * (1 - 2 * (i % 2))) % 32) for i i...]
    unnamed x26 -> x28, local copies, waits for them, and re-layouts: 6.64 us -> 6.64 us
where the time goes in v2:
time: 123 us; the launch traced here: 122 us
  starting transfers between devices  55.4 us (45%)
  waiting for transfers between devices  39.3 us (32%)
  Pallas kernels  20.2 us (16%)
  local copies, waits for them, and re-layouts  6.64 us (5%)
    ppermute x18, starting transfers between devices, xor_head(): return lax.ppermute(a, 'head', [(i, i ^ k) for i in range(GROUPS)])  31.8 us
    pallas_call x15, Pallas kernels, call(): pl.pallas_call(body, out_shape=outs, in_specs=smem(len(scalars)) + vmem(l...  20.2 us
    ppermute x6, starting transfers between devices, apart(): lax.ppermute(a, 'ctx', [(i, (i + 4 * k * (1 - 2 * (i % 2))) % 32) for i i...  13.2 us
    ppermute x6, waiting for transfers between devices, apart(): lax.ppermute(a, 'ctx', [(i, (i + 4 * k * (1 - 2 * (i % 2))) % 32) for i i...  11.6 us
    ppermute x12, waiting for transfers between devices, xor_ctx(): return lax.ppermute(a, 'ctx', [(i, i ^ k) for i in range(32)])  10.7 us
    ppermute x18, waiting for transfers between devices, xor_head(): return lax.ppermute(a, 'head', [(i, i ^ k) for i in range(GROUPS)])  10.1 us
    ppermute x2, waiting for transfers between devices, turn(): return lax.ppermute(a, 'ctx', [(i, (i + 4 * k) % 32) for i in range(32)])  6.83 us
    unnamed x28, local copies, waits for them, and re-layouts  6.64 us
  transfers between devices with their start and end apart: 38, of which 15 were waited for; matrix products, arithmetic and copies ran while one was open for 0% of the time, Pallas kernels for 5%

profile of v2, /device:TPU:32, one launch (start us, length us, event | category | flops | bytes accessed | tf_op | source)
XLA Modules:
  0.0 122.5 jit_solution(14428302068619119360)
XLA Ops:
  0.6 1.6 %collective-permute-start.6 = (bf16[128,512]{1,0:T(8,128)(2,1)}, bf16[128,512]{1,0:T(8,128)(2,1)S(1)}, u32[]{:S(2)}, u32[]{:S(2)}) collective-permute-start(bf16[128,512]{1,0:T(8,128)(2,1)} %refs_7_.1), channel_id=1, source_target_pairs={{0,1},{1,0},{2,3},{3,2},{4,5},{5,4},{6,7},{7,6},{8,9},{9,8},{10,11... | collective-permute-start | bytes 393224 | tf_op jit(solution)/shard_map/ppermute | solution.py:343
  2.2 1.6 %collective-permute-start.5 = (bf16[128,512]{1,0:T(8,128)(2,1)}, bf16[128,512]{1,0:T(8,128)(2,1)S(1)}, u32[]{:S(2)}, u32[]{:S(2)}) collective-permute-start(bf16[128,512]{1,0:T(8,128)(2,1)} %refs_7_.1), channel_id=1, source_target_pairs={{0,2},{1,3},{2,0},{3,1},{4,6},{5,7},{6,4},{7,5},{8,10},{9,11},{10,... | collective-permute-start | bytes 393224 | tf_op jit(solution)/shard_map/ppermute | solution.py:343
  3.8 2.9 %collective-permute-start.4 = (bf16[128,512]{1,0:T(8,128)(2,1)}, bf16[128,512]{1,0:T(8,128)(2,1)S(1)}, u32[]{:S(2)}, u32[]{:S(2)}) collective-permute-start(bf16[128,512]{1,0:T(8,128)(2,1)} %refs_7_.1), channel_id=1, source_target_pairs={{0,4},{1,5},{2,6},{3,7},{4,0},{5,1},{6,2},{7,3},{8,12},{9,13},{10,... | collective-permute-start | bytes 393224 | tf_op jit(solution)/shard_map/ppermute | solution.py:343
  6.7 0.6 collective-permute-start.3
  7.3 1.4 %collective-permute-start.2 = (bf16[128,512]{1,0:T(8,128)(2,1)}, bf16[128,512]{1,0:T(8,128)(2,1)S(1)}, u32[]{:S(2)}, u32[]{:S(2)}) collective-permute-start(bf16[128,512]{1,0:T(8,128)(2,1)} %refs_7_.1), channel_id=1, source_target_pairs={{0,3},{1,2},{2,1},{3,0},{4,7},{5,6},{6,5},{7,4},{8,11},{9,10},{10,... | collective-permute-start | bytes 393224 | tf_op jit(solution)/shard_map/ppermute | solution.py:343
  8.7 3.0 %collective-permute-start.1 = (bf16[128,512]{1,0:T(8,128)(2,1)}, bf16[128,512]{1,0:T(8,128)(2,1)S(1)}, u32[]{:S(2)}, u32[]{:S(2)}) collective-permute-start(bf16[128,512]{1,0:T(8,128)(2,1)} %refs_7_.1), channel_id=1, source_target_pairs={{0,6},{1,7},{2,4},{3,5},{4,2},{5,3},{6,0},{7,1},{8,14},{9,15},{10,... | collective-permute-start | bytes 393224 | tf_op jit(solution)/shard_map/ppermute | solution.py:343
  11.7 4.0 %collective-permute-start = (bf16[128,512]{1,0:T(8,128)(2,1)}, bf16[128,512]{1,0:T(8,128)(2,1)S(1)}, u32[]{:S(2)}, u32[]{:S(2)}) collective-permute-start(bf16[128,512]{1,0:T(8,128)(2,1)} %refs_7_.1), channel_id=1, source_target_pairs={{0,7},{1,6},{2,5},{3,4},{4,3},{5,2},{6,1},{7,0},{8,15},{9,14},{10,... | collective-permute-start | bytes 393224 | tf_op jit(solution)/shard_map/ppermute | solution.py:343
  15.7 1.4 %copy-done.3 = bf16[4096,128]{1,0:T(8,128)(2,1)S(1)} copy-done((bf16[4096,128]{1,0:T(8,128)(2,1)S(1)}, bf16[4096,128]{1,0:T(8,128)(2,1)}, u32[]{:S(2)}) %copy-start.3) | copy-done | bytes 1048600
  17.1 1.4 %copy-done.5 = bf16[4096,128]{1,0:T(8,128)(2,1)S(1)} copy-done((bf16[4096,128]{1,0:T(8,128)(2,1)S(1)}, bf16[4096,128]{1,0:T(8,128)(2,1)}, u32[]{:S(2)}) %copy-start.5) | copy-done | bytes 1048600
  18.5 0.9 copy-done.7
  19.4 0.7 copy-done.10
  20.1 1.5 %collective-permute-start.7 = (bf16[128,512]{1,0:T(8,128)(2,1)}, bf16[128,512]{1,0:T(8,128)(2,1)S(1)}, u32[]{:S(2)}, u32[]{:S(2)}) collective-permute-start(bf16[128,512]{1,0:T(8,128)(2,1)} %refs_8_.1), channel_id=1, source_target_pairs={{0,1},{1,0},{2,3},{3,2},{4,5},{5,4},{6,7},{7,6},{8,9},{9,8},{10,11... | collective-permute-start | bytes 393224 | tf_op jit(solution)/shard_map/ppermute | solution.py:343
  21.7 1.8 %norm_kv.1 = (bf16[128,256]{1,0:T(8,128)(2,1)S(1)}, bf16[128,4096]{1,0:T(8,128)(2,1)S(1)}, f32[128,128]{1,0:T(8,128)S(1)}, f32[8,128]{1,0:T(8,128)S(1)}) custom-call(s32[2]{0:T(128)S(1)} %pad_add_fusion.ids, bf16[128,512]{1,0:T(8,128)(2,1)S(1)} %copy-done.7, bf16[128,512]{1,0:T(8,128)(2,1)S(1)} %collective-permute-done.refs_1_.refs_3_, ...), custom_call_target="tpu_custom_call" | custom-call | flops 268435456 | bytes 5242880 | tf_op jit(solution)/shard_map/norm_kv/pallas_call | solution.py:55
  23.5 1.7 %collective-permute-done.7.other = bf16[128,512]{1,0:T(8,128)(2,1)S(1)} collective-permute-done((bf16[128,512]{1,0:T(8,128)(2,1)}, bf16[128,512]{1,0:T(8,128)(2,1)S(1)}, u32[]{:S(2)}, u32[]{:S(2)}) %collective-permute-start.7) | collective-permute-done | bytes 131104 | tf_op jit(solution)/shard_map/ppermute | solution.py:343
  25.3 0.1 collective-permute-start.10
  25.4 2.7 %collective-permute-start.9 = (bf16[256,512]{1,0:T(8,128)(2,1)S(1)}, bf16[256,512]{1,0:T(8,128)(2,1)S(1)}, u32[]{:S(2)}, u32[]{:S(2)}) collective-permute-start(bf16[256,512]{1,0:T(8,128)(2,1)S(1)} %hold.1.refs_8_), channel_id=1, source_target_pairs={{0,4},{1,5},{2,6},{3,7},{4,0},{5,1},{6,2},{7,3},{8,12},{9,13},{10,... | collective-permute-start | bytes 786440 | tf_op jit(solution)/shard_map/ppermute | solution.py:343
  28.1 1.4 %collective-permute-start.8 = (bf16[256,512]{1,0:T(8,128)(2,1)S(1)}, bf16[256,512]{1,0:T(8,128)(2,1)S(1)}, u32[]{:S(2)}, u32[]{:S(2)}) collective-permute-start(bf16[256,512]{1,0:T(8,128)(2,1)S(1)} %hold.1.refs_8_), channel_id=1, source_target_pairs={{0,2},{1,3},{2,0},{3,1},{4,6},{5,7},{6,4},{7,5},{8,10},{9,11},{10,... | collective-permute-start | bytes 786440 | tf_op jit(solution)/shard_map/ppermute | solution.py:343
  29.5 1.3 %collective-permute-done.12.other = bf16[128,256]{1,0:T(8,128)(2,1)S(1)} collective-permute-done((bf16[128,256]{1,0:T(8,128)(2,1)S(1)}, bf16[128,256]{1,0:T(8,128)(2,1)S(1)}, u32[]{:S(2)}, u32[]{:S(2)}) %collective-permute-start.12) | collective-permute-done | bytes 65568 | tf_op jit(solution)/shard_map/ppermute | solution.py:347
  30.8 0.6 join.1
  31.3 5.9 %collective-permute-start.13 = (bf16[256,256]{1,0:T(8,128)(2,1)S(1)}, bf16[256,256]{1,0:T(8,128)(2,1)S(1)}, u32[]{:S(2)}, u32[]{:S(2)}) collective-permute-start(bf16[256,256]{1,0:T(8,128)(2,1)S(1)} %join.1), channel_id=1, source_target_pairs={{0,96},{8,168},{16,112},{24,184},{32,128},{40,200},{48,144},{56,21... | collective-permute-start | bytes 393224 | tf_op jit(solution)/shard_map/ppermute | solution.py:359
  37.2 0.6 collective-permute-start.11
  37.8 2.2 %copy-done.1 = bf16[512,4096]{1,0:T(8,128)(2,1)S(1)} copy-done((bf16[512,4096]{1,0:T(8,128)(2,1)S(1)}, bf16[512,4096]{1,0:T(8,128)(2,1)}, u32[]{:S(2)}) %copy-start.1) | copy-done | bytes 4194328
  40.0 5.4 %collective-permute-done.11.refs_16_.refs_3_.refs_5_ = bf16[128,256]{1,0:T(8,128)(2,1)S(1)} collective-permute-done((bf16[128,256]{1,0:T(8,128)(2,1)S(1)}, bf16[128,256]{1,0:T(8,128)(2,1)S(1)}, u32[]{:S(2)}, u32[]{:S(2)}) %collective-permute-start.11) | collective-permute-done | bytes 65568 | tf_op jit(solution)/shard_map/ppermute | solution.py:355
  45.5 2.8 %project.1 = (bf16[256,512]{1,0:T(8,128)(2,1)S(1)}, f32[8,128]{1,0:T(8,128)S(1)}) custom-call(s32[2]{0:T(128)S(1)} %pad_add_fusion.ids, bf16[128,512]{1,0:T(8,128)(2,1)S(1)} %copy-done.8, bf16[128,512]{1,0:T(8,128)(2,1)S(1)} %collective-permute-done.refs_1_.refs_3_, bf16[128,512]{1,0:T(8,128)(2,1)S(1)} %collective-permute-done.1.refs_2_.refs_4_, ...), custom_call_target="tpu_custom_call" | custom-call | flops 1073741824 | bytes 10485760 | tf_op jit(solution)/shard_map/project/pallas_call | solution.py:55
  48.2 3.1 %collective-permute-start.15 = (bf16[256,512]{1,0:T(8,128)(2,1)S(1)}, bf16[256,512]{1,0:T(8,128)(2,1)S(1)}, u32[]{:S(2)}, u32[]{:S(2)}) collective-permute-start(bf16[256,512]{1,0:T(8,128)(2,1)S(1)} %get-tuple-element.38.refs_0_), channel_id=1, source_target_pairs={{0,16},{8,24},{16,0},{24,8},{32,48},{40,56},{48,32},{56,40},{64,80... | collective-permute-start | bytes 786440 | tf_op jit(solution)/shard_map/ppermute | solution.py:347
  51.4 1.5 %collective-permute-start.18 = (bf16[256,256]{1,0:T(8,128)(2,1)S(1)}, bf16[256,256]{1,0:T(8,128)(2,1)S(1)}, u32[]{:S(2)}, u32[]{:S(2)}) collective-permute-start(bf16[256,256]{1,0:T(8,128)(2,1)S(1)} %join.1), channel_id=1, source_target_pairs={{0,64},{8,200},{16,80},{24,216},{32,96},{40,232},{48,112},{56,248}... | collective-permute-start | bytes 393224 | tf_op jit(solution)/shard_map/ppermute | solution.py:359
  52.9 2.8 %collective-permute-start.17 = (bf16[256,256]{1,0:T(8,128)(2,1)S(1)}, bf16[256,256]{1,0:T(8,128)(2,1)S(1)}, u32[]{:S(2)}, u32[]{:S(2)}) collective-permute-start(bf16[256,256]{1,0:T(8,128)(2,1)S(1)} %join.1), channel_id=1, source_target_pairs={{0,32},{8,232},{16,48},{24,248},{32,64},{40,8},{48,80},{56,24},{64... | collective-permute-start | bytes 393224 | tf_op jit(solution)/shard_map/ppermute | solution.py:359
  55.6 1.5 %collective-permute-done.15.refs_2_ = bf16[256,512]{1,0:T(8,128)(2,1)S(1)} collective-permute-done((bf16[256,512]{1,0:T(8,128)(2,1)S(1)}, bf16[256,512]{1,0:T(8,128)(2,1)S(1)}, u32[]{:S(2)}, u32[]{:S(2)}) %collective-permute-start.15) | collective-permute-done | bytes 262176 | tf_op jit(solution)/shard_map/ppermute | solution.py:347
  57.2 1.4 %collective-permute-done.18.refs_1_.refs_7_ = bf16[256,256]{1,0:T(8,128)(2,1)S(1)} collective-permute-done((bf16[256,256]{1,0:T(8,128)(2,1)S(1)}, bf16[256,256]{1,0:T(8,128)(2,1)S(1)}, u32[]{:S(2)}, u32[]{:S(2)}) %collective-permute-start.18) | collective-permute-done | bytes 131104 | tf_op jit(solution)/shard_map/ppermute | solution.py:359
  58.5 2.1 %collective-permute-done.17.refs_0_.refs_6_ = bf16[256,256]{1,0:T(8,128)(2,1)S(1)} collective-permute-done((bf16[256,256]{1,0:T(8,128)(2,1)S(1)}, bf16[256,256]{1,0:T(8,128)(2,1)S(1)}, u32[]{:S(2)}, u32[]{:S(2)}) %collective-permute-start.17) | collective-permute-done | bytes 131104 | tf_op jit(solution)/shard_map/ppermute | solution.py:359
  60.7 0.6 sort.1
  61.2 0.1 collective-permute-start.19
  61.3 1.4 %collective-permute-done.19.refs_9_ = bf16[384,256]{1,0:T(8,128)(2,1)S(1)} collective-permute-done((bf16[384,256]{1,0:T(8,128)(2,1)S(1)}, bf16[384,256]{1,0:T(8,128)(2,1)S(1)}, u32[]{:S(2)}, u32[]{:S(2)}) %collective-permute-start.19) | collective-permute-done | bytes 196640 | tf_op jit(solution)/shard_map/ppermute | solution.py:347
  62.8 4.7 %softmax.1 = (bf16[2048,1024]{1,0:T(8,128)(2,1)S(1)}, f32[128,128]{1,0:T(8,128)S(1)}, bf16[1024,128]{1,0:T(8,128)(2,1)S(1)}, bf16[1024,128]{1,0:T(8,128)(2,1)S(1)}) custom-call(s32[2]{0:T(128)S(1)} %pad_add_fusion.ids, s32[64]{0:T(128)S(1)} %copy-done.12, s32[8]{0:T(128)S(1)} %copy-done.13, bf16[256,512]{1,0:T(8,128)(2,1)S(1)} %get-tuple-element.38.refs_0_, ...), custom_call_target="tpu_custom_call" | custom-call | flops 1073741824 | bytes 6291456 | tf_op jit(solution)/shard_map/softmax/pallas_call | solution.py:55
  67.5 0.6 collective-permute-start.21
  68.1 5.3 %collective-permute-done.21.refs_9_ = f32[128,128]{1,0:T(8,128)S(1)} collective-permute-done((f32[128,128]{1,0:T(8,128)S(1)}, f32[128,128]{1,0:T(8,128)S(1)}, u32[]{:S(2)}, u32[]{:S(2)}) %collective-permute-start.21) | collective-permute-done | bytes 65568 | tf_op jit(solution)/shard_map/ppermute | solution.py:347
  73.4 1.2 %collective-permute-done.22.refs_10_ = f32[128,128]{1,0:T(8,128)S(1)} collective-permute-done((f32[128,128]{1,0:T(8,128)S(1)}, f32[128,128]{1,0:T(8,128)S(1)}, u32[]{:S(2)}, u32[]{:S(2)}) %collective-permute-start.22) | collective-permute-done | bytes 65568 | tf_op jit(solution)/shard_map/ppermute | solution.py:347
  74.6 4.1 %gradient.1 = (bf16[256,128]{1,0:T(8,128)(2,1)S(1)}, bf16[256,128]{1,0:T(8,128)(2,1)S(1)}, bf16[3,256,128]{2,1,0:T(8,128)(2,1)S(1)}, bf16[3,256,128]{2,1,0:T(8,1...) custom-call(bf16[256,512]{1,0:T(8,128)(2,1)S(1)} %get-tuple-element.38.refs_0_, ...), custom_call_target="tpu_custom_call" | custom-call | flops 2147483648 | bytes 6291456 | tf_op jit(solution)/shard_map/gradient/pallas_call | solution.py:55
  78.7 0.5 collective-permute-start.29
  79.2 0.4 collective-permute-start.24
  79.5 4.6 %collective-permute-start.23 = (bf16[256,128]{1,0:T(8,128)(2,1)S(1)}, bf16[256,128]{1,0:T(8,128)(2,1)S(1)}, u32[]{:S(2)}, u32[]{:S(2)}) collective-permute-start(bf16[256,128]{1,0:T(8,128)(2,1)S(1)} %get-tuple-element.43), channel_id=1, source_target_pairs={{0,128},{8,136},{16,144},{24,152},{32,160},{40,168},{48,176},{56,1... | collective-permute-start | bytes 196616 | tf_op jit(solution)/shard_map/ppermute | solution.py:355
  84.2 0.6 pair.1
  84.8 0.6 collective-permute-start.25
  85.4 0.5 collective-permute-start.26
  85.9 1.9 %collective-permute-start.27 = (bf16[2,256,128]{2,1,0:T(8,128)(2,1)S(1)}, bf16[2,256,128]{2,1,0:T(8,128)(2,1)S(1)}, u32[]{:S(2)}, u32[]{:S(2)}) collective-permute-start(bf16[2,256,128]{2,1,0:T(8,128)(2,1)S(1)} %get-tuple-element.48), channel_id=1, source_target_pairs={{0,160},{8,104},{16,176},{24,120},{32,192},{40,136},{48,208},{56,1... | collective-permute-start | bytes 393224 | tf_op jit(solution)/shard_map/ppermute | solution.py:359
  87.8 1.4 %collective-permute-done.23.refs_0_._ = bf16[256,128]{1,0:T(8,128)(2,1)S(1)} collective-permute-done((bf16[256,128]{1,0:T(8,128)(2,1)S(1)}, bf16[256,128]{1,0:T(8,128)(2,1)S(1)}, u32[]{:S(2)}, u32[]{:S(2)}) %collective-permute-start.23) | collective-permute-done | bytes 65568 | tf_op jit(solution)/shard_map/ppermute | solution.py:355
  89.2 0.5 collective-permute-start.30
  89.7 3.1 %collective-permute-done.25.refs_1_ = bf16[2,256,128]{2,1,0:T(8,128)(2,1)S(1)} collective-permute-done((bf16[2,256,128]{2,1,0:T(8,128)(2,1)S(1)}, bf16[2,256,128]{2,1,0:T(8,128)(2,1)S(1)}, u32[]{:S(2)}, u32[]{:S(2)}) %collective-permute-start.25) | collective-permute-done | bytes 131104 | tf_op jit(solution)/shard_map/ppermute | solution.py:359
  92.9 5.0 %collective-permute-done.27.refs_3_ = bf16[2,256,128]{2,1,0:T(8,128)(2,1)S(1)} collective-permute-done((bf16[2,256,128]{2,1,0:T(8,128)(2,1)S(1)}, bf16[2,256,128]{2,1,0:T(8,128)(2,1)S(1)}, u32[]{:S(2)}, u32[]{:S(2)}) %collective-permute-start.27) | collective-permute-done | bytes 131104 | tf_op jit(solution)/shard_map/ppermute | solution.py:359
  97.9 0.6 sum.1
  98.5 0.1 collective-permute-start.28
  98.6 1.5 %back_query.1.refs_11_ = f32[128,4096]{1,0:T(8,128)S(1)} custom-call(f32[128,512]{1,0:T(8,128)S(1)} %get-tuple-element.54.stay, bf16[128,512]{1,0:T(8,128)(2,1)S(1)} %collective-permute-done.30.got, bf16[4096,512]{1,0:T(8,128)(2,1)S(1)} %copy-done), custom_call_target="tpu_custom_call" | custom-call | flops 536870912 | bytes 6291456 | tf_op jit(solution)/shard_map/back_query/pallas_call | solution.py:55
  100.1 1.5 %back_kv.1 = (f32[128,512]{1,0:T(8,128)S(1)}, bf16[16,256]{1,0:T(8,128)(2,1)S(1)}, bf16[144,512]{1,0:T(8,128)(2,1)S(1)}, bf16[144,512]{1,0:T(8,128)(2,1)S(1)}, b...) custom-call(s32[2]{0:T(128)S(1)} %pad_add_fusion.ids, ...), custom_call_target="tpu_custom_call" | custom-call | flops 268435456 | bytes 7340032 | tf_op jit(solution)/shard_map/back_kv/pallas_call | solution.py:55
  101.6 0.7 collective-permute-start.31
  102.2 1.1 collective-permute-start.32
  103.4 0.4 collective-permute-start.33
  103.8 3.6 %collective-permute-start.34 = (bf16[144,512]{1,0:T(8,128)(2,1)S(1)}, bf16[144,512]{1,0:T(8,128)(2,1)S(1)}, u32[]{:S(2)}, u32[]{:S(2)}) collective-permute-start(bf16[144,512]{1,0:T(8,128)(2,1)S(1)} %get-tuple-element.61), channel_id=1, source_target_pairs={{0,5},{1,4},{2,7},{3,6},{4,1},{5,0},{6,3},{7,2},{8,13},{9,12},{10,... | collective-permute-start | bytes 442376 | tf_op jit(solution)/shard_map/ppermute | solution.py:343
  107.4 1.3 %collective-permute-start.35 = (bf16[144,512]{1,0:T(8,128)(2,1)S(1)}, bf16[144,512]{1,0:T(8,128)(2,1)S(1)}, u32[]{:S(2)}, u32[]{:S(2)}) collective-permute-start(bf16[144,512]{1,0:T(8,128)(2,1)S(1)} %get-tuple-element.62), channel_id=1, source_target_pairs={{0,3},{1,2},{2,1},{3,0},{4,7},{5,6},{6,5},{7,4},{8,11},{9,10},{10,... | collective-permute-start | bytes 442376 | tf_op jit(solution)/shard_map/ppermute | solution.py:343
  108.7 0.1 collective-permute-start.36
  108.8 0.1 collective-permute-done.32.refs_1_
  108.9 3.9 %collective-permute-start.37 = (bf16[144,512]{1,0:T(8,128)(2,1)S(1)}, bf16[144,512]{1,0:T(8,128)(2,1)S(1)}, u32[]{:S(2)}, u32[]{:S(2)}) collective-permute-start(bf16[144,512]{1,0:T(8,128)(2,1)S(1)} %get-tuple-element.64), channel_id=1, source_target_pairs={{0,7},{1,6},{2,5},{3,4},{4,3},{5,2},{6,1},{7,0},{8,15},{9,14},{10,... | collective-permute-start | bytes 442376 | tf_op jit(solution)/shard_map/ppermute | solution.py:343
  112.8 5.6 %collective-permute-done.33.refs_2_ = bf16[144,512]{1,0:T(8,128)(2,1)S(1)} collective-permute-done((bf16[144,512]{1,0:T(8,128)(2,1)S(1)}, bf16[144,512]{1,0:T(8,128)(2,1)S(1)}, u32[]{:S(2)}, u32[]{:S(2)}) %collective-permute-start.33) | collective-permute-done | bytes 147488 | tf_op jit(solution)/shard_map/ppermute | solution.py:343
  118.4 2.6 %collective-permute-done.36.refs_5_ = bf16[144,512]{1,0:T(8,128)(2,1)S(1)} collective-permute-done((bf16[144,512]{1,0:T(8,128)(2,1)S(1)}, bf16[144,512]{1,0:T(8,128)(2,1)S(1)}, u32[]{:S(2)}, u32[]{:S(2)}) %collective-permute-start.36) | collective-permute-done | bytes 147488 | tf_op jit(solution)/shard_map/ppermute | solution.py:343
  121.0 1.5 %last.1 = (bf16[128,512]{1,0:T(8,128)(2,1)}, f32[1,128]{1,0:T(1,128)}) custom-call(s32[2]{0:T(128)S(1)} %pad_add_fusion.ids, f32[128,512]{1,0:T(8,128)S(1)} %get-tuple-element.56.own, bf16[16,256]{1,0:T(8,128)(2,1)S(1)} %get-tuple-element.57.own_row, bf16[144,512]{1,0:T(8,128)(2,1)S(1)} %collective-permute-done.31.refs_0_, ...), custom_call_target="tpu_custom_call" | custom-call | flops 655360 | bytes 3145728 | tf_op jit(solution)/shard_map/last/pallas_call | solution.py:55
  (56 shorter events, 0.3 us)
Async XLA Ops:
  0.6 8.0 %collective-permute-start.6 = (bf16[128,512]{1,0:T(8,128)(2,1)}, bf16[128,512]{1,0:T(8,128)(2,1)S(1)}, u32[]{:S(2)}, u32[]{:S(2)}) collective-permute-start(bf16[128,512]{1,0:T(8,128)(2,1)} %refs_7_.1), channel_id=1, source_target_pairs={{0,1},{1,0},{2,3},{3,2},{4,5},{5,4},{6,7},{7,6},{8,9},{9,8},{10,11... | collective-permute-start | bytes 393224 | tf_op jit(solution)/shard_map/ppermute | solution.py:343
  2.2 9.5 %collective-permute-start.5 = (bf16[128,512]{1,0:T(8,128)(2,1)}, bf16[128,512]{1,0:T(8,128)(2,1)S(1)}, u32[]{:S(2)}, u32[]{:S(2)}) collective-permute-start(bf16[128,512]{1,0:T(8,128)(2,1)} %refs_7_.1), channel_id=1, source_target_pairs={{0,2},{1,3},{2,0},{3,1},{4,6},{5,7},{6,4},{7,5},{8,10},{9,11},{10,... | collective-permute-start | bytes 393224 | tf_op jit(solution)/shard_map/ppermute | solution.py:343
  3.8 16.3 %collective-permute-start.4 = (bf16[128,512]{1,0:T(8,128)(2,1)}, bf16[128,512]{1,0:T(8,128)(2,1)S(1)}, u32[]{:S(2)}, u32[]{:S(2)}) collective-permute-start(bf16[128,512]{1,0:T(8,128)(2,1)} %refs_7_.1), channel_id=1, source_target_pairs={{0,4},{1,5},{2,6},{3,7},{4,0},{5,1},{6,2},{7,3},{8,12},{9,13},{10,... | collective-permute-start | bytes 393224 | tf_op jit(solution)/shard_map/ppermute | solution.py:343
  6.7 15.0 %collective-permute-start.3 = (bf16[128,512]{1,0:T(8,128)(2,1)}, bf16[128,512]{1,0:T(8,128)(2,1)S(1)}, u32[]{:S(2)}, u32[]{:S(2)}) collective-permute-start(bf16[128,512]{1,0:T(8,128)(2,1)} %refs_7_.1), channel_id=1, source_target_pairs={{0,5},{1,4},{2,7},{3,6},{4,1},{5,0},{6,3},{7,2},{8,13},{9,12},{10,... | collective-permute-start | bytes 393224 | tf_op jit(solution)/shard_map/ppermute | solution.py:343
  7.3 14.4 %collective-permute-start.2 = (bf16[128,512]{1,0:T(8,128)(2,1)}, bf16[128,512]{1,0:T(8,128)(2,1)S(1)}, u32[]{:S(2)}, u32[]{:S(2)}) collective-permute-start(bf16[128,512]{1,0:T(8,128)(2,1)} %refs_7_.1), channel_id=1, source_target_pairs={{0,3},{1,2},{2,1},{3,0},{4,7},{5,6},{6,5},{7,4},{8,11},{9,10},{10,... | collective-permute-start | bytes 393224 | tf_op jit(solution)/shard_map/ppermute | solution.py:343
  8.7 13.0 %collective-permute-start.1 = (bf16[128,512]{1,0:T(8,128)(2,1)}, bf16[128,512]{1,0:T(8,128)(2,1)S(1)}, u32[]{:S(2)}, u32[]{:S(2)}) collective-permute-start(bf16[128,512]{1,0:T(8,128)(2,1)} %refs_7_.1), channel_id=1, source_target_pairs={{0,6},{1,7},{2,4},{3,5},{4,2},{5,3},{6,0},{7,1},{8,14},{9,15},{10,... | collective-permute-start | bytes 393224 | tf_op jit(solution)/shard_map/ppermute | solution.py:343
  11.7 10.0 %collective-permute-start = (bf16[128,512]{1,0:T(8,128)(2,1)}, bf16[128,512]{1,0:T(8,128)(2,1)S(1)}, u32[]{:S(2)}, u32[]{:S(2)}) collective-permute-start(bf16[128,512]{1,0:T(8,128)(2,1)} %refs_7_.1), channel_id=1, source_target_pairs={{0,7},{1,6},{2,5},{3,4},{4,3},{5,2},{6,1},{7,0},{8,15},{9,14},{10,... | collective-permute-start | bytes 393224 | tf_op jit(solution)/shard_map/ppermute | solution.py:343
  15.7 22.1 %copy-start = (bf16[4096,512]{1,0:T(8,128)(2,1)S(1)}, bf16[4096,512]{1,0:T(8,128)(2,1)}, u32[]{:S(2)}) copy-start(bf16[4096,512]{1,0:T(8,128)(2,1)} %w_query.1) | copy-start | bytes 12582916
  15.7 1.4 %copy-start.3 = (bf16[4096,128]{1,0:T(8,128)(2,1)S(1)}, bf16[4096,128]{1,0:T(8,128)(2,1)}, u32[]{:S(2)}) copy-start(bf16[4096,128]{1,0:T(8,128)(2,1)} %refs_12_.3) | copy-start | bytes 3145732
  17.1 1.4 %copy-start.5 = (bf16[4096,128]{1,0:T(8,128)(2,1)S(1)}, bf16[4096,128]{1,0:T(8,128)(2,1)}, u32[]{:S(2)}) copy-start(bf16[4096,128]{1,0:T(8,128)(2,1)} %refs_13_.1) | copy-start | bytes 3145732
  18.5 0.9 copy-start.7
  19.4 0.7 copy-start.10
  20.1 5.2 %copy-start.9 = (bf16[128,512]{1,0:T(8,128)(2,1)S(1)}, bf16[128,512]{1,0:T(8,128)(2,1)}, u32[]{:S(2)}) copy-start(bf16[128,512]{1,0:T(8,128)(2,1)} %refs_8_.1) | copy-start | bytes 393220
  20.1 5.2 %collective-permute-start.7 = (bf16[128,512]{1,0:T(8,128)(2,1)}, bf16[128,512]{1,0:T(8,128)(2,1)S(1)}, u32[]{:S(2)}, u32[]{:S(2)}) collective-permute-start(bf16[128,512]{1,0:T(8,128)(2,1)} %refs_8_.1), channel_id=1, source_target_pairs={{0,1},{1,0},{2,3},{3,2},{4,5},{5,4},{6,7},{7,6},{8,9},{9,8},{10,11... | collective-permute-start | bytes 393224 | tf_op jit(solution)/shard_map/ppermute | solution.py:343
  25.3 20.1 %collective-permute-start.10 = (bf16[256,512]{1,0:T(8,128)(2,1)S(1)}, bf16[256,512]{1,0:T(8,128)(2,1)S(1)}, u32[]{:S(2)}, u32[]{:S(2)}) collective-permute-start(bf16[256,512]{1,0:T(8,128)(2,1)S(1)} %hold.1.refs_8_), channel_id=1, source_target_pairs={{0,6},{1,7},{2,4},{3,5},{4,2},{5,3},{6,0},{7,1},{8,14},{9,15},{10,... | collective-permute-start | bytes 786440 | tf_op jit(solution)/shard_map/ppermute | solution.py:343
  25.4 20.0 %collective-permute-start.9 = (bf16[256,512]{1,0:T(8,128)(2,1)S(1)}, bf16[256,512]{1,0:T(8,128)(2,1)S(1)}, u32[]{:S(2)}, u32[]{:S(2)}) collective-permute-start(bf16[256,512]{1,0:T(8,128)(2,1)S(1)} %hold.1.refs_8_), channel_id=1, source_target_pairs={{0,4},{1,5},{2,6},{3,7},{4,0},{5,1},{6,2},{7,3},{8,12},{9,13},{10,... | collective-permute-start | bytes 786440 | tf_op jit(solution)/shard_map/ppermute | solution.py:343
  28.1 17.3 %collective-permute-start.8 = (bf16[256,512]{1,0:T(8,128)(2,1)S(1)}, bf16[256,512]{1,0:T(8,128)(2,1)S(1)}, u32[]{:S(2)}, u32[]{:S(2)}) collective-permute-start(bf16[256,512]{1,0:T(8,128)(2,1)S(1)} %hold.1.refs_8_), channel_id=1, source_target_pairs={{0,2},{1,3},{2,0},{3,1},{4,6},{5,7},{6,4},{7,5},{8,10},{9,11},{10,... | collective-permute-start | bytes 786440 | tf_op jit(solution)/shard_map/ppermute | solution.py:343
  29.5 1.3 %collective-permute-start.12 = (bf16[128,256]{1,0:T(8,128)(2,1)S(1)}, bf16[128,256]{1,0:T(8,128)(2,1)S(1)}, u32[]{:S(2)}, u32[]{:S(2)}) collective-permute-start(bf16[128,256]{1,0:T(8,128)(2,1)S(1)} %get-tuple-element.36.refs_0_.mine.refs_4_), channel_id=1, source_target_pairs={{0,8},{8,0},{16,24},{24,16},{32,40},{40,32},{48,56},{56,48},{64,72... | collective-permute-start | bytes 196616 | tf_op jit(solution)/shard_map/ppermute | solution.py:347
  31.3 14.1 %collective-permute-start.13 = (bf16[256,256]{1,0:T(8,128)(2,1)S(1)}, bf16[256,256]{1,0:T(8,128)(2,1)S(1)}, u32[]{:S(2)}, u32[]{:S(2)}) collective-permute-start(bf16[256,256]{1,0:T(8,128)(2,1)S(1)} %join.1), channel_id=1, source_target_pairs={{0,96},{8,168},{16,112},{24,184},{32,128},{40,200},{48,144},{56,21... | collective-permute-start | bytes 393224 | tf_op jit(solution)/shard_map/ppermute | solution.py:359
  37.2 8.2 %collective-permute-start.11 = (bf16[128,256]{1,0:T(8,128)(2,1)S(1)}, bf16[128,256]{1,0:T(8,128)(2,1)S(1)}, u32[]{:S(2)}, u32[]{:S(2)}) collective-permute-start(bf16[128,256]{1,0:T(8,128)(2,1)S(1)} %get-tuple-element.36.refs_0_.mine.refs_4_), channel_id=1, source_target_pairs={{0,128},{8,136},{16,144},{24,152},{32,160},{40,168},{48,176},{56,1... | collective-permute-start | bytes 196616 | tf_op jit(solution)/shard_map/ppermute | solution.py:355
  37.8 2.2 %copy-start.1 = (bf16[512,4096]{1,0:T(8,128)(2,1)S(1)}, bf16[512,4096]{1,0:T(8,128)(2,1)}, u32[]{:S(2)}) copy-start(bf16[512,4096]{1,0:T(8,128)(2,1)} %refs_12_.2) | copy-start | bytes 12582916
  40.0 5.5 %copy-start.2 = (bf16[512,4096]{1,0:T(8,128)(2,1)S(1)}, bf16[512,4096]{1,0:T(8,128)(2,1)}, u32[]{:S(2)}) copy-start(bf16[512,4096]{1,0:T(8,128)(2,1)} %refs_12_.2) | copy-start | bytes 12582916
  40.0 5.5 %copy-start.8 = (bf16[128,512]{1,0:T(8,128)(2,1)S(1)}, bf16[128,512]{1,0:T(8,128)(2,1)}, u32[]{:S(2)}) copy-start(bf16[128,512]{1,0:T(8,128)(2,1)} %refs_7_.1) | copy-start | bytes 393220
  40.0 22.8 %copy-start.12 = (s32[64]{0:T(128)S(1)}, s32[64]{0:T(128)}, u32[]{:S(2)}) copy-start(s32[64]{0:T(128)} %order.1) | copy-start | bytes 772
  40.0 22.8 %copy-start.13 = (s32[8]{0:T(128)S(1)}, s32[8]{0:T(128)}, u32[]{:S(2)}) copy-start(s32[8]{0:T(128)} %lengths.1) | copy-start | bytes 100
  48.2 8.9 %collective-permute-start.15 = (bf16[256,512]{1,0:T(8,128)(2,1)S(1)}, bf16[256,512]{1,0:T(8,128)(2,1)S(1)}, u32[]{:S(2)}, u32[]{:S(2)}) collective-permute-start(bf16[256,512]{1,0:T(8,128)(2,1)S(1)} %get-tuple-element.38.refs_0_), channel_id=1, source_target_pairs={{0,16},{8,24},{16,0},{24,8},{32,48},{40,56},{48,32},{56,40},{64,80... | collective-permute-start | bytes 786440 | tf_op jit(solution)/shard_map/ppermute | solution.py:347
  51.4 7.2 %collective-permute-start.18 = (bf16[256,256]{1,0:T(8,128)(2,1)S(1)}, bf16[256,256]{1,0:T(8,128)(2,1)S(1)}, u32[]{:S(2)}, u32[]{:S(2)}) collective-permute-start(bf16[256,256]{1,0:T(8,128)(2,1)S(1)} %join.1), channel_id=1, source_target_pairs={{0,64},{8,200},{16,80},{24,216},{32,96},{40,232},{48,112},{56,248}... | collective-permute-start | bytes 393224 | tf_op jit(solution)/shard_map/ppermute | solution.py:359
  52.9 7.8 %collective-permute-start.17 = (bf16[256,256]{1,0:T(8,128)(2,1)S(1)}, bf16[256,256]{1,0:T(8,128)(2,1)S(1)}, u32[]{:S(2)}, u32[]{:S(2)}) collective-permute-start(bf16[256,256]{1,0:T(8,128)(2,1)S(1)} %join.1), channel_id=1, source_target_pairs={{0,32},{8,232},{16,48},{24,248},{32,64},{40,8},{48,80},{56,24},{64... | collective-permute-start | bytes 393224 | tf_op jit(solution)/shard_map/ppermute | solution.py:359
  55.6 7.1 %collective-permute-start.14 = (bf16[256,512]{1,0:T(8,128)(2,1)S(1)}, bf16[256,512]{1,0:T(8,128)(2,1)S(1)}, u32[]{:S(2)}, u32[]{:S(2)}) collective-permute-start(bf16[256,512]{1,0:T(8,128)(2,1)S(1)} %get-tuple-element.38.refs_0_), channel_id=1, source_target_pairs={{0,8},{8,0},{16,24},{24,16},{32,40},{40,32},{48,56},{56,48},{64,72... | collective-permute-start | bytes 786440 | tf_op jit(solution)/shard_map/ppermute | solution.py:347
  57.2 5.6 %collective-permute-start.16 = (bf16[256,512]{1,0:T(8,128)(2,1)S(1)}, bf16[256,512]{1,0:T(8,128)(2,1)S(1)}, u32[]{:S(2)}, u32[]{:S(2)}) collective-permute-start(bf16[256,512]{1,0:T(8,128)(2,1)S(1)} %collective-permute-done.15.refs_2_), channel_id=1, source_target_pairs={{0,8},{8,0},{16,24},{24,16},{32,40},{40,32},{48,56},{56,48},{64,72... | collective-permute-start | bytes 786440 | tf_op jit(solution)/shard_map/ppermute | solution.py:347
  61.2 1.5 %collective-permute-start.19 = (bf16[384,256]{1,0:T(8,128)(2,1)S(1)}, bf16[384,256]{1,0:T(8,128)(2,1)S(1)}, u32[]{:S(2)}, u32[]{:S(2)}) collective-permute-start(bf16[384,256]{1,0:T(8,128)(2,1)S(1)} %sort.1), channel_id=1, source_target_pairs={{0,8},{8,0},{16,24},{24,16},{32,40},{40,32},{48,56},{56,48},{64,72... | collective-permute-start | bytes 589832 | tf_op jit(solution)/shard_map/ppermute | solution.py:347
  67.5 5.8 %collective-permute-start.21 = (f32[128,128]{1,0:T(8,128)S(1)}, f32[128,128]{1,0:T(8,128)S(1)}, u32[]{:S(2)}, u32[]{:S(2)}) collective-permute-start(f32[128,128]{1,0:T(8,128)S(1)} %get-tuple-element.42.refs_7_), channel_id=1, source_target_pairs={{0,16},{8,24},{16,0},{24,8},{32,48},{40,56},{48,32},{56,40},{64,80... | collective-permute-start | bytes 196616 | tf_op jit(solution)/shard_map/ppermute | solution.py:347
  68.1 5.3 %collective-permute-start.20 = (f32[128,128]{1,0:T(8,128)S(1)}, f32[128,128]{1,0:T(8,128)S(1)}, u32[]{:S(2)}, u32[]{:S(2)}) collective-permute-start(f32[128,128]{1,0:T(8,128)S(1)} %get-tuple-element.42.refs_7_), channel_id=1, source_target_pairs={{0,8},{8,0},{16,24},{24,16},{32,40},{40,32},{48,56},{56,48},{64,72... | collective-permute-start | bytes 196616 | tf_op jit(solution)/shard_map/ppermute | solution.py:347
  73.4 1.3 %collective-permute-start.22 = (f32[128,128]{1,0:T(8,128)S(1)}, f32[128,128]{1,0:T(8,128)S(1)}, u32[]{:S(2)}, u32[]{:S(2)}) collective-permute-start(f32[128,128]{1,0:T(8,128)S(1)} %collective-permute-done.21.refs_9_), channel_id=1, source_target_pairs={{0,8},{8,0},{16,24},{24,16},{32,40},{40,32},{48,56},{56,48},{64,72... | collective-permute-start | bytes 196616 | tf_op jit(solution)/shard_map/ppermute | solution.py:347
  78.7 10.5 %collective-permute-start.29 = (bf16[256,512]{1,0:T(8,128)(2,1)S(1)}, bf16[256,512]{1,0:T(8,128)(2,1)S(1)}, u32[]{:S(2)}, u32[]{:S(2)}) collective-permute-start(bf16[256,512]{1,0:T(8,128)(2,1)S(1)} %get-tuple-element.53), channel_id=1, source_target_pairs={{0,8},{8,0},{16,24},{24,16},{32,40},{40,32},{48,56},{56,48},{64,72... | collective-permute-start | bytes 786440 | tf_op jit(solution)/shard_map/ppermute | solution.py:347
  79.2 5.0 %collective-permute-start.24 = (bf16[3,256,128]{2,1,0:T(8,128)(2,1)S(1)}, bf16[3,256,128]{2,1,0:T(8,128)(2,1)S(1)}, u32[]{:S(2)}, u32[]{:S(2)}) collective-permute-start(bf16[3,256,128]{2,1,0:T(8,128)(2,1)S(1)} %get-tuple-element.45), channel_id=1, source_target_pairs={{0,8},{8,0},{16,24},{24,16},{32,40},{40,32},{48,56},{56,48},{64,72... | collective-permute-start | bytes 589832 | tf_op jit(solution)/shard_map/ppermute | solution.py:347
  79.5 9.7 %collective-permute-start.23 = (bf16[256,128]{1,0:T(8,128)(2,1)S(1)}, bf16[256,128]{1,0:T(8,128)(2,1)S(1)}, u32[]{:S(2)}, u32[]{:S(2)}) collective-permute-start(bf16[256,128]{1,0:T(8,128)(2,1)S(1)} %get-tuple-element.43), channel_id=1, source_target_pairs={{0,128},{8,136},{16,144},{24,152},{32,160},{40,168},{48,176},{56,1... | collective-permute-start | bytes 196616 | tf_op jit(solution)/shard_map/ppermute | solution.py:355
  84.2 15.9 %copy-start.4 = (bf16[4096,128]{1,0:T(8,128)(2,1)S(1)}, bf16[4096,128]{1,0:T(8,128)(2,1)}, u32[]{:S(2)}) copy-start(bf16[4096,128]{1,0:T(8,128)(2,1)} %refs_12_.3) | copy-start | bytes 3145732
  84.2 15.9 %copy-start.6 = (bf16[4096,128]{1,0:T(8,128)(2,1)S(1)}, bf16[4096,128]{1,0:T(8,128)(2,1)}, u32[]{:S(2)}) copy-start(bf16[4096,128]{1,0:T(8,128)(2,1)} %refs_13_.1) | copy-start | bytes 3145732
  84.2 15.9 %copy-start.11 = (f32[4096]{0:T(1024)S(1)}, f32[4096]{0:T(1024)}, u32[]{:S(2)}) copy-start(f32[4096]{0:T(1024)} %param.11) | copy-start | bytes 49156
  84.8 8.1 %collective-permute-start.25 = (bf16[2,256,128]{2,1,0:T(8,128)(2,1)S(1)}, bf16[2,256,128]{2,1,0:T(8,128)(2,1)S(1)}, u32[]{:S(2)}, u32[]{:S(2)}) collective-permute-start(bf16[2,256,128]{2,1,0:T(8,128)(2,1)S(1)} %get-tuple-element.46), channel_id=1, source_target_pairs={{0,224},{8,40},{16,240},{24,56},{32,0},{40,72},{48,16},{56,88},{64... | collective-permute-start | bytes 393224 | tf_op jit(solution)/shard_map/ppermute | solution.py:359
  85.4 7.5 %collective-permute-start.26 = (bf16[2,256,128]{2,1,0:T(8,128)(2,1)S(1)}, bf16[2,256,128]{2,1,0:T(8,128)(2,1)S(1)}, u32[]{:S(2)}, u32[]{:S(2)}) collective-permute-start(bf16[2,256,128]{2,1,0:T(8,128)(2,1)S(1)} %get-tuple-element.47), channel_id=1, source_target_pairs={{0,192},{8,72},{16,208},{24,88},{32,224},{40,104},{48,240},{56,120... | collective-permute-start | bytes 393224 | tf_op jit(solution)/shard_map/ppermute | solution.py:359
  85.9 12.0 %collective-permute-start.27 = (bf16[2,256,128]{2,1,0:T(8,128)(2,1)S(1)}, bf16[2,256,128]{2,1,0:T(8,128)(2,1)S(1)}, u32[]{:S(2)}, u32[]{:S(2)}) collective-permute-start(bf16[2,256,128]{2,1,0:T(8,128)(2,1)S(1)} %get-tuple-element.48), channel_id=1, source_target_pairs={{0,160},{8,104},{16,176},{24,120},{32,192},{40,136},{48,208},{56,1... | collective-permute-start | bytes 393224 | tf_op jit(solution)/shard_map/ppermute | solution.py:359
  89.2 9.3 %collective-permute-start.30 = (bf16[128,512]{1,0:T(8,128)(2,1)S(1)}, bf16[128,512]{1,0:T(8,128)(2,1)S(1)}, u32[]{:S(2)}, u32[]{:S(2)}) collective-permute-start(bf16[128,512]{1,0:T(8,128)(2,1)S(1)} %get-tuple-element.55), channel_id=1, source_target_pairs={{0,16},{8,24},{16,0},{24,8},{32,48},{40,56},{48,32},{56,40},{64,80... | collective-permute-start | bytes 393224 | tf_op jit(solution)/shard_map/ppermute | solution.py:347
  98.5 1.6 %collective-permute-start.28 = (bf16[256,128]{1,0:T(8,128)(2,1)S(1)}, bf16[256,128]{1,0:T(8,128)(2,1)S(1)}, u32[]{:S(2)}, u32[]{:S(2)}) collective-permute-start(bf16[256,128]{1,0:T(8,128)(2,1)S(1)} %get-tuple-element.51), channel_id=1, source_target_pairs={{0,8},{8,0},{16,24},{24,16},{32,40},{40,32},{48,56},{56,48},{64,72... | collective-permute-start | bytes 196616 | tf_op jit(solution)/shard_map/ppermute | solution.py:347
  101.6 7.1 %collective-permute-start.31 = (bf16[144,512]{1,0:T(8,128)(2,1)S(1)}, bf16[144,512]{1,0:T(8,128)(2,1)S(1)}, u32[]{:S(2)}, u32[]{:S(2)}) collective-permute-start(bf16[144,512]{1,0:T(8,128)(2,1)S(1)} %get-tuple-element.58), channel_id=1, source_target_pairs={{0,1},{1,0},{2,3},{3,2},{4,5},{5,4},{6,7},{7,6},{8,9},{9,8},{10,11... | collective-permute-start | bytes 442376 | tf_op jit(solution)/shard_map/ppermute | solution.py:343
  102.2 6.7 %collective-permute-start.32 = (bf16[144,512]{1,0:T(8,128)(2,1)S(1)}, bf16[144,512]{1,0:T(8,128)(2,1)S(1)}, u32[]{:S(2)}, u32[]{:S(2)}) collective-permute-start(bf16[144,512]{1,0:T(8,128)(2,1)S(1)} %get-tuple-element.59), channel_id=1, source_target_pairs={{0,2},{1,3},{2,0},{3,1},{4,6},{5,7},{6,4},{7,5},{8,10},{9,11},{10,... | collective-permute-start | bytes 442376 | tf_op jit(solution)/shard_map/ppermute | solution.py:343
  103.4 15.0 %collective-permute-start.33 = (bf16[144,512]{1,0:T(8,128)(2,1)S(1)}, bf16[144,512]{1,0:T(8,128)(2,1)S(1)}, u32[]{:S(2)}, u32[]{:S(2)}) collective-permute-start(bf16[144,512]{1,0:T(8,128)(2,1)S(1)} %get-tuple-element.60), channel_id=1, source_target_pairs={{0,4},{1,5},{2,6},{3,7},{4,0},{5,1},{6,2},{7,3},{8,12},{9,13},{10,... | collective-permute-start | bytes 442376 | tf_op jit(solution)/shard_map/ppermute | solution.py:343
  103.8 14.6 %collective-permute-start.34 = (bf16[144,512]{1,0:T(8,128)(2,1)S(1)}, bf16[144,512]{1,0:T(8,128)(2,1)S(1)}, u32[]{:S(2)}, u32[]{:S(2)}) collective-permute-start(bf16[144,512]{1,0:T(8,128)(2,1)S(1)} %get-tuple-element.61), channel_id=1, source_target_pairs={{0,5},{1,4},{2,7},{3,6},{4,1},{5,0},{6,3},{7,2},{8,13},{9,12},{10,... | collective-permute-start | bytes 442376 | tf_op jit(solution)/shard_map/ppermute | solution.py:343
  107.4 11.0 %collective-permute-start.35 = (bf16[144,512]{1,0:T(8,128)(2,1)S(1)}, bf16[144,512]{1,0:T(8,128)(2,1)S(1)}, u32[]{:S(2)}, u32[]{:S(2)}) collective-permute-start(bf16[144,512]{1,0:T(8,128)(2,1)S(1)} %get-tuple-element.62), channel_id=1, source_target_pairs={{0,3},{1,2},{2,1},{3,0},{4,7},{5,6},{6,5},{7,4},{8,11},{9,10},{10,... | collective-permute-start | bytes 442376 | tf_op jit(solution)/shard_map/ppermute | solution.py:343
  108.7 12.3 %collective-permute-start.36 = (bf16[144,512]{1,0:T(8,128)(2,1)S(1)}, bf16[144,512]{1,0:T(8,128)(2,1)S(1)}, u32[]{:S(2)}, u32[]{:S(2)}) collective-permute-start(bf16[144,512]{1,0:T(8,128)(2,1)S(1)} %get-tuple-element.63), channel_id=1, source_target_pairs={{0,6},{1,7},{2,4},{3,5},{4,2},{5,3},{6,0},{7,1},{8,14},{9,15},{10,... | collective-permute-start | bytes 442376 | tf_op jit(solution)/shard_map/ppermute | solution.py:343
  108.9 12.0 %collective-permute-start.37 = (bf16[144,512]{1,0:T(8,128)(2,1)S(1)}, bf16[144,512]{1,0:T(8,128)(2,1)S(1)}, u32[]{:S(2)}, u32[]{:S(2)}) collective-permute-start(bf16[144,512]{1,0:T(8,128)(2,1)S(1)} %get-tuple-element.64), channel_id=1, source_target_pairs={{0,7},{1,6},{2,5},{3,4},{4,3},{5,2},{6,1},{7,0},{8,15},{9,14},{10,... | collective-permute-start | bytes 442376 | tf_op jit(solution)/shard_map/ppermute | solution.py:343

commit v3 on v2

--- a/solution.py
+++ b/solution.py
@@ -403,7 +403,7 @@
     projected, dot_row = call(
         project_kernel,
         [ids],
-        [*xs, *dys, w_out, normed, w_query, ready_out, kvs[1], near[2]],
+        [*xs, *dys, w_out, normed, w_query, ready_out, near[2]],
         [shape((2 * ROWS, SHARE), bf16), shape((8, ROWS), f32)],
         24,
         flops=4 * ROWS * D * SHARE,

time: 123 us -> 125 us (1.016)
  starting transfers between devices: 55.4 us -> 58.6 us
    ppermute x6, starting transfers between devices: 13.2 us -> 17.4 us  [apart(): lax.ppermute(a, 'ctx', [(i, (i + 4 * k * (1 - 2 * (i % 2))) % 32) for i i...]
    ppermute x18, waiting for transfers between devices: 10.1 us -> 14.1 us  [xor_head(): return lax.ppermute(a, 'head', [(i, i ^ k) for i in range(GROUPS)])]
    ppermute x18, starting transfers between devices: 31.8 us -> 27.9 us  [xor_head(): return lax.ppermute(a, 'head', [(i, i ^ k) for i in range(GROUPS)])]
    ppermute x2, waiting for transfers between devices: 6.83 us -> 4.59 us  [turn(): return lax.ppermute(a, 'ctx', [(i, (i + 4 * k) % 32) for i in range(32)])]
    ppermute x2, starting transfers between devices: 5.18 us -> 7.27 us  [turn(): return lax.ppermute(a, 'ctx', [(i, (i + 4 * k) % 32) for i in range(32)])]
    ppermute x12, waiting for transfers between devices: 10.7 us -> 9.21 us  [xor_ctx(): return lax.ppermute(a, 'ctx', [(i, i ^ k) for i in range(32)])]
    ppermute x6, waiting for transfers between devices: 11.6 us -> 10.3 us  [apart(): lax.ppermute(a, 'ctx', [(i, (i + 4 * k * (1 - 2 * (i % 2))) % 32) for i i...]
  transfers between devices with their start and end apart: 38 -> 38, of which waited for: 15 -> 13; matrix products, arithmetic and copies ran while one was open for 0% -> 0% of each run, Pallas kernels for 5% -> 5%
where the time goes in v3:
time: 125 us
  starting transfers between devices  58.6 us (47%)
  waiting for transfers between devices  38.3 us (31%)
  Pallas kernels  20.2 us (16%)
  local copies, waits for them, and re-layouts  6.64 us (5%)
    ppermute x18, starting transfers between devices, xor_head(): return lax.ppermute(a, 'head', [(i, i ^ k) for i in range(GROUPS)])  27.9 us
    pallas_call x15, Pallas kernels, call(): pl.pallas_call(body, out_shape=outs, in_specs=smem(len(scalars)) + vmem(l...  20.2 us
    ppermute x6, starting transfers between devices, apart(): lax.ppermute(a, 'ctx', [(i, (i + 4 * k * (1 - 2 * (i % 2))) % 32) for i i...  17.4 us
    ppermute x18, waiting for transfers between devices, xor_head(): return lax.ppermute(a, 'head', [(i, i ^ k) for i in range(GROUPS)])  14.1 us
    ppermute x6, waiting for transfers between devices, apart(): lax.ppermute(a, 'ctx', [(i, (i + 4 * k * (1 - 2 * (i % 2))) % 32) for i i...  10.3 us
    ppermute x12, waiting for transfers between devices, xor_ctx(): return lax.ppermute(a, 'ctx', [(i, i ^ k) for i in range(32)])  9.21 us
    ppermute x2, starting transfers between devices, turn(): return lax.ppermute(a, 'ctx', [(i, (i + 4 * k) % 32) for i in range(32)])  7.27 us
    unnamed x28, local copies, waits for them, and re-layouts  6.64 us
  transfers between devices with their start and end apart: 38, of which 13 were waited for; matrix products, arithmetic and copies ran while one was open for 0% of the time, Pallas kernels for 5%

profile of v3, /device:TPU:32, one launch (start us, length us, event | category | flops | bytes accessed | tf_op | source)
XLA Modules:
  0.0 124.7 jit_solution(8868195669057776512)
XLA Ops:
  0.6 1.6 %collective-permute-start.6 = (bf16[128,512]{1,0:T(8,128)(2,1)}, bf16[128,512]{1,0:T(8,128)(2,1)S(1)}, u32[]{:S(2)}, u32[]{:S(2)}) collective-permute-start(bf16[128,512]{1,0:T(8,128)(2,1)} %refs_7_.1), channel_id=1, source_target_pairs={{0,1},{1,0},{2,3},{3,2},{4,5},{5,4},{6,7},{7,6},{8,9},{9,8},{10,11... | collective-permute-start | bytes 393224 | tf_op jit(solution)/shard_map/ppermute | solution.py:343
  2.2 1.6 %collective-permute-start.5 = (bf16[128,512]{1,0:T(8,128)(2,1)}, bf16[128,512]{1,0:T(8,128)(2,1)S(1)}, u32[]{:S(2)}, u32[]{:S(2)}) collective-permute-start(bf16[128,512]{1,0:T(8,128)(2,1)} %refs_7_.1), channel_id=1, source_target_pairs={{0,2},{1,3},{2,0},{3,1},{4,6},{5,7},{6,4},{7,5},{8,10},{9,11},{10,... | collective-permute-start | bytes 393224 | tf_op jit(solution)/shard_map/ppermute | solution.py:343
  3.8 2.9 %collective-permute-start.4 = (bf16[128,512]{1,0:T(8,128)(2,1)}, bf16[128,512]{1,0:T(8,128)(2,1)S(1)}, u32[]{:S(2)}, u32[]{:S(2)}) collective-permute-start(bf16[128,512]{1,0:T(8,128)(2,1)} %refs_7_.1), channel_id=1, source_target_pairs={{0,4},{1,5},{2,6},{3,7},{4,0},{5,1},{6,2},{7,3},{8,12},{9,13},{10,... | collective-permute-start | bytes 393224 | tf_op jit(solution)/shard_map/ppermute | solution.py:343
  6.7 0.6 collective-permute-start.3
  7.3 1.4 %collective-permute-start.2 = (bf16[128,512]{1,0:T(8,128)(2,1)}, bf16[128,512]{1,0:T(8,128)(2,1)S(1)}, u32[]{:S(2)}, u32[]{:S(2)}) collective-permute-start(bf16[128,512]{1,0:T(8,128)(2,1)} %refs_7_.1), channel_id=1, source_target_pairs={{0,3},{1,2},{2,1},{3,0},{4,7},{5,6},{6,5},{7,4},{8,11},{9,10},{10,... | collective-permute-start | bytes 393224 | tf_op jit(solution)/shard_map/ppermute | solution.py:343
  8.7 3.0 %collective-permute-start.1 = (bf16[128,512]{1,0:T(8,128)(2,1)}, bf16[128,512]{1,0:T(8,128)(2,1)S(1)}, u32[]{:S(2)}, u32[]{:S(2)}) collective-permute-start(bf16[128,512]{1,0:T(8,128)(2,1)} %refs_7_.1), channel_id=1, source_target_pairs={{0,6},{1,7},{2,4},{3,5},{4,2},{5,3},{6,0},{7,1},{8,14},{9,15},{10,... | collective-permute-start | bytes 393224 | tf_op jit(solution)/shard_map/ppermute | solution.py:343
  11.7 4.0 %collective-permute-start = (bf16[128,512]{1,0:T(8,128)(2,1)}, bf16[128,512]{1,0:T(8,128)(2,1)S(1)}, u32[]{:S(2)}, u32[]{:S(2)}) collective-permute-start(bf16[128,512]{1,0:T(8,128)(2,1)} %refs_7_.1), channel_id=1, source_target_pairs={{0,7},{1,6},{2,5},{3,4},{4,3},{5,2},{6,1},{7,0},{8,15},{9,14},{10,... | collective-permute-start | bytes 393224 | tf_op jit(solution)/shard_map/ppermute | solution.py:343
  15.7 1.4 %copy-done.3 = bf16[4096,128]{1,0:T(8,128)(2,1)S(1)} copy-done((bf16[4096,128]{1,0:T(8,128)(2,1)S(1)}, bf16[4096,128]{1,0:T(8,128)(2,1)}, u32[]{:S(2)}) %copy-start.3) | copy-done | bytes 1048600
  17.1 1.4 %copy-done.5 = bf16[4096,128]{1,0:T(8,128)(2,1)S(1)} copy-done((bf16[4096,128]{1,0:T(8,128)(2,1)S(1)}, bf16[4096,128]{1,0:T(8,128)(2,1)}, u32[]{:S(2)}) %copy-start.5) | copy-done | bytes 1048600
  18.5 0.9 copy-done.7
  19.4 0.7 copy-done.10
  20.1 1.5 %collective-permute-start.7 = (bf16[128,512]{1,0:T(8,128)(2,1)}, bf16[128,512]{1,0:T(8,128)(2,1)S(1)}, u32[]{:S(2)}, u32[]{:S(2)}) collective-permute-start(bf16[128,512]{1,0:T(8,128)(2,1)} %refs_8_.1), channel_id=1, source_target_pairs={{0,1},{1,0},{2,3},{3,2},{4,5},{5,4},{6,7},{7,6},{8,9},{9,8},{10,11... | collective-permute-start | bytes 393224 | tf_op jit(solution)/shard_map/ppermute | solution.py:343
  21.6 0.1 pad_add_fusion.ids
  21.7 1.8 %norm_kv.1 = (bf16[128,256]{1,0:T(8,128)(2,1)S(1)}, bf16[128,4096]{1,0:T(8,128)(2,1)S(1)}, f32[128,128]{1,0:T(8,128)S(1)}, f32[8,128]{1,0:T(8,128)S(1)}) custom-call(s32[2]{0:T(128)S(1)} %pad_add_fusion.ids, bf16[128,512]{1,0:T(8,128)(2,1)S(1)} %copy-done.7, bf16[128,512]{1,0:T(8,128)(2,1)S(1)} %collective-permute-done.refs_1_.refs_3_, ...), custom_call_target="tpu_custom_call" | custom-call | flops 268435456 | bytes 5242880 | tf_op jit(solution)/shard_map/norm_kv/pallas_call | solution.py:55
  23.5 1.7 %collective-permute-done.7.other = bf16[128,512]{1,0:T(8,128)(2,1)S(1)} collective-permute-done((bf16[128,512]{1,0:T(8,128)(2,1)}, bf16[128,512]{1,0:T(8,128)(2,1)S(1)}, u32[]{:S(2)}, u32[]{:S(2)}) %collective-permute-start.7) | collective-permute-done | bytes 131104 | tf_op jit(solution)/shard_map/ppermute | solution.py:343
  25.3 0.1 collective-permute-start.10
  25.4 2.7 %collective-permute-start.9 = (bf16[256,512]{1,0:T(8,128)(2,1)S(1)}, bf16[256,512]{1,0:T(8,128)(2,1)S(1)}, u32[]{:S(2)}, u32[]{:S(2)}) collective-permute-start(bf16[256,512]{1,0:T(8,128)(2,1)S(1)} %hold.1.refs_8_), channel_id=1, source_target_pairs={{0,4},{1,5},{2,6},{3,7},{4,0},{5,1},{6,2},{7,3},{8,12},{9,13},{10,... | collective-permute-start | bytes 786440 | tf_op jit(solution)/shard_map/ppermute | solution.py:343
  28.1 1.4 %collective-permute-start.8 = (bf16[256,512]{1,0:T(8,128)(2,1)S(1)}, bf16[256,512]{1,0:T(8,128)(2,1)S(1)}, u32[]{:S(2)}, u32[]{:S(2)}) collective-permute-start(bf16[256,512]{1,0:T(8,128)(2,1)S(1)} %hold.1.refs_8_), channel_id=1, source_target_pairs={{0,2},{1,3},{2,0},{3,1},{4,6},{5,7},{6,4},{7,5},{8,10},{9,11},{10,... | collective-permute-start | bytes 786440 | tf_op jit(solution)/shard_map/ppermute | solution.py:343
  29.5 1.3 %collective-permute-done.11.other = bf16[128,256]{1,0:T(8,128)(2,1)S(1)} collective-permute-done((bf16[128,256]{1,0:T(8,128)(2,1)S(1)}, bf16[128,256]{1,0:T(8,128)(2,1)S(1)}, u32[]{:S(2)}, u32[]{:S(2)}) %collective-permute-start.11) | collective-permute-done | bytes 65568 | tf_op jit(solution)/shard_map/ppermute | solution.py:347
  30.8 0.6 join.1
  31.3 5.9 %collective-permute-start.12 = (bf16[256,256]{1,0:T(8,128)(2,1)S(1)}, bf16[256,256]{1,0:T(8,128)(2,1)S(1)}, u32[]{:S(2)}, u32[]{:S(2)}) collective-permute-start(bf16[256,256]{1,0:T(8,128)(2,1)S(1)} %join.1), channel_id=1, source_target_pairs={{0,96},{8,168},{16,112},{24,184},{32,128},{40,200},{48,144},{56,21... | collective-permute-start | bytes 393224 | tf_op jit(solution)/shard_map/ppermute | solution.py:359
  37.2 2.2 %copy-done.1 = bf16[512,4096]{1,0:T(8,128)(2,1)S(1)} copy-done((bf16[512,4096]{1,0:T(8,128)(2,1)S(1)}, bf16[512,4096]{1,0:T(8,128)(2,1)}, u32[]{:S(2)}) %copy-start.1) | copy-done | bytes 4194328
  39.4 0.0 copy-start.13
  39.5 2.2 %collective-permute-done.12.refs_16_.refs_2_.refs_8_ = bf16[256,256]{1,0:T(8,128)(2,1)S(1)} collective-permute-done((bf16[256,256]{1,0:T(8,128)(2,1)S(1)}, bf16[256,256]{1,0:T(8,128)(2,1)S(1)}, u32[]{:S(2)}, u32[]{:S(2)}) %collective-permute-start.12) | collective-permute-done | bytes 131104 | tf_op jit(solution)/shard_map/ppermute | solution.py:359
  41.7 2.8 %project.1 = (bf16[256,512]{1,0:T(8,128)(2,1)S(1)}, f32[8,128]{1,0:T(8,128)S(1)}) custom-call(s32[2]{0:T(128)S(1)} %pad_add_fusion.ids, bf16[128,512]{1,0:T(8,128)(2,1)S(1)} %copy-done.8, bf16[128,512]{1,0:T(8,128)(2,1)S(1)} %collective-permute-done.refs_1_.refs_3_, bf16[128,512]{1,0:T(8,128)(2,1)S(1)} %collective-permute-done.1.refs_2_.refs_4_, ...), custom_call_target="tpu_custom_call" | custom-call | flops 1073741824 | bytes 10485760 | tf_op jit(solution)/shard_map/project/pallas_call | solution.py:55
  44.5 3.1 %collective-permute-start.14 = (bf16[256,512]{1,0:T(8,128)(2,1)S(1)}, bf16[256,512]{1,0:T(8,128)(2,1)S(1)}, u32[]{:S(2)}, u32[]{:S(2)}) collective-permute-start(bf16[256,512]{1,0:T(8,128)(2,1)S(1)} %get-tuple-element.38.refs_0_), channel_id=1, source_target_pairs={{0,16},{8,24},{16,0},{24,8},{32,48},{40,56},{48,32},{56,40},{64,80... | collective-permute-start | bytes 786440 | tf_op jit(solution)/shard_map/ppermute | solution.py:347
  47.7 2.3 %collective-permute-start.18 = (bf16[256,256]{1,0:T(8,128)(2,1)S(1)}, bf16[256,256]{1,0:T(8,128)(2,1)S(1)}, u32[]{:S(2)}, u32[]{:S(2)}) collective-permute-start(bf16[256,256]{1,0:T(8,128)(2,1)S(1)} %join.1), channel_id=1, source_target_pairs={{0,64},{8,200},{16,80},{24,216},{32,96},{40,232},{48,112},{56,248}... | collective-permute-start | bytes 393224 | tf_op jit(solution)/shard_map/ppermute | solution.py:359
  50.0 2.4 %collective-permute-start.17 = (bf16[256,256]{1,0:T(8,128)(2,1)S(1)}, bf16[256,256]{1,0:T(8,128)(2,1)S(1)}, u32[]{:S(2)}, u32[]{:S(2)}) collective-permute-start(bf16[256,256]{1,0:T(8,128)(2,1)S(1)} %join.1), channel_id=1, source_target_pairs={{0,32},{8,232},{16,48},{24,248},{32,64},{40,8},{48,80},{56,24},{64... | collective-permute-start | bytes 393224 | tf_op jit(solution)/shard_map/ppermute | solution.py:359
  52.4 3.1 %collective-permute-start.16 = (bf16[128,256]{1,0:T(8,128)(2,1)S(1)}, bf16[128,256]{1,0:T(8,128)(2,1)S(1)}, u32[]{:S(2)}, u32[]{:S(2)}) collective-permute-start(bf16[128,256]{1,0:T(8,128)(2,1)S(1)} %get-tuple-element.36.refs_0_.mine.refs_4_), channel_id=1, source_target_pairs={{0,128},{8,136},{16,144},{24,152},{32,160},{40,168},{48,176},{56,1... | collective-permute-start | bytes 196616 | tf_op jit(solution)/shard_map/ppermute | solution.py:355
  55.4 0.5 collective-permute-start.15
  55.9 4.6 %collective-permute-done.16.refs_3_.refs_5_ = bf16[128,256]{1,0:T(8,128)(2,1)S(1)} collective-permute-done((bf16[128,256]{1,0:T(8,128)(2,1)S(1)}, bf16[128,256]{1,0:T(8,128)(2,1)S(1)}, u32[]{:S(2)}, u32[]{:S(2)}) %collective-permute-start.16) | collective-permute-done | bytes 65568 | tf_op jit(solution)/shard_map/ppermute | solution.py:355
  60.5 0.6 sort.1
  61.1 0.1 collective-permute-start.19
  61.2 1.4 %collective-permute-done.19.refs_9_ = bf16[384,256]{1,0:T(8,128)(2,1)S(1)} collective-permute-done((bf16[384,256]{1,0:T(8,128)(2,1)S(1)}, bf16[384,256]{1,0:T(8,128)(2,1)S(1)}, u32[]{:S(2)}, u32[]{:S(2)}) %collective-permute-start.19) | collective-permute-done | bytes 196640 | tf_op jit(solution)/shard_map/ppermute | solution.py:347
  62.7 4.7 %softmax.1 = (bf16[2048,1024]{1,0:T(8,128)(2,1)S(1)}, f32[128,128]{1,0:T(8,128)S(1)}, bf16[1024,128]{1,0:T(8,128)(2,1)S(1)}, bf16[1024,128]{1,0:T(8,128)(2,1)S(1)}) custom-call(s32[2]{0:T(128)S(1)} %pad_add_fusion.ids, s32[64]{0:T(128)S(1)} %copy-done.12, s32[8]{0:T(128)S(1)} %copy-done.13, bf16[256,512]{1,0:T(8,128)(2,1)S(1)} %get-tuple-element.38.refs_0_, ...), custom_call_target="tpu_custom_call" | custom-call | flops 1073741824 | bytes 6291456 | tf_op jit(solution)/shard_map/softmax/pallas_call | solution.py:55
  67.4 0.6 collective-permute-start.21
  68.0 5.3 %collective-permute-done.21.refs_9_ = f32[128,128]{1,0:T(8,128)S(1)} collective-permute-done((f32[128,128]{1,0:T(8,128)S(1)}, f32[128,128]{1,0:T(8,128)S(1)}, u32[]{:S(2)}, u32[]{:S(2)}) %collective-permute-start.21) | collective-permute-done | bytes 65568 | tf_op jit(solution)/shard_map/ppermute | solution.py:347
  73.2 1.2 %collective-permute-done.22.refs_10_ = f32[128,128]{1,0:T(8,128)S(1)} collective-permute-done((f32[128,128]{1,0:T(8,128)S(1)}, f32[128,128]{1,0:T(8,128)S(1)}, u32[]{:S(2)}, u32[]{:S(2)}) %collective-permute-start.22) | collective-permute-done | bytes 65568 | tf_op jit(solution)/shard_map/ppermute | solution.py:347
  74.5 4.1 %gradient.1 = (bf16[256,128]{1,0:T(8,128)(2,1)S(1)}, bf16[256,128]{1,0:T(8,128)(2,1)S(1)}, bf16[3,256,128]{2,1,0:T(8,128)(2,1)S(1)}, bf16[3,256,128]{2,1,0:T(8,1...) custom-call(bf16[256,512]{1,0:T(8,128)(2,1)S(1)} %get-tuple-element.38.refs_0_, ...), custom_call_target="tpu_custom_call" | custom-call | flops 2147483648 | bytes 6291456 | tf_op jit(solution)/shard_map/gradient/pallas_call | solution.py:55
  78.6 0.5 collective-permute-start.29
  79.0 0.4 collective-permute-start.24
  79.4 4.2 %collective-permute-start.23 = (bf16[256,128]{1,0:T(8,128)(2,1)S(1)}, bf16[256,128]{1,0:T(8,128)(2,1)S(1)}, u32[]{:S(2)}, u32[]{:S(2)}) collective-permute-start(bf16[256,128]{1,0:T(8,128)(2,1)S(1)} %get-tuple-element.43), channel_id=1, source_target_pairs={{0,128},{8,136},{16,144},{24,152},{32,160},{40,168},{48,176},{56,1... | collective-permute-start | bytes 196616 | tf_op jit(solution)/shard_map/ppermute | solution.py:355
  83.6 0.6 pair.1
  84.2 2.1 %collective-permute-start.25 = (bf16[2,256,128]{2,1,0:T(8,128)(2,1)S(1)}, bf16[2,256,128]{2,1,0:T(8,128)(2,1)S(1)}, u32[]{:S(2)}, u32[]{:S(2)}) collective-permute-start(bf16[2,256,128]{2,1,0:T(8,128)(2,1)S(1)} %get-tuple-element.46), channel_id=1, source_target_pairs={{0,224},{8,40},{16,240},{24,56},{32,0},{40,72},{48,16},{56,88},{64... | collective-permute-start | bytes 393224 | tf_op jit(solution)/shard_map/ppermute | solution.py:359
  86.3 1.3 %collective-permute-start.26 = (bf16[2,256,128]{2,1,0:T(8,128)(2,1)S(1)}, bf16[2,256,128]{2,1,0:T(8,128)(2,1)S(1)}, u32[]{:S(2)}, u32[]{:S(2)}) collective-permute-start(bf16[2,256,128]{2,1,0:T(8,128)(2,1)S(1)} %get-tuple-element.47), channel_id=1, source_target_pairs={{0,192},{8,72},{16,208},{24,88},{32,224},{40,104},{48,240},{56,120... | collective-permute-start | bytes 393224 | tf_op jit(solution)/shard_map/ppermute | solution.py:359
  87.5 3.5 %collective-permute-start.27 = (bf16[2,256,128]{2,1,0:T(8,128)(2,1)S(1)}, bf16[2,256,128]{2,1,0:T(8,128)(2,1)S(1)}, u32[]{:S(2)}, u32[]{:S(2)}) collective-permute-start(bf16[2,256,128]{2,1,0:T(8,128)(2,1)S(1)} %get-tuple-element.48), channel_id=1, source_target_pairs={{0,160},{8,104},{16,176},{24,120},{32,192},{40,136},{48,208},{56,1... | collective-permute-start | bytes 393224 | tf_op jit(solution)/shard_map/ppermute | solution.py:359
  91.1 0.6 collective-permute-start.30
  91.7 0.6 collective-permute-done.26.refs_2_
  92.2 7.5 %collective-permute-done.27.refs_3_ = bf16[2,256,128]{2,1,0:T(8,128)(2,1)S(1)} collective-permute-done((bf16[2,256,128]{2,1,0:T(8,128)(2,1)S(1)}, bf16[2,256,128]{2,1,0:T(8,128)(2,1)S(1)}, u32[]{:S(2)}, u32[]{:S(2)}) %collective-permute-start.27) | collective-permute-done | bytes 131104 | tf_op jit(solution)/shard_map/ppermute | solution.py:359
  99.7 0.6 sum.1
  100.3 0.2 collective-permute-start.28
  100.6 1.5 %back_query.1.refs_11_ = f32[128,4096]{1,0:T(8,128)S(1)} custom-call(f32[128,512]{1,0:T(8,128)S(1)} %get-tuple-element.54.stay, bf16[128,512]{1,0:T(8,128)(2,1)S(1)} %collective-permute-done.30.got, bf16[4096,512]{1,0:T(8,128)(2,1)S(1)} %copy-done), custom_call_target="tpu_custom_call" | custom-call | flops 536870912 | bytes 6291456 | tf_op jit(solution)/shard_map/back_query/pallas_call | solution.py:55
  102.1 1.5 %back_kv.1 = (f32[128,512]{1,0:T(8,128)S(1)}, bf16[16,256]{1,0:T(8,128)(2,1)S(1)}, bf16[144,512]{1,0:T(8,128)(2,1)S(1)}, bf16[144,512]{1,0:T(8,128)(2,1)S(1)}, b...) custom-call(s32[2]{0:T(128)S(1)} %pad_add_fusion.ids, ...), custom_call_target="tpu_custom_call" | custom-call | flops 268435456 | bytes 7340032 | tf_op jit(solution)/shard_map/back_kv/pallas_call | solution.py:55
  103.6 0.7 collective-permute-start.31
  104.2 1.1 collective-permute-start.32
  105.4 0.4 collective-permute-start.33
  105.8 3.6 %collective-permute-start.34 = (bf16[144,512]{1,0:T(8,128)(2,1)S(1)}, bf16[144,512]{1,0:T(8,128)(2,1)S(1)}, u32[]{:S(2)}, u32[]{:S(2)}) collective-permute-start(bf16[144,512]{1,0:T(8,128)(2,1)S(1)} %get-tuple-element.61), channel_id=1, source_target_pairs={{0,5},{1,4},{2,7},{3,6},{4,1},{5,0},{6,3},{7,2},{8,13},{9,12},{10,... | collective-permute-start | bytes 442376 | tf_op jit(solution)/shard_map/ppermute | solution.py:343
  109.4 1.3 %collective-permute-start.35 = (bf16[144,512]{1,0:T(8,128)(2,1)S(1)}, bf16[144,512]{1,0:T(8,128)(2,1)S(1)}, u32[]{:S(2)}, u32[]{:S(2)}) collective-permute-start(bf16[144,512]{1,0:T(8,128)(2,1)S(1)} %get-tuple-element.62), channel_id=1, source_target_pairs={{0,3},{1,2},{2,1},{3,0},{4,7},{5,6},{6,5},{7,4},{8,11},{9,10},{10,... | collective-permute-start | bytes 442376 | tf_op jit(solution)/shard_map/ppermute | solution.py:343
  110.7 0.1 collective-permute-start.36
  110.8 5.1 %collective-permute-done.32.refs_1_ = bf16[144,512]{1,0:T(8,128)(2,1)S(1)} collective-permute-done((bf16[144,512]{1,0:T(8,128)(2,1)S(1)}, bf16[144,512]{1,0:T(8,128)(2,1)S(1)}, u32[]{:S(2)}, u32[]{:S(2)}) %collective-permute-start.32) | collective-permute-done | bytes 147488 | tf_op jit(solution)/shard_map/ppermute | solution.py:343
  115.9 3.6 %collective-permute-done.33.refs_2_ = bf16[144,512]{1,0:T(8,128)(2,1)S(1)} collective-permute-done((bf16[144,512]{1,0:T(8,128)(2,1)S(1)}, bf16[144,512]{1,0:T(8,128)(2,1)S(1)}, u32[]{:S(2)}, u32[]{:S(2)}) %collective-permute-start.33) | collective-permute-done | bytes 147488 | tf_op jit(solution)/shard_map/ppermute | solution.py:343
  119.6 2.1 %collective-permute-done.36.refs_5_ = bf16[144,512]{1,0:T(8,128)(2,1)S(1)} collective-permute-done((bf16[144,512]{1,0:T(8,128)(2,1)S(1)}, bf16[144,512]{1,0:T(8,128)(2,1)S(1)}, u32[]{:S(2)}, u32[]{:S(2)}) %collective-permute-start.36) | collective-permute-done | bytes 147488 | tf_op jit(solution)/shard_map/ppermute | solution.py:343
  121.6 1.5 %collective-permute-done.37.refs_6_ = bf16[144,512]{1,0:T(8,128)(2,1)S(1)} collective-permute-done((bf16[144,512]{1,0:T(8,128)(2,1)S(1)}, bf16[144,512]{1,0:T(8,128)(2,1)S(1)}, u32[]{:S(2)}, u32[]{:S(2)}) %collective-permute-start.37) | collective-permute-done | bytes 147488 | tf_op jit(solution)/shard_map/ppermute | solution.py:343
  123.2 1.5 %last.1 = (bf16[128,512]{1,0:T(8,128)(2,1)}, f32[1,128]{1,0:T(1,128)}) custom-call(s32[2]{0:T(128)S(1)} %pad_add_fusion.ids, f32[128,512]{1,0:T(8,128)S(1)} %get-tuple-element.56.own, bf16[16,256]{1,0:T(8,128)(2,1)S(1)} %get-tuple-element.57.own_row, bf16[144,512]{1,0:T(8,128)(2,1)S(1)} %collective-permute-done.31.refs_0_, ...), custom_call_target="tpu_custom_call" | custom-call | flops 655360 | bytes 3145728 | tf_op jit(solution)/shard_map/last/pallas_call | solution.py:55
  (56 shorter events, 0.2 us)
Async XLA Ops:
  0.6 8.0 %collective-permute-start.6 = (bf16[128,512]{1,0:T(8,128)(2,1)}, bf16[128,512]{1,0:T(8,128)(2,1)S(1)}, u32[]{:S(2)}, u32[]{:S(2)}) collective-permute-start(bf16[128,512]{1,0:T(8,128)(2,1)} %refs_7_.1), channel_id=1, source_target_pairs={{0,1},{1,0},{2,3},{3,2},{4,5},{5,4},{6,7},{7,6},{8,9},{9,8},{10,11... | collective-permute-start | bytes 393224 | tf_op jit(solution)/shard_map/ppermute | solution.py:343
  2.2 9.5 %collective-permute-start.5 = (bf16[128,512]{1,0:T(8,128)(2,1)}, bf16[128,512]{1,0:T(8,128)(2,1)S(1)}, u32[]{:S(2)}, u32[]{:S(2)}) collective-permute-start(bf16[128,512]{1,0:T(8,128)(2,1)} %refs_7_.1), channel_id=1, source_target_pairs={{0,2},{1,3},{2,0},{3,1},{4,6},{5,7},{6,4},{7,5},{8,10},{9,11},{10,... | collective-permute-start | bytes 393224 | tf_op jit(solution)/shard_map/ppermute | solution.py:343
  3.8 16.3 %collective-permute-start.4 = (bf16[128,512]{1,0:T(8,128)(2,1)}, bf16[128,512]{1,0:T(8,128)(2,1)S(1)}, u32[]{:S(2)}, u32[]{:S(2)}) collective-permute-start(bf16[128,512]{1,0:T(8,128)(2,1)} %refs_7_.1), channel_id=1, source_target_pairs={{0,4},{1,5},{2,6},{3,7},{4,0},{5,1},{6,2},{7,3},{8,12},{9,13},{10,... | collective-permute-start | bytes 393224 | tf_op jit(solution)/shard_map/ppermute | solution.py:343
  6.7 15.0 %collective-permute-start.3 = (bf16[128,512]{1,0:T(8,128)(2,1)}, bf16[128,512]{1,0:T(8,128)(2,1)S(1)}, u32[]{:S(2)}, u32[]{:S(2)}) collective-permute-start(bf16[128,512]{1,0:T(8,128)(2,1)} %refs_7_.1), channel_id=1, source_target_pairs={{0,5},{1,4},{2,7},{3,6},{4,1},{5,0},{6,3},{7,2},{8,13},{9,12},{10,... | collective-permute-start | bytes 393224 | tf_op jit(solution)/shard_map/ppermute | solution.py:343
  7.3 14.4 %collective-permute-start.2 = (bf16[128,512]{1,0:T(8,128)(2,1)}, bf16[128,512]{1,0:T(8,128)(2,1)S(1)}, u32[]{:S(2)}, u32[]{:S(2)}) collective-permute-start(bf16[128,512]{1,0:T(8,128)(2,1)} %refs_7_.1), channel_id=1, source_target_pairs={{0,3},{1,2},{2,1},{3,0},{4,7},{5,6},{6,5},{7,4},{8,11},{9,10},{10,... | collective-permute-start | bytes 393224 | tf_op jit(solution)/shard_map/ppermute | solution.py:343
  8.7 13.0 %collective-permute-start.1 = (bf16[128,512]{1,0:T(8,128)(2,1)}, bf16[128,512]{1,0:T(8,128)(2,1)S(1)}, u32[]{:S(2)}, u32[]{:S(2)}) collective-permute-start(bf16[128,512]{1,0:T(8,128)(2,1)} %refs_7_.1), channel_id=1, source_target_pairs={{0,6},{1,7},{2,4},{3,5},{4,2},{5,3},{6,0},{7,1},{8,14},{9,15},{10,... | collective-permute-start | bytes 393224 | tf_op jit(solution)/shard_map/ppermute | solution.py:343
  11.7 10.0 %collective-permute-start = (bf16[128,512]{1,0:T(8,128)(2,1)}, bf16[128,512]{1,0:T(8,128)(2,1)S(1)}, u32[]{:S(2)}, u32[]{:S(2)}) collective-permute-start(bf16[128,512]{1,0:T(8,128)(2,1)} %refs_7_.1), channel_id=1, source_target_pairs={{0,7},{1,6},{2,5},{3,4},{4,3},{5,2},{6,1},{7,0},{8,15},{9,14},{10,... | collective-permute-start | bytes 393224 | tf_op jit(solution)/shard_map/ppermute | solution.py:343
  15.7 21.6 %copy-start = (bf16[4096,512]{1,0:T(8,128)(2,1)S(1)}, bf16[4096,512]{1,0:T(8,128)(2,1)}, u32[]{:S(2)}) copy-start(bf16[4096,512]{1,0:T(8,128)(2,1)} %w_query.1) | copy-start | bytes 12582916
  15.7 1.4 %copy-start.3 = (bf16[4096,128]{1,0:T(8,128)(2,1)S(1)}, bf16[4096,128]{1,0:T(8,128)(2,1)}, u32[]{:S(2)}) copy-start(bf16[4096,128]{1,0:T(8,128)(2,1)} %refs_12_.3) | copy-start | bytes 3145732
  17.1 1.4 %copy-start.5 = (bf16[4096,128]{1,0:T(8,128)(2,1)S(1)}, bf16[4096,128]{1,0:T(8,128)(2,1)}, u32[]{:S(2)}) copy-start(bf16[4096,128]{1,0:T(8,128)(2,1)} %refs_13_.1) | copy-start | bytes 3145732
  18.5 0.9 copy-start.7
  19.4 0.7 copy-start.10
  20.1 5.2 %copy-start.9 = (bf16[128,512]{1,0:T(8,128)(2,1)S(1)}, bf16[128,512]{1,0:T(8,128)(2,1)}, u32[]{:S(2)}) copy-start(bf16[128,512]{1,0:T(8,128)(2,1)} %refs_8_.1) | copy-start | bytes 393220
  20.1 5.2 %collective-permute-start.7 = (bf16[128,512]{1,0:T(8,128)(2,1)}, bf16[128,512]{1,0:T(8,128)(2,1)S(1)}, u32[]{:S(2)}, u32[]{:S(2)}) collective-permute-start(bf16[128,512]{1,0:T(8,128)(2,1)} %refs_8_.1), channel_id=1, source_target_pairs={{0,1},{1,0},{2,3},{3,2},{4,5},{5,4},{6,7},{7,6},{8,9},{9,8},{10,11... | collective-permute-start | bytes 393224 | tf_op jit(solution)/shard_map/ppermute | solution.py:343
  25.3 16.4 %collective-permute-start.10 = (bf16[256,512]{1,0:T(8,128)(2,1)S(1)}, bf16[256,512]{1,0:T(8,128)(2,1)S(1)}, u32[]{:S(2)}, u32[]{:S(2)}) collective-permute-start(bf16[256,512]{1,0:T(8,128)(2,1)S(1)} %hold.1.refs_8_), channel_id=1, source_target_pairs={{0,6},{1,7},{2,4},{3,5},{4,2},{5,3},{6,0},{7,1},{8,14},{9,15},{10,... | collective-permute-start | bytes 786440 | tf_op jit(solution)/shard_map/ppermute | solution.py:343
  25.4 16.3 %collective-permute-start.9 = (bf16[256,512]{1,0:T(8,128)(2,1)S(1)}, bf16[256,512]{1,0:T(8,128)(2,1)S(1)}, u32[]{:S(2)}, u32[]{:S(2)}) collective-permute-start(bf16[256,512]{1,0:T(8,128)(2,1)S(1)} %hold.1.refs_8_), channel_id=1, source_target_pairs={{0,4},{1,5},{2,6},{3,7},{4,0},{5,1},{6,2},{7,3},{8,12},{9,13},{10,... | collective-permute-start | bytes 786440 | tf_op jit(solution)/shard_map/ppermute | solution.py:343
  28.1 13.6 %collective-permute-start.8 = (bf16[256,512]{1,0:T(8,128)(2,1)S(1)}, bf16[256,512]{1,0:T(8,128)(2,1)S(1)}, u32[]{:S(2)}, u32[]{:S(2)}) collective-permute-start(bf16[256,512]{1,0:T(8,128)(2,1)S(1)} %hold.1.refs_8_), channel_id=1, source_target_pairs={{0,2},{1,3},{2,0},{3,1},{4,6},{5,7},{6,4},{7,5},{8,10},{9,11},{10,... | collective-permute-start | bytes 786440 | tf_op jit(solution)/shard_map/ppermute | solution.py:343
  29.5 1.3 %collective-permute-start.11 = (bf16[128,256]{1,0:T(8,128)(2,1)S(1)}, bf16[128,256]{1,0:T(8,128)(2,1)S(1)}, u32[]{:S(2)}, u32[]{:S(2)}) collective-permute-start(bf16[128,256]{1,0:T(8,128)(2,1)S(1)} %get-tuple-element.36.refs_0_.mine.refs_4_), channel_id=1, source_target_pairs={{0,8},{8,0},{16,24},{24,16},{32,40},{40,32},{48,56},{56,48},{64,72... | collective-permute-start | bytes 196616 | tf_op jit(solution)/shard_map/ppermute | solution.py:347
  31.3 10.4 %collective-permute-start.12 = (bf16[256,256]{1,0:T(8,128)(2,1)S(1)}, bf16[256,256]{1,0:T(8,128)(2,1)S(1)}, u32[]{:S(2)}, u32[]{:S(2)}) collective-permute-start(bf16[256,256]{1,0:T(8,128)(2,1)S(1)} %join.1), channel_id=1, source_target_pairs={{0,96},{8,168},{16,112},{24,184},{32,128},{40,200},{48,144},{56,21... | collective-permute-start | bytes 393224 | tf_op jit(solution)/shard_map/ppermute | solution.py:359
  37.2 2.2 %copy-start.1 = (bf16[512,4096]{1,0:T(8,128)(2,1)S(1)}, bf16[512,4096]{1,0:T(8,128)(2,1)}, u32[]{:S(2)}) copy-start(bf16[512,4096]{1,0:T(8,128)(2,1)} %refs_12_.2) | copy-start | bytes 12582916
  39.4 2.3 %copy-start.2 = (bf16[512,4096]{1,0:T(8,128)(2,1)S(1)}, bf16[512,4096]{1,0:T(8,128)(2,1)}, u32[]{:S(2)}) copy-start(bf16[512,4096]{1,0:T(8,128)(2,1)} %refs_12_.2) | copy-start | bytes 12582916
  39.4 2.3 %copy-start.8 = (bf16[128,512]{1,0:T(8,128)(2,1)S(1)}, bf16[128,512]{1,0:T(8,128)(2,1)}, u32[]{:S(2)}) copy-start(bf16[128,512]{1,0:T(8,128)(2,1)} %refs_7_.1) | copy-start | bytes 393220
  39.4 23.2 %copy-start.12 = (s32[64]{0:T(128)S(1)}, s32[64]{0:T(128)}, u32[]{:S(2)}) copy-start(s32[64]{0:T(128)} %order.1) | copy-start | bytes 772
  39.4 23.2 %copy-start.13 = (s32[8]{0:T(128)S(1)}, s32[8]{0:T(128)}, u32[]{:S(2)}) copy-start(s32[8]{0:T(128)} %lengths.1) | copy-start | bytes 100
  44.5 10.9 %collective-permute-start.14 = (bf16[256,512]{1,0:T(8,128)(2,1)S(1)}, bf16[256,512]{1,0:T(8,128)(2,1)S(1)}, u32[]{:S(2)}, u32[]{:S(2)}) collective-permute-start(bf16[256,512]{1,0:T(8,128)(2,1)S(1)} %get-tuple-element.38.refs_0_), channel_id=1, source_target_pairs={{0,16},{8,24},{16,0},{24,8},{32,48},{40,56},{48,32},{56,40},{64,80... | collective-permute-start | bytes 786440 | tf_op jit(solution)/shard_map/ppermute | solution.py:347
  47.7 12.9 %collective-permute-start.18 = (bf16[256,256]{1,0:T(8,128)(2,1)S(1)}, bf16[256,256]{1,0:T(8,128)(2,1)S(1)}, u32[]{:S(2)}, u32[]{:S(2)}) collective-permute-start(bf16[256,256]{1,0:T(8,128)(2,1)S(1)} %join.1), channel_id=1, source_target_pairs={{0,64},{8,200},{16,80},{24,216},{32,96},{40,232},{48,112},{56,248}... | collective-permute-start | bytes 393224 | tf_op jit(solution)/shard_map/ppermute | solution.py:359
  50.0 10.6 %collective-permute-start.17 = (bf16[256,256]{1,0:T(8,128)(2,1)S(1)}, bf16[256,256]{1,0:T(8,128)(2,1)S(1)}, u32[]{:S(2)}, u32[]{:S(2)}) collective-permute-start(bf16[256,256]{1,0:T(8,128)(2,1)S(1)} %join.1), channel_id=1, source_target_pairs={{0,32},{8,232},{16,48},{24,248},{32,64},{40,8},{48,80},{56,24},{64... | collective-permute-start | bytes 393224 | tf_op jit(solution)/shard_map/ppermute | solution.py:359
  52.4 8.2 %collective-permute-start.16 = (bf16[128,256]{1,0:T(8,128)(2,1)S(1)}, bf16[128,256]{1,0:T(8,128)(2,1)S(1)}, u32[]{:S(2)}, u32[]{:S(2)}) collective-permute-start(bf16[128,256]{1,0:T(8,128)(2,1)S(1)} %get-tuple-element.36.refs_0_.mine.refs_4_), channel_id=1, source_target_pairs={{0,128},{8,136},{16,144},{24,152},{32,160},{40,168},{48,176},{56,1... | collective-permute-start | bytes 196616 | tf_op jit(solution)/shard_map/ppermute | solution.py:355
  55.4 7.2 %collective-permute-start.13 = (bf16[256,512]{1,0:T(8,128)(2,1)S(1)}, bf16[256,512]{1,0:T(8,128)(2,1)S(1)}, u32[]{:S(2)}, u32[]{:S(2)}) collective-permute-start(bf16[256,512]{1,0:T(8,128)(2,1)S(1)} %get-tuple-element.38.refs_0_), channel_id=1, source_target_pairs={{0,8},{8,0},{16,24},{24,16},{32,40},{40,32},{48,56},{56,48},{64,72... | collective-permute-start | bytes 786440 | tf_op jit(solution)/shard_map/ppermute | solution.py:347
  55.4 7.2 %collective-permute-start.15 = (bf16[256,512]{1,0:T(8,128)(2,1)S(1)}, bf16[256,512]{1,0:T(8,128)(2,1)S(1)}, u32[]{:S(2)}, u32[]{:S(2)}) collective-permute-start(bf16[256,512]{1,0:T(8,128)(2,1)S(1)} %collective-permute-done.14.refs_2_), channel_id=1, source_target_pairs={{0,8},{8,0},{16,24},{24,16},{32,40},{40,32},{48,56},{56,48},{64,72... | collective-permute-start | bytes 786440 | tf_op jit(solution)/shard_map/ppermute | solution.py:347
  61.1 1.5 %collective-permute-start.19 = (bf16[384,256]{1,0:T(8,128)(2,1)S(1)}, bf16[384,256]{1,0:T(8,128)(2,1)S(1)}, u32[]{:S(2)}, u32[]{:S(2)}) collective-permute-start(bf16[384,256]{1,0:T(8,128)(2,1)S(1)} %sort.1), channel_id=1, source_target_pairs={{0,8},{8,0},{16,24},{24,16},{32,40},{40,32},{48,56},{56,48},{64,72... | collective-permute-start | bytes 589832 | tf_op jit(solution)/shard_map/ppermute | solution.py:347
  67.4 5.8 %collective-permute-start.21 = (f32[128,128]{1,0:T(8,128)S(1)}, f32[128,128]{1,0:T(8,128)S(1)}, u32[]{:S(2)}, u32[]{:S(2)}) collective-permute-start(f32[128,128]{1,0:T(8,128)S(1)} %get-tuple-element.42.refs_7_), channel_id=1, source_target_pairs={{0,16},{8,24},{16,0},{24,8},{32,48},{40,56},{48,32},{56,40},{64,80... | collective-permute-start | bytes 196616 | tf_op jit(solution)/shard_map/ppermute | solution.py:347
  68.0 5.3 %collective-permute-start.20 = (f32[128,128]{1,0:T(8,128)S(1)}, f32[128,128]{1,0:T(8,128)S(1)}, u32[]{:S(2)}, u32[]{:S(2)}) collective-permute-start(f32[128,128]{1,0:T(8,128)S(1)} %get-tuple-element.42.refs_7_), channel_id=1, source_target_pairs={{0,8},{8,0},{16,24},{24,16},{32,40},{40,32},{48,56},{56,48},{64,72... | collective-permute-start | bytes 196616 | tf_op jit(solution)/shard_map/ppermute | solution.py:347
  73.2 1.3 %collective-permute-start.22 = (f32[128,128]{1,0:T(8,128)S(1)}, f32[128,128]{1,0:T(8,128)S(1)}, u32[]{:S(2)}, u32[]{:S(2)}) collective-permute-start(f32[128,128]{1,0:T(8,128)S(1)} %collective-permute-done.21.refs_9_), channel_id=1, source_target_pairs={{0,8},{8,0},{16,24},{24,16},{32,40},{40,32},{48,56},{56,48},{64,72... | collective-permute-start | bytes 196616 | tf_op jit(solution)/shard_map/ppermute | solution.py:347
  78.6 12.4 %collective-permute-start.29 = (bf16[256,512]{1,0:T(8,128)(2,1)S(1)}, bf16[256,512]{1,0:T(8,128)(2,1)S(1)}, u32[]{:S(2)}, u32[]{:S(2)}) collective-permute-start(bf16[256,512]{1,0:T(8,128)(2,1)S(1)} %get-tuple-element.53), channel_id=1, source_target_pairs={{0,8},{8,0},{16,24},{24,16},{32,40},{40,32},{48,56},{56,48},{64,72... | collective-permute-start | bytes 786440 | tf_op jit(solution)/shard_map/ppermute | solution.py:347
  79.0 4.6 %collective-permute-start.24 = (bf16[3,256,128]{2,1,0:T(8,128)(2,1)S(1)}, bf16[3,256,128]{2,1,0:T(8,128)(2,1)S(1)}, u32[]{:S(2)}, u32[]{:S(2)}) collective-permute-start(bf16[3,256,128]{2,1,0:T(8,128)(2,1)S(1)} %get-tuple-element.45), channel_id=1, source_target_pairs={{0,8},{8,0},{16,24},{24,16},{32,40},{40,32},{48,56},{56,48},{64,72... | collective-permute-start | bytes 589832 | tf_op jit(solution)/shard_map/ppermute | solution.py:347
  79.4 11.6 %collective-permute-start.23 = (bf16[256,128]{1,0:T(8,128)(2,1)S(1)}, bf16[256,128]{1,0:T(8,128)(2,1)S(1)}, u32[]{:S(2)}, u32[]{:S(2)}) collective-permute-start(bf16[256,128]{1,0:T(8,128)(2,1)S(1)} %get-tuple-element.43), channel_id=1, source_target_pairs={{0,128},{8,136},{16,144},{24,152},{32,160},{40,168},{48,176},{56,1... | collective-permute-start | bytes 196616 | tf_op jit(solution)/shard_map/ppermute | solution.py:355
  83.6 18.5 %copy-start.4 = (bf16[4096,128]{1,0:T(8,128)(2,1)S(1)}, bf16[4096,128]{1,0:T(8,128)(2,1)}, u32[]{:S(2)}) copy-start(bf16[4096,128]{1,0:T(8,128)(2,1)} %refs_12_.3) | copy-start | bytes 3145732
  83.6 18.5 %copy-start.6 = (bf16[4096,128]{1,0:T(8,128)(2,1)S(1)}, bf16[4096,128]{1,0:T(8,128)(2,1)}, u32[]{:S(2)}) copy-start(bf16[4096,128]{1,0:T(8,128)(2,1)} %refs_13_.1) | copy-start | bytes 3145732
  83.6 18.5 %copy-start.11 = (f32[4096]{0:T(1024)S(1)}, f32[4096]{0:T(1024)}, u32[]{:S(2)}) copy-start(f32[4096]{0:T(1024)} %param.11) | copy-start | bytes 49156
  84.2 7.5 %collective-permute-start.25 = (bf16[2,256,128]{2,1,0:T(8,128)(2,1)S(1)}, bf16[2,256,128]{2,1,0:T(8,128)(2,1)S(1)}, u32[]{:S(2)}, u32[]{:S(2)}) collective-permute-start(bf16[2,256,128]{2,1,0:T(8,128)(2,1)S(1)} %get-tuple-element.46), channel_id=1, source_target_pairs={{0,224},{8,40},{16,240},{24,56},{32,0},{40,72},{48,16},{56,88},{64... | collective-permute-start | bytes 393224 | tf_op jit(solution)/shard_map/ppermute | solution.py:359
  86.3 6.0 %collective-permute-start.26 = (bf16[2,256,128]{2,1,0:T(8,128)(2,1)S(1)}, bf16[2,256,128]{2,1,0:T(8,128)(2,1)S(1)}, u32[]{:S(2)}, u32[]{:S(2)}) collective-permute-start(bf16[2,256,128]{2,1,0:T(8,128)(2,1)S(1)} %get-tuple-element.47), channel_id=1, source_target_pairs={{0,192},{8,72},{16,208},{24,88},{32,224},{40,104},{48,240},{56,120... | collective-permute-start | bytes 393224 | tf_op jit(solution)/shard_map/ppermute | solution.py:359
  87.5 12.2 %collective-permute-start.27 = (bf16[2,256,128]{2,1,0:T(8,128)(2,1)S(1)}, bf16[2,256,128]{2,1,0:T(8,128)(2,1)S(1)}, u32[]{:S(2)}, u32[]{:S(2)}) collective-permute-start(bf16[2,256,128]{2,1,0:T(8,128)(2,1)S(1)} %get-tuple-element.48), channel_id=1, source_target_pairs={{0,160},{8,104},{16,176},{24,120},{32,192},{40,136},{48,208},{56,1... | collective-permute-start | bytes 393224 | tf_op jit(solution)/shard_map/ppermute | solution.py:359
  91.1 9.5 %collective-permute-start.30 = (bf16[128,512]{1,0:T(8,128)(2,1)S(1)}, bf16[128,512]{1,0:T(8,128)(2,1)S(1)}, u32[]{:S(2)}, u32[]{:S(2)}) collective-permute-start(bf16[128,512]{1,0:T(8,128)(2,1)S(1)} %get-tuple-element.55), channel_id=1, source_target_pairs={{0,16},{8,24},{16,0},{24,8},{32,48},{40,56},{48,32},{56,40},{64,80... | collective-permute-start | bytes 393224 | tf_op jit(solution)/shard_map/ppermute | solution.py:347
  100.3 1.7 %collective-permute-start.28 = (bf16[256,128]{1,0:T(8,128)(2,1)S(1)}, bf16[256,128]{1,0:T(8,128)(2,1)S(1)}, u32[]{:S(2)}, u32[]{:S(2)}) collective-permute-start(bf16[256,128]{1,0:T(8,128)(2,1)S(1)} %get-tuple-element.51), channel_id=1, source_target_pairs={{0,8},{8,0},{16,24},{24,16},{32,40},{40,32},{48,56},{56,48},{64,72... | collective-permute-start | bytes 196616 | tf_op jit(solution)/shard_map/ppermute | solution.py:347
  103.6 7.1 %collective-permute-start.31 = (bf16[144,512]{1,0:T(8,128)(2,1)S(1)}, bf16[144,512]{1,0:T(8,128)(2,1)S(1)}, u32[]{:S(2)}, u32[]{:S(2)}) collective-permute-start(bf16[144,512]{1,0:T(8,128)(2,1)S(1)} %get-tuple-element.58), channel_id=1, source_target_pairs={{0,1},{1,0},{2,3},{3,2},{4,5},{5,4},{6,7},{7,6},{8,9},{9,8},{10,11... | collective-permute-start | bytes 442376 | tf_op jit(solution)/shard_map/ppermute | solution.py:343
  104.2 11.7 %collective-permute-start.32 = (bf16[144,512]{1,0:T(8,128)(2,1)S(1)}, bf16[144,512]{1,0:T(8,128)(2,1)S(1)}, u32[]{:S(2)}, u32[]{:S(2)}) collective-permute-start(bf16[144,512]{1,0:T(8,128)(2,1)S(1)} %get-tuple-element.59), channel_id=1, source_target_pairs={{0,2},{1,3},{2,0},{3,1},{4,6},{5,7},{6,4},{7,5},{8,10},{9,11},{10,... | collective-permute-start | bytes 442376 | tf_op jit(solution)/shard_map/ppermute | solution.py:343
  105.4 14.2 %collective-permute-start.33 = (bf16[144,512]{1,0:T(8,128)(2,1)S(1)}, bf16[144,512]{1,0:T(8,128)(2,1)S(1)}, u32[]{:S(2)}, u32[]{:S(2)}) collective-permute-start(bf16[144,512]{1,0:T(8,128)(2,1)S(1)} %get-tuple-element.60), channel_id=1, source_target_pairs={{0,4},{1,5},{2,6},{3,7},{4,0},{5,1},{6,2},{7,3},{8,12},{9,13},{10,... | collective-permute-start | bytes 442376 | tf_op jit(solution)/shard_map/ppermute | solution.py:343
  105.8 13.8 %collective-permute-start.34 = (bf16[144,512]{1,0:T(8,128)(2,1)S(1)}, bf16[144,512]{1,0:T(8,128)(2,1)S(1)}, u32[]{:S(2)}, u32[]{:S(2)}) collective-permute-start(bf16[144,512]{1,0:T(8,128)(2,1)S(1)} %get-tuple-element.61), channel_id=1, source_target_pairs={{0,5},{1,4},{2,7},{3,6},{4,1},{5,0},{6,3},{7,2},{8,13},{9,12},{10,... | collective-permute-start | bytes 442376 | tf_op jit(solution)/shard_map/ppermute | solution.py:343
  109.4 10.2 %collective-permute-start.35 = (bf16[144,512]{1,0:T(8,128)(2,1)S(1)}, bf16[144,512]{1,0:T(8,128)(2,1)S(1)}, u32[]{:S(2)}, u32[]{:S(2)}) collective-permute-start(bf16[144,512]{1,0:T(8,128)(2,1)S(1)} %get-tuple-element.62), channel_id=1, source_target_pairs={{0,3},{1,2},{2,1},{3,0},{4,7},{5,6},{6,5},{7,4},{8,11},{9,10},{10,... | collective-permute-start | bytes 442376 | tf_op jit(solution)/shard_map/ppermute | solution.py:343
  110.7 10.9 %collective-permute-start.36 = (bf16[144,512]{1,0:T(8,128)(2,1)S(1)}, bf16[144,512]{1,0:T(8,128)(2,1)S(1)}, u32[]{:S(2)}, u32[]{:S(2)}) collective-permute-start(bf16[144,512]{1,0:T(8,128)(2,1)S(1)} %get-tuple-element.63), channel_id=1, source_target_pairs={{0,6},{1,7},{2,4},{3,5},{4,2},{5,3},{6,0},{7,1},{8,14},{9,15},{10,... | collective-permute-start | bytes 442376 | tf_op jit(solution)/shard_map/ppermute | solution.py:343
  115.9 7.3 %collective-permute-start.37 = (bf16[144,512]{1,0:T(8,128)(2,1)S(1)}, bf16[144,512]{1,0:T(8,128)(2,1)S(1)}, u32[]{:S(2)}, u32[]{:S(2)}) collective-permute-start(bf16[144,512]{1,0:T(8,128)(2,1)S(1)} %get-tuple-element.64), channel_id=1, source_target_pairs={{0,7},{1,6},{2,5},{3,4},{4,3},{5,2},{6,1},{7,0},{8,15},{9,14},{10,... | collective-permute-start | bytes 442376 | tf_op jit(solution)/shard_map/ppermute | solution.py:343

commit v4 on v2

--- a/solution.py
+++ b/solution.py
@@ -82,6 +82,10 @@
 
 def touch_kernel(*refs):
     refs[-1][...] = jnp.zeros((8, ROWS), f32)
+
+
+def copy_kernel(x, out):
+    out[...] = x[...]
 
 
 def hold_kernel(own, other, *refs):
@@ -389,10 +393,11 @@
     kvs = [kv, turn(kv, RING // 2), *near]
     given = call(sort_kernel, [ids], [*near, kvs[1]], shape((SIDE * ROWS, WIDE), bf16), 4, moved=1 << 19, name="sort")
     kvs.append(xor_ctx(given, 1))
+    grad = call(copy_kernel, [], [out_grad], shape((ROWS, SHARE), bf16), 4, moved=1 << 18, name="copy")
     held = call(
         hold_kernel,
         [],
-        [out_grad, xor_head(out_grad, 1), kv],
+        [grad, xor_head(grad, 1), kv],
         shape((2 * ROWS, SHARE), bf16),
         4,
         moved=1 << 19,

time: 123 us -> 123 us (level)
    unnamed x28 -> x30, local copies, waits for them, and re-layouts: 6.64 us -> 7.53 us
    pallas_call x15 -> x16, Pallas kernels: 20.2 us -> 20.2 us  [call(): pl.pallas_call(body, out_shape=outs, in_specs=smem(len(scalars)) + vmem(l...]
where the time goes in v4:
time: 123 us
  starting transfers between devices  55.4 us (45%)
  waiting for transfers between devices  39 us (32%)
  Pallas kernels  20.2 us (16%)
  local copies, waits for them, and re-layouts  7.53 us (6%)
    ppermute x18, starting transfers between devices, xor_head(): return lax.ppermute(a, 'head', [(i, i ^ k) for i in range(GROUPS)])  31.8 us
    pallas_call x16, Pallas kernels, call(): pl.pallas_call(body, out_shape=outs, in_specs=smem(len(scalars)) + vmem(l...  20.2 us
    ppermute x6, starting transfers between devices, apart(): lax.ppermute(a, 'ctx', [(i, (i + 4 * k * (1 - 2 * (i % 2))) % 32) for i i...  13.2 us
    ppermute x6, waiting for transfers between devices, apart(): lax.ppermute(a, 'ctx', [(i, (i + 4 * k * (1 - 2 * (i % 2))) % 32) for i i...  11.6 us
    ppermute x12, waiting for transfers between devices, xor_ctx(): return lax.ppermute(a, 'ctx', [(i, i ^ k) for i in range(32)])  10.7 us
    ppermute x18, waiting for transfers between devices, xor_head(): return lax.ppermute(a, 'head', [(i, i ^ k) for i in range(GROUPS)])  9.85 us
    unnamed x30, local copies, waits for them, and re-layouts  7.53 us
    ppermute x2, waiting for transfers between devices, turn(): return lax.ppermute(a, 'ctx', [(i, (i + 4 * k) % 32) for i in range(32)])  6.82 us
  transfers between devices with their start and end apart: 38, of which 15 were waited for; matrix products, arithmetic and copies ran while one was open for 0% of the time, Pallas kernels for 5%

profile of v4, /device:TPU:32, one launch (start us, length us, event | category | flops | bytes accessed | tf_op | source)
XLA Modules:
  0.0 123.2 jit_solution(5936740061303402373)
XLA Ops:
  0.6 1.6 %collective-permute-start.6 = (bf16[128,512]{1,0:T(8,128)(2,1)}, bf16[128,512]{1,0:T(8,128)(2,1)S(1)}, u32[]{:S(2)}, u32[]{:S(2)}) collective-permute-start(bf16[128,512]{1,0:T(8,128)(2,1)} %refs_7_.1), channel_id=1, source_target_pairs={{0,1},{1,0},{2,3},{3,2},{4,5},{5,4},{6,7},{7,6},{8,9},{9,8},{10,11... | collective-permute-start | bytes 393224 | tf_op jit(solution)/shard_map/ppermute | solution.py:347
  2.2 1.6 %collective-permute-start.5 = (bf16[128,512]{1,0:T(8,128)(2,1)}, bf16[128,512]{1,0:T(8,128)(2,1)S(1)}, u32[]{:S(2)}, u32[]{:S(2)}) collective-permute-start(bf16[128,512]{1,0:T(8,128)(2,1)} %refs_7_.1), channel_id=1, source_target_pairs={{0,2},{1,3},{2,0},{3,1},{4,6},{5,7},{6,4},{7,5},{8,10},{9,11},{10,... | collective-permute-start | bytes 393224 | tf_op jit(solution)/shard_map/ppermute | solution.py:347
  3.8 2.9 %collective-permute-start.4 = (bf16[128,512]{1,0:T(8,128)(2,1)}, bf16[128,512]{1,0:T(8,128)(2,1)S(1)}, u32[]{:S(2)}, u32[]{:S(2)}) collective-permute-start(bf16[128,512]{1,0:T(8,128)(2,1)} %refs_7_.1), channel_id=1, source_target_pairs={{0,4},{1,5},{2,6},{3,7},{4,0},{5,1},{6,2},{7,3},{8,12},{9,13},{10,... | collective-permute-start | bytes 393224 | tf_op jit(solution)/shard_map/ppermute | solution.py:347
  6.7 0.6 collective-permute-start.3
  7.3 1.4 %collective-permute-start.2 = (bf16[128,512]{1,0:T(8,128)(2,1)}, bf16[128,512]{1,0:T(8,128)(2,1)S(1)}, u32[]{:S(2)}, u32[]{:S(2)}) collective-permute-start(bf16[128,512]{1,0:T(8,128)(2,1)} %refs_7_.1), channel_id=1, source_target_pairs={{0,3},{1,2},{2,1},{3,0},{4,7},{5,6},{6,5},{7,4},{8,11},{9,10},{10,... | collective-permute-start | bytes 393224 | tf_op jit(solution)/shard_map/ppermute | solution.py:347
  8.7 3.0 %collective-permute-start.1 = (bf16[128,512]{1,0:T(8,128)(2,1)}, bf16[128,512]{1,0:T(8,128)(2,1)S(1)}, u32[]{:S(2)}, u32[]{:S(2)}) collective-permute-start(bf16[128,512]{1,0:T(8,128)(2,1)} %refs_7_.1), channel_id=1, source_target_pairs={{0,6},{1,7},{2,4},{3,5},{4,2},{5,3},{6,0},{7,1},{8,14},{9,15},{10,... | collective-permute-start | bytes 393224 | tf_op jit(solution)/shard_map/ppermute | solution.py:347
  11.7 4.0 %collective-permute-start = (bf16[128,512]{1,0:T(8,128)(2,1)}, bf16[128,512]{1,0:T(8,128)(2,1)S(1)}, u32[]{:S(2)}, u32[]{:S(2)}) collective-permute-start(bf16[128,512]{1,0:T(8,128)(2,1)} %refs_7_.1), channel_id=1, source_target_pairs={{0,7},{1,6},{2,5},{3,4},{4,3},{5,2},{6,1},{7,0},{8,15},{9,14},{10,... | collective-permute-start | bytes 393224 | tf_op jit(solution)/shard_map/ppermute | solution.py:347
  15.7 0.9 copy-done.9
  16.6 1.4 %copy-done.3 = bf16[4096,128]{1,0:T(8,128)(2,1)S(1)} copy-done((bf16[4096,128]{1,0:T(8,128)(2,1)S(1)}, bf16[4096,128]{1,0:T(8,128)(2,1)}, u32[]{:S(2)}) %copy-start.3) | copy-done | bytes 1048600
  18.0 1.4 %copy-done.5 = bf16[4096,128]{1,0:T(8,128)(2,1)S(1)} copy-done((bf16[4096,128]{1,0:T(8,128)(2,1)S(1)}, bf16[4096,128]{1,0:T(8,128)(2,1)}, u32[]{:S(2)}) %copy-start.5) | copy-done | bytes 1048600
  19.4 0.9 copy-done.7
  20.3 0.7 copy-done.11
  21.0 1.5 %collective-permute-start.7 = (bf16[128,512]{1,0:T(8,128)(2,1)S(1)}, bf16[128,512]{1,0:T(8,128)(2,1)S(1)}, u32[]{:S(2)}, u32[]{:S(2)}) collective-permute-start(bf16[128,512]{1,0:T(8,128)(2,1)S(1)} %copy.12.own), channel_id=1, source_target_pairs={{0,1},{1,0},{2,3},{3,2},{4,5},{5,4},{6,7},{7,6},{8,9},{9,8},{10,11... | collective-permute-start | bytes 393224 | tf_op jit(solution)/shard_map/ppermute | solution.py:347
  22.6 1.8 %norm_kv.1 = (bf16[128,256]{1,0:T(8,128)(2,1)S(1)}, bf16[128,4096]{1,0:T(8,128)(2,1)S(1)}, f32[128,128]{1,0:T(8,128)S(1)}, f32[8,128]{1,0:T(8,128)S(1)}) custom-call(s32[2]{0:T(128)S(1)} %pad_add_fusion.ids, bf16[128,512]{1,0:T(8,128)(2,1)S(1)} %copy-done.7, bf16[128,512]{1,0:T(8,128)(2,1)S(1)} %collective-permute-done.refs_1_.refs_3_, ...), custom_call_target="tpu_custom_call" | custom-call | flops 268435456 | bytes 5242880 | tf_op jit(solution)/shard_map/norm_kv/pallas_call | solution.py:55
  24.4 1.5 %collective-permute-done.7.other = bf16[128,512]{1,0:T(8,128)(2,1)S(1)} collective-permute-done((bf16[128,512]{1,0:T(8,128)(2,1)S(1)}, bf16[128,512]{1,0:T(8,128)(2,1)S(1)}, u32[]{:S(2)}, u32[]{:S(2)}) %collective-permute-start.7) | collective-permute-done | bytes 131104 | tf_op jit(solution)/shard_map/ppermute | solution.py:347
  26.0 0.1 collective-permute-start.10
  26.1 2.6 %collective-permute-start.9 = (bf16[256,512]{1,0:T(8,128)(2,1)S(1)}, bf16[256,512]{1,0:T(8,128)(2,1)S(1)}, u32[]{:S(2)}, u32[]{:S(2)}) collective-permute-start(bf16[256,512]{1,0:T(8,128)(2,1)S(1)} %hold.1.refs_8_), channel_id=1, source_target_pairs={{0,4},{1,5},{2,6},{3,7},{4,0},{5,1},{6,2},{7,3},{8,12},{9,13},{10,... | collective-permute-start | bytes 786440 | tf_op jit(solution)/shard_map/ppermute | solution.py:347
  28.8 1.4 %collective-permute-start.8 = (bf16[256,512]{1,0:T(8,128)(2,1)S(1)}, bf16[256,512]{1,0:T(8,128)(2,1)S(1)}, u32[]{:S(2)}, u32[]{:S(2)}) collective-permute-start(bf16[256,512]{1,0:T(8,128)(2,1)S(1)} %hold.1.refs_8_), channel_id=1, source_target_pairs={{0,2},{1,3},{2,0},{3,1},{4,6},{5,7},{6,4},{7,5},{8,10},{9,11},{10,... | collective-permute-start | bytes 786440 | tf_op jit(solution)/shard_map/ppermute | solution.py:347
  30.2 1.3 %collective-permute-done.12.other = bf16[128,256]{1,0:T(8,128)(2,1)S(1)} collective-permute-done((bf16[128,256]{1,0:T(8,128)(2,1)S(1)}, bf16[128,256]{1,0:T(8,128)(2,1)S(1)}, u32[]{:S(2)}, u32[]{:S(2)}) %collective-permute-start.12) | collective-permute-done | bytes 65568 | tf_op jit(solution)/shard_map/ppermute | solution.py:351
  31.4 0.6 join.1
  32.0 5.9 %collective-permute-start.13 = (bf16[256,256]{1,0:T(8,128)(2,1)S(1)}, bf16[256,256]{1,0:T(8,128)(2,1)S(1)}, u32[]{:S(2)}, u32[]{:S(2)}) collective-permute-start(bf16[256,256]{1,0:T(8,128)(2,1)S(1)} %join.1), channel_id=1, source_target_pairs={{0,96},{8,168},{16,112},{24,184},{32,128},{40,200},{48,144},{56,21... | collective-permute-start | bytes 393224 | tf_op jit(solution)/shard_map/ppermute | solution.py:363
  37.9 0.6 collective-permute-start.11
  38.5 2.2 %copy-done.1 = bf16[512,4096]{1,0:T(8,128)(2,1)S(1)} copy-done((bf16[512,4096]{1,0:T(8,128)(2,1)S(1)}, bf16[512,4096]{1,0:T(8,128)(2,1)}, u32[]{:S(2)}) %copy-start.1) | copy-done | bytes 4194328
  40.7 5.4 %collective-permute-done.11.refs_16_.refs_3_.refs_5_ = bf16[128,256]{1,0:T(8,128)(2,1)S(1)} collective-permute-done((bf16[128,256]{1,0:T(8,128)(2,1)S(1)}, bf16[128,256]{1,0:T(8,128)(2,1)S(1)}, u32[]{:S(2)}, u32[]{:S(2)}) %collective-permute-start.11) | collective-permute-done | bytes 65568 | tf_op jit(solution)/shard_map/ppermute | solution.py:359
  46.1 2.8 %project.1 = (bf16[256,512]{1,0:T(8,128)(2,1)S(1)}, f32[8,128]{1,0:T(8,128)S(1)}) custom-call(s32[2]{0:T(128)S(1)} %pad_add_fusion.ids, bf16[128,512]{1,0:T(8,128)(2,1)S(1)} %copy-done.8, bf16[128,512]{1,0:T(8,128)(2,1)S(1)} %collective-permute-done.refs_1_.refs_3_, bf16[128,512]{1,0:T(8,128)(2,1)S(1)} %collective-permute-done.1.refs_2_.refs_4_, ...), custom_call_target="tpu_custom_call" | custom-call | flops 1073741824 | bytes 10485760 | tf_op jit(solution)/shard_map/project/pallas_call | solution.py:55
  48.9 3.1 %collective-permute-start.15 = (bf16[256,512]{1,0:T(8,128)(2,1)S(1)}, bf16[256,512]{1,0:T(8,128)(2,1)S(1)}, u32[]{:S(2)}, u32[]{:S(2)}) collective-permute-start(bf16[256,512]{1,0:T(8,128)(2,1)S(1)} %get-tuple-element.38.refs_0_), channel_id=1, source_target_pairs={{0,16},{8,24},{16,0},{24,8},{32,48},{40,56},{48,32},{56,40},{64,80... | collective-permute-start | bytes 786440 | tf_op jit(solution)/shard_map/ppermute | solution.py:351
  52.0 1.5 %collective-permute-start.18 = (bf16[256,256]{1,0:T(8,128)(2,1)S(1)}, bf16[256,256]{1,0:T(8,128)(2,1)S(1)}, u32[]{:S(2)}, u32[]{:S(2)}) collective-permute-start(bf16[256,256]{1,0:T(8,128)(2,1)S(1)} %join.1), channel_id=1, source_target_pairs={{0,64},{8,200},{16,80},{24,216},{32,96},{40,232},{48,112},{56,248}... | collective-permute-start | bytes 393224 | tf_op jit(solution)/shard_map/ppermute | solution.py:363
  53.6 2.8 %collective-permute-start.17 = (bf16[256,256]{1,0:T(8,128)(2,1)S(1)}, bf16[256,256]{1,0:T(8,128)(2,1)S(1)}, u32[]{:S(2)}, u32[]{:S(2)}) collective-permute-start(bf16[256,256]{1,0:T(8,128)(2,1)S(1)} %join.1), channel_id=1, source_target_pairs={{0,32},{8,232},{16,48},{24,248},{32,64},{40,8},{48,80},{56,24},{64... | collective-permute-start | bytes 393224 | tf_op jit(solution)/shard_map/ppermute | solution.py:363
  56.3 1.5 %collective-permute-done.15.refs_2_ = bf16[256,512]{1,0:T(8,128)(2,1)S(1)} collective-permute-done((bf16[256,512]{1,0:T(8,128)(2,1)S(1)}, bf16[256,512]{1,0:T(8,128)(2,1)S(1)}, u32[]{:S(2)}, u32[]{:S(2)}) %collective-permute-start.15) | collective-permute-done | bytes 262176 | tf_op jit(solution)/shard_map/ppermute | solution.py:351
  57.9 1.4 %collective-permute-done.18.refs_1_.refs_7_ = bf16[256,256]{1,0:T(8,128)(2,1)S(1)} collective-permute-done((bf16[256,256]{1,0:T(8,128)(2,1)S(1)}, bf16[256,256]{1,0:T(8,128)(2,1)S(1)}, u32[]{:S(2)}, u32[]{:S(2)}) %collective-permute-start.18) | collective-permute-done | bytes 131104 | tf_op jit(solution)/shard_map/ppermute | solution.py:363
  59.2 2.1 %collective-permute-done.17.refs_0_.refs_6_ = bf16[256,256]{1,0:T(8,128)(2,1)S(1)} collective-permute-done((bf16[256,256]{1,0:T(8,128)(2,1)S(1)}, bf16[256,256]{1,0:T(8,128)(2,1)S(1)}, u32[]{:S(2)}, u32[]{:S(2)}) %collective-permute-start.17) | collective-permute-done | bytes 131104 | tf_op jit(solution)/shard_map/ppermute | solution.py:363
  61.4 0.6 sort.1
  61.9 0.1 collective-permute-start.19
  62.0 1.4 %collective-permute-done.19.refs_9_ = bf16[384,256]{1,0:T(8,128)(2,1)S(1)} collective-permute-done((bf16[384,256]{1,0:T(8,128)(2,1)S(1)}, bf16[384,256]{1,0:T(8,128)(2,1)S(1)}, u32[]{:S(2)}, u32[]{:S(2)}) %collective-permute-start.19) | collective-permute-done | bytes 196640 | tf_op jit(solution)/shard_map/ppermute | solution.py:351
  63.5 4.7 %softmax.1 = (bf16[2048,1024]{1,0:T(8,128)(2,1)S(1)}, f32[128,128]{1,0:T(8,128)S(1)}, bf16[1024,128]{1,0:T(8,128)(2,1)S(1)}, bf16[1024,128]{1,0:T(8,128)(2,1)S(1)}) custom-call(s32[2]{0:T(128)S(1)} %pad_add_fusion.ids, s32[64]{0:T(128)S(1)} %copy-done.13, s32[8]{0:T(128)S(1)} %copy-done.14, bf16[256,512]{1,0:T(8,128)(2,1)S(1)} %get-tuple-element.38.refs_0_, ...), custom_call_target="tpu_custom_call" | custom-call | flops 1073741824 | bytes 6291456 | tf_op jit(solution)/shard_map/softmax/pallas_call | solution.py:55
  68.2 0.6 collective-permute-start.21
  68.8 5.3 %collective-permute-done.21.refs_9_ = f32[128,128]{1,0:T(8,128)S(1)} collective-permute-done((f32[128,128]{1,0:T(8,128)S(1)}, f32[128,128]{1,0:T(8,128)S(1)}, u32[]{:S(2)}, u32[]{:S(2)}) %collective-permute-start.21) | collective-permute-done | bytes 65568 | tf_op jit(solution)/shard_map/ppermute | solution.py:351
  74.1 1.2 %collective-permute-done.22.refs_10_ = f32[128,128]{1,0:T(8,128)S(1)} collective-permute-done((f32[128,128]{1,0:T(8,128)S(1)}, f32[128,128]{1,0:T(8,128)S(1)}, u32[]{:S(2)}, u32[]{:S(2)}) %collective-permute-start.22) | collective-permute-done | bytes 65568 | tf_op jit(solution)/shard_map/ppermute | solution.py:351
  75.3 4.1 %gradient.1 = (bf16[256,128]{1,0:T(8,128)(2,1)S(1)}, bf16[256,128]{1,0:T(8,128)(2,1)S(1)}, bf16[3,256,128]{2,1,0:T(8,128)(2,1)S(1)}, bf16[3,256,128]{2,1,0:T(8,1...) custom-call(bf16[256,512]{1,0:T(8,128)(2,1)S(1)} %get-tuple-element.38.refs_0_, ...), custom_call_target="tpu_custom_call" | custom-call | flops 2147483648 | bytes 6291456 | tf_op jit(solution)/shard_map/gradient/pallas_call | solution.py:55
  79.4 0.5 collective-permute-start.29
  79.9 0.4 collective-permute-start.24
  80.2 4.6 %collective-permute-start.23 = (bf16[256,128]{1,0:T(8,128)(2,1)S(1)}, bf16[256,128]{1,0:T(8,128)(2,1)S(1)}, u32[]{:S(2)}, u32[]{:S(2)}) collective-permute-start(bf16[256,128]{1,0:T(8,128)(2,1)S(1)} %get-tuple-element.43), channel_id=1, source_target_pairs={{0,128},{8,136},{16,144},{24,152},{32,160},{40,168},{48,176},{56,1... | collective-permute-start | bytes 196616 | tf_op jit(solution)/shard_map/ppermute | solution.py:359
  84.9 0.6 pair.1
  85.4 0.6 collective-permute-start.25
  86.1 0.5 collective-permute-start.26
  86.6 1.9 %collective-permute-start.27 = (bf16[2,256,128]{2,1,0:T(8,128)(2,1)S(1)}, bf16[2,256,128]{2,1,0:T(8,128)(2,1)S(1)}, u32[]{:S(2)}, u32[]{:S(2)}) collective-permute-start(bf16[2,256,128]{2,1,0:T(8,128)(2,1)S(1)} %get-tuple-element.48), channel_id=1, source_target_pairs={{0,160},{8,104},{16,176},{24,120},{32,192},{40,136},{48,208},{56,1... | collective-permute-start | bytes 393224 | tf_op jit(solution)/shard_map/ppermute | solution.py:363
  88.5 1.4 %collective-permute-done.23.refs_0_._ = bf16[256,128]{1,0:T(8,128)(2,1)S(1)} collective-permute-done((bf16[256,128]{1,0:T(8,128)(2,1)S(1)}, bf16[256,128]{1,0:T(8,128)(2,1)S(1)}, u32[]{:S(2)}, u32[]{:S(2)}) %collective-permute-start.23) | collective-permute-done | bytes 65568 | tf_op jit(solution)/shard_map/ppermute | solution.py:359
  89.9 0.5 collective-permute-start.30
  90.4 3.1 %collective-permute-done.25.refs_1_ = bf16[2,256,128]{2,1,0:T(8,128)(2,1)S(1)} collective-permute-done((bf16[2,256,128]{2,1,0:T(8,128)(2,1)S(1)}, bf16[2,256,128]{2,1,0:T(8,128)(2,1)S(1)}, u32[]{:S(2)}, u32[]{:S(2)}) %collective-permute-start.25) | collective-permute-done | bytes 131104 | tf_op jit(solution)/shard_map/ppermute | solution.py:363
  93.5 5.0 %collective-permute-done.27.refs_3_ = bf16[2,256,128]{2,1,0:T(8,128)(2,1)S(1)} collective-permute-done((bf16[2,256,128]{2,1,0:T(8,128)(2,1)S(1)}, bf16[2,256,128]{2,1,0:T(8,128)(2,1)S(1)}, u32[]{:S(2)}, u32[]{:S(2)}) %collective-permute-start.27) | collective-permute-done | bytes 131104 | tf_op jit(solution)/shard_map/ppermute | solution.py:363
  98.6 0.6 sum.1
  99.2 0.1 collective-permute-start.28
  99.3 1.5 %back_query.1.refs_11_ = f32[128,4096]{1,0:T(8,128)S(1)} custom-call(f32[128,512]{1,0:T(8,128)S(1)} %get-tuple-element.54.stay, bf16[128,512]{1,0:T(8,128)(2,1)S(1)} %collective-permute-done.30.got, bf16[4096,512]{1,0:T(8,128)(2,1)S(1)} %copy-done), custom_call_target="tpu_custom_call" | custom-call | flops 536870912 | bytes 6291456 | tf_op jit(solution)/shard_map/back_query/pallas_call | solution.py:55
  100.8 1.5 %back_kv.1 = (f32[128,512]{1,0:T(8,128)S(1)}, bf16[16,256]{1,0:T(8,128)(2,1)S(1)}, bf16[144,512]{1,0:T(8,128)(2,1)S(1)}, bf16[144,512]{1,0:T(8,128)(2,1)S(1)}, b...) custom-call(s32[2]{0:T(128)S(1)} %pad_add_fusion.ids, ...), custom_call_target="tpu_custom_call" | custom-call | flops 268435456 | bytes 7340032 | tf_op jit(solution)/shard_map/back_kv/pallas_call | solution.py:55
  102.3 0.7 collective-permute-start.31
  102.9 1.1 collective-permute-start.32
  104.1 0.4 collective-permute-start.33
  104.5 3.6 %collective-permute-start.34 = (bf16[144,512]{1,0:T(8,128)(2,1)S(1)}, bf16[144,512]{1,0:T(8,128)(2,1)S(1)}, u32[]{:S(2)}, u32[]{:S(2)}) collective-permute-start(bf16[144,512]{1,0:T(8,128)(2,1)S(1)} %get-tuple-element.61), channel_id=1, source_target_pairs={{0,5},{1,4},{2,7},{3,6},{4,1},{5,0},{6,3},{7,2},{8,13},{9,12},{10,... | collective-permute-start | bytes 442376 | tf_op jit(solution)/shard_map/ppermute | solution.py:347
  108.1 1.3 %collective-permute-start.35 = (bf16[144,512]{1,0:T(8,128)(2,1)S(1)}, bf16[144,512]{1,0:T(8,128)(2,1)S(1)}, u32[]{:S(2)}, u32[]{:S(2)}) collective-permute-start(bf16[144,512]{1,0:T(8,128)(2,1)S(1)} %get-tuple-element.62), channel_id=1, source_target_pairs={{0,3},{1,2},{2,1},{3,0},{4,7},{5,6},{6,5},{7,4},{8,11},{9,10},{10,... | collective-permute-start | bytes 442376 | tf_op jit(solution)/shard_map/ppermute | solution.py:347
  109.5 0.2 collective-permute-done.32.refs_1_
  109.6 3.9 %collective-permute-start.37 = (bf16[144,512]{1,0:T(8,128)(2,1)S(1)}, bf16[144,512]{1,0:T(8,128)(2,1)S(1)}, u32[]{:S(2)}, u32[]{:S(2)}) collective-permute-start(bf16[144,512]{1,0:T(8,128)(2,1)S(1)} %get-tuple-element.64), channel_id=1, source_target_pairs={{0,7},{1,6},{2,5},{3,4},{4,3},{5,2},{6,1},{7,0},{8,15},{9,14},{10,... | collective-permute-start | bytes 442376 | tf_op jit(solution)/shard_map/ppermute | solution.py:347
  113.5 5.6 %collective-permute-done.33.refs_2_ = bf16[144,512]{1,0:T(8,128)(2,1)S(1)} collective-permute-done((bf16[144,512]{1,0:T(8,128)(2,1)S(1)}, bf16[144,512]{1,0:T(8,128)(2,1)S(1)}, u32[]{:S(2)}, u32[]{:S(2)}) %collective-permute-start.33) | collective-permute-done | bytes 147488 | tf_op jit(solution)/shard_map/ppermute | solution.py:347
  119.1 2.6 %collective-permute-done.36.refs_5_ = bf16[144,512]{1,0:T(8,128)(2,1)S(1)} collective-permute-done((bf16[144,512]{1,0:T(8,128)(2,1)S(1)}, bf16[144,512]{1,0:T(8,128)(2,1)S(1)}, u32[]{:S(2)}, u32[]{:S(2)}) %collective-permute-start.36) | collective-permute-done | bytes 147488 | tf_op jit(solution)/shard_map/ppermute | solution.py:347
  121.7 1.5 %last.1 = (bf16[128,512]{1,0:T(8,128)(2,1)}, f32[1,128]{1,0:T(1,128)}) custom-call(s32[2]{0:T(128)S(1)} %pad_add_fusion.ids, f32[128,512]{1,0:T(8,128)S(1)} %get-tuple-element.56.own, bf16[16,256]{1,0:T(8,128)(2,1)S(1)} %get-tuple-element.57.own_row, bf16[144,512]{1,0:T(8,128)(2,1)S(1)} %collective-permute-done.31.refs_0_, ...), custom_call_target="tpu_custom_call" | custom-call | flops 655360 | bytes 3145728 | tf_op jit(solution)/shard_map/last/pallas_call | solution.py:55
  (59 shorter events, 0.4 us)
Async XLA Ops:
  0.6 8.0 %collective-permute-start.6 = (bf16[128,512]{1,0:T(8,128)(2,1)}, bf16[128,512]{1,0:T(8,128)(2,1)S(1)}, u32[]{:S(2)}, u32[]{:S(2)}) collective-permute-start(bf16[128,512]{1,0:T(8,128)(2,1)} %refs_7_.1), channel_id=1, source_target_pairs={{0,1},{1,0},{2,3},{3,2},{4,5},{5,4},{6,7},{7,6},{8,9},{9,8},{10,11... | collective-permute-start | bytes 393224 | tf_op jit(solution)/shard_map/ppermute | solution.py:347
  2.2 9.5 %collective-permute-start.5 = (bf16[128,512]{1,0:T(8,128)(2,1)}, bf16[128,512]{1,0:T(8,128)(2,1)S(1)}, u32[]{:S(2)}, u32[]{:S(2)}) collective-permute-start(bf16[128,512]{1,0:T(8,128)(2,1)} %refs_7_.1), channel_id=1, source_target_pairs={{0,2},{1,3},{2,0},{3,1},{4,6},{5,7},{6,4},{7,5},{8,10},{9,11},{10,... | collective-permute-start | bytes 393224 | tf_op jit(solution)/shard_map/ppermute | solution.py:347
  3.8 17.2 %collective-permute-start.4 = (bf16[128,512]{1,0:T(8,128)(2,1)}, bf16[128,512]{1,0:T(8,128)(2,1)S(1)}, u32[]{:S(2)}, u32[]{:S(2)}) collective-permute-start(bf16[128,512]{1,0:T(8,128)(2,1)} %refs_7_.1), channel_id=1, source_target_pairs={{0,4},{1,5},{2,6},{3,7},{4,0},{5,1},{6,2},{7,3},{8,12},{9,13},{10,... | collective-permute-start | bytes 393224 | tf_op jit(solution)/shard_map/ppermute | solution.py:347
  6.7 15.9 %collective-permute-start.3 = (bf16[128,512]{1,0:T(8,128)(2,1)}, bf16[128,512]{1,0:T(8,128)(2,1)S(1)}, u32[]{:S(2)}, u32[]{:S(2)}) collective-permute-start(bf16[128,512]{1,0:T(8,128)(2,1)} %refs_7_.1), channel_id=1, source_target_pairs={{0,5},{1,4},{2,7},{3,6},{4,1},{5,0},{6,3},{7,2},{8,13},{9,12},{10,... | collective-permute-start | bytes 393224 | tf_op jit(solution)/shard_map/ppermute | solution.py:347
  7.3 15.3 %collective-permute-start.2 = (bf16[128,512]{1,0:T(8,128)(2,1)}, bf16[128,512]{1,0:T(8,128)(2,1)S(1)}, u32[]{:S(2)}, u32[]{:S(2)}) collective-permute-start(bf16[128,512]{1,0:T(8,128)(2,1)} %refs_7_.1), channel_id=1, source_target_pairs={{0,3},{1,2},{2,1},{3,0},{4,7},{5,6},{6,5},{7,4},{8,11},{9,10},{10,... | collective-permute-start | bytes 393224 | tf_op jit(solution)/shard_map/ppermute | solution.py:347
  8.7 13.9 %collective-permute-start.1 = (bf16[128,512]{1,0:T(8,128)(2,1)}, bf16[128,512]{1,0:T(8,128)(2,1)S(1)}, u32[]{:S(2)}, u32[]{:S(2)}) collective-permute-start(bf16[128,512]{1,0:T(8,128)(2,1)} %refs_7_.1), channel_id=1, source_target_pairs={{0,6},{1,7},{2,4},{3,5},{4,2},{5,3},{6,0},{7,1},{8,14},{9,15},{10,... | collective-permute-start | bytes 393224 | tf_op jit(solution)/shard_map/ppermute | solution.py:347
  11.7 10.9 %collective-permute-start = (bf16[128,512]{1,0:T(8,128)(2,1)}, bf16[128,512]{1,0:T(8,128)(2,1)S(1)}, u32[]{:S(2)}, u32[]{:S(2)}) collective-permute-start(bf16[128,512]{1,0:T(8,128)(2,1)} %refs_7_.1), channel_id=1, source_target_pairs={{0,7},{1,6},{2,5},{3,4},{4,3},{5,2},{6,1},{7,0},{8,15},{9,14},{10,... | collective-permute-start | bytes 393224 | tf_op jit(solution)/shard_map/ppermute | solution.py:347
  15.7 0.9 copy-start.9
  16.6 21.9 %copy-start = (bf16[4096,512]{1,0:T(8,128)(2,1)S(1)}, bf16[4096,512]{1,0:T(8,128)(2,1)}, u32[]{:S(2)}) copy-start(bf16[4096,512]{1,0:T(8,128)(2,1)} %w_query.1) | copy-start | bytes 12582916
  16.6 1.4 %copy-start.3 = (bf16[4096,128]{1,0:T(8,128)(2,1)S(1)}, bf16[4096,128]{1,0:T(8,128)(2,1)}, u32[]{:S(2)}) copy-start(bf16[4096,128]{1,0:T(8,128)(2,1)} %refs_12_.3) | copy-start | bytes 3145732
  18.0 1.4 %copy-start.5 = (bf16[4096,128]{1,0:T(8,128)(2,1)S(1)}, bf16[4096,128]{1,0:T(8,128)(2,1)}, u32[]{:S(2)}) copy-start(bf16[4096,128]{1,0:T(8,128)(2,1)} %refs_13_.1) | copy-start | bytes 3145732
  19.4 0.9 copy-start.7
  20.3 0.7 copy-start.11
  21.0 5.0 %collective-permute-start.7 = (bf16[128,512]{1,0:T(8,128)(2,1)S(1)}, bf16[128,512]{1,0:T(8,128)(2,1)S(1)}, u32[]{:S(2)}, u32[]{:S(2)}) collective-permute-start(bf16[128,512]{1,0:T(8,128)(2,1)S(1)} %copy.12.own), channel_id=1, source_target_pairs={{0,1},{1,0},{2,3},{3,2},{4,5},{5,4},{6,7},{7,6},{8,9},{9,8},{10,11... | collective-permute-start | bytes 393224 | tf_op jit(solution)/shard_map/ppermute | solution.py:347
  26.0 20.1 %collective-permute-start.10 = (bf16[256,512]{1,0:T(8,128)(2,1)S(1)}, bf16[256,512]{1,0:T(8,128)(2,1)S(1)}, u32[]{:S(2)}, u32[]{:S(2)}) collective-permute-start(bf16[256,512]{1,0:T(8,128)(2,1)S(1)} %hold.1.refs_8_), channel_id=1, source_target_pairs={{0,6},{1,7},{2,4},{3,5},{4,2},{5,3},{6,0},{7,1},{8,14},{9,15},{10,... | collective-permute-start | bytes 786440 | tf_op jit(solution)/shard_map/ppermute | solution.py:347
  26.1 20.0 %collective-permute-start.9 = (bf16[256,512]{1,0:T(8,128)(2,1)S(1)}, bf16[256,512]{1,0:T(8,128)(2,1)S(1)}, u32[]{:S(2)}, u32[]{:S(2)}) collective-permute-start(bf16[256,512]{1,0:T(8,128)(2,1)S(1)} %hold.1.refs_8_), channel_id=1, source_target_pairs={{0,4},{1,5},{2,6},{3,7},{4,0},{5,1},{6,2},{7,3},{8,12},{9,13},{10,... | collective-permute-start | bytes 786440 | tf_op jit(solution)/shard_map/ppermute | solution.py:347
  28.8 17.4 %collective-permute-start.8 = (bf16[256,512]{1,0:T(8,128)(2,1)S(1)}, bf16[256,512]{1,0:T(8,128)(2,1)S(1)}, u32[]{:S(2)}, u32[]{:S(2)}) collective-permute-start(bf16[256,512]{1,0:T(8,128)(2,1)S(1)} %hold.1.refs_8_), channel_id=1, source_target_pairs={{0,2},{1,3},{2,0},{3,1},{4,6},{5,7},{6,4},{7,5},{8,10},{9,11},{10,... | collective-permute-start | bytes 786440 | tf_op jit(solution)/shard_map/ppermute | solution.py:347
  30.2 1.3 %collective-permute-start.12 = (bf16[128,256]{1,0:T(8,128)(2,1)S(1)}, bf16[128,256]{1,0:T(8,128)(2,1)S(1)}, u32[]{:S(2)}, u32[]{:S(2)}) collective-permute-start(bf16[128,256]{1,0:T(8,128)(2,1)S(1)} %get-tuple-element.36.refs_0_.mine.refs_4_), channel_id=1, source_target_pairs={{0,8},{8,0},{16,24},{24,16},{32,40},{40,32},{48,56},{56,48},{64,72... | collective-permute-start | bytes 196616 | tf_op jit(solution)/shard_map/ppermute | solution.py:351
  32.0 14.1 %collective-permute-start.13 = (bf16[256,256]{1,0:T(8,128)(2,1)S(1)}, bf16[256,256]{1,0:T(8,128)(2,1)S(1)}, u32[]{:S(2)}, u32[]{:S(2)}) collective-permute-start(bf16[256,256]{1,0:T(8,128)(2,1)S(1)} %join.1), channel_id=1, source_target_pairs={{0,96},{8,168},{16,112},{24,184},{32,128},{40,200},{48,144},{56,21... | collective-permute-start | bytes 393224 | tf_op jit(solution)/shard_map/ppermute | solution.py:363
  37.9 8.2 %collective-permute-start.11 = (bf16[128,256]{1,0:T(8,128)(2,1)S(1)}, bf16[128,256]{1,0:T(8,128)(2,1)S(1)}, u32[]{:S(2)}, u32[]{:S(2)}) collective-permute-start(bf16[128,256]{1,0:T(8,128)(2,1)S(1)} %get-tuple-element.36.refs_0_.mine.refs_4_), channel_id=1, source_target_pairs={{0,128},{8,136},{16,144},{24,152},{32,160},{40,168},{48,176},{56,1... | collective-permute-start | bytes 196616 | tf_op jit(solution)/shard_map/ppermute | solution.py:359
  38.5 2.2 %copy-start.1 = (bf16[512,4096]{1,0:T(8,128)(2,1)S(1)}, bf16[512,4096]{1,0:T(8,128)(2,1)}, u32[]{:S(2)}) copy-start(bf16[512,4096]{1,0:T(8,128)(2,1)} %refs_12_.2) | copy-start | bytes 12582916
  40.7 5.5 %copy-start.2 = (bf16[512,4096]{1,0:T(8,128)(2,1)S(1)}, bf16[512,4096]{1,0:T(8,128)(2,1)}, u32[]{:S(2)}) copy-start(bf16[512,4096]{1,0:T(8,128)(2,1)} %refs_12_.2) | copy-start | bytes 12582916
  40.7 5.5 %copy-start.8 = (bf16[128,512]{1,0:T(8,128)(2,1)S(1)}, bf16[128,512]{1,0:T(8,128)(2,1)}, u32[]{:S(2)}) copy-start(bf16[128,512]{1,0:T(8,128)(2,1)} %refs_7_.1) | copy-start | bytes 393220
  40.7 22.8 %copy-start.13 = (s32[64]{0:T(128)S(1)}, s32[64]{0:T(128)}, u32[]{:S(2)}) copy-start(s32[64]{0:T(128)} %order.1) | copy-start | bytes 772
  40.7 22.8 %copy-start.14 = (s32[8]{0:T(128)S(1)}, s32[8]{0:T(128)}, u32[]{:S(2)}) copy-start(s32[8]{0:T(128)} %lengths.1) | copy-start | bytes 100
  48.9 8.9 %collective-permute-start.15 = (bf16[256,512]{1,0:T(8,128)(2,1)S(1)}, bf16[256,512]{1,0:T(8,128)(2,1)S(1)}, u32[]{:S(2)}, u32[]{:S(2)}) collective-permute-start(bf16[256,512]{1,0:T(8,128)(2,1)S(1)} %get-tuple-element.38.refs_0_), channel_id=1, source_target_pairs={{0,16},{8,24},{16,0},{24,8},{32,48},{40,56},{48,32},{56,40},{64,80... | collective-permute-start | bytes 786440 | tf_op jit(solution)/shard_map/ppermute | solution.py:351
  52.0 7.2 %collective-permute-start.18 = (bf16[256,256]{1,0:T(8,128)(2,1)S(1)}, bf16[256,256]{1,0:T(8,128)(2,1)S(1)}, u32[]{:S(2)}, u32[]{:S(2)}) collective-permute-start(bf16[256,256]{1,0:T(8,128)(2,1)S(1)} %join.1), channel_id=1, source_target_pairs={{0,64},{8,200},{16,80},{24,216},{32,96},{40,232},{48,112},{56,248}... | collective-permute-start | bytes 393224 | tf_op jit(solution)/shard_map/ppermute | solution.py:363
  53.6 7.8 %collective-permute-start.17 = (bf16[256,256]{1,0:T(8,128)(2,1)S(1)}, bf16[256,256]{1,0:T(8,128)(2,1)S(1)}, u32[]{:S(2)}, u32[]{:S(2)}) collective-permute-start(bf16[256,256]{1,0:T(8,128)(2,1)S(1)} %join.1), channel_id=1, source_target_pairs={{0,32},{8,232},{16,48},{24,248},{32,64},{40,8},{48,80},{56,24},{64... | collective-permute-start | bytes 393224 | tf_op jit(solution)/shard_map/ppermute | solution.py:363
  56.3 7.1 %collective-permute-start.14 = (bf16[256,512]{1,0:T(8,128)(2,1)S(1)}, bf16[256,512]{1,0:T(8,128)(2,1)S(1)}, u32[]{:S(2)}, u32[]{:S(2)}) collective-permute-start(bf16[256,512]{1,0:T(8,128)(2,1)S(1)} %get-tuple-element.38.refs_0_), channel_id=1, source_target_pairs={{0,8},{8,0},{16,24},{24,16},{32,40},{40,32},{48,56},{56,48},{64,72... | collective-permute-start | bytes 786440 | tf_op jit(solution)/shard_map/ppermute | solution.py:351
  57.9 5.6 %collective-permute-start.16 = (bf16[256,512]{1,0:T(8,128)(2,1)S(1)}, bf16[256,512]{1,0:T(8,128)(2,1)S(1)}, u32[]{:S(2)}, u32[]{:S(2)}) collective-permute-start(bf16[256,512]{1,0:T(8,128)(2,1)S(1)} %collective-permute-done.15.refs_2_), channel_id=1, source_target_pairs={{0,8},{8,0},{16,24},{24,16},{32,40},{40,32},{48,56},{56,48},{64,72... | collective-permute-start | bytes 786440 | tf_op jit(solution)/shard_map/ppermute | solution.py:351
  61.9 1.5 %collective-permute-start.19 = (bf16[384,256]{1,0:T(8,128)(2,1)S(1)}, bf16[384,256]{1,0:T(8,128)(2,1)S(1)}, u32[]{:S(2)}, u32[]{:S(2)}) collective-permute-start(bf16[384,256]{1,0:T(8,128)(2,1)S(1)} %sort.1), channel_id=1, source_target_pairs={{0,8},{8,0},{16,24},{24,16},{32,40},{40,32},{48,56},{56,48},{64,72... | collective-permute-start | bytes 589832 | tf_op jit(solution)/shard_map/ppermute | solution.py:351
  68.2 5.8 %collective-permute-start.21 = (f32[128,128]{1,0:T(8,128)S(1)}, f32[128,128]{1,0:T(8,128)S(1)}, u32[]{:S(2)}, u32[]{:S(2)}) collective-permute-start(f32[128,128]{1,0:T(8,128)S(1)} %get-tuple-element.42.refs_7_), channel_id=1, source_target_pairs={{0,16},{8,24},{16,0},{24,8},{32,48},{40,56},{48,32},{56,40},{64,80... | collective-permute-start | bytes 196616 | tf_op jit(solution)/shard_map/ppermute | solution.py:351
  68.8 5.3 %collective-permute-start.20 = (f32[128,128]{1,0:T(8,128)S(1)}, f32[128,128]{1,0:T(8,128)S(1)}, u32[]{:S(2)}, u32[]{:S(2)}) collective-permute-start(f32[128,128]{1,0:T(8,128)S(1)} %get-tuple-element.42.refs_7_), channel_id=1, source_target_pairs={{0,8},{8,0},{16,24},{24,16},{32,40},{40,32},{48,56},{56,48},{64,72... | collective-permute-start | bytes 196616 | tf_op jit(solution)/shard_map/ppermute | solution.py:351
  74.1 1.3 %collective-permute-start.22 = (f32[128,128]{1,0:T(8,128)S(1)}, f32[128,128]{1,0:T(8,128)S(1)}, u32[]{:S(2)}, u32[]{:S(2)}) collective-permute-start(f32[128,128]{1,0:T(8,128)S(1)} %collective-permute-done.21.refs_9_), channel_id=1, source_target_pairs={{0,8},{8,0},{16,24},{24,16},{32,40},{40,32},{48,56},{56,48},{64,72... | collective-permute-start | bytes 196616 | tf_op jit(solution)/shard_map/ppermute | solution.py:351
  79.4 10.5 %collective-permute-start.29 = (bf16[256,512]{1,0:T(8,128)(2,1)S(1)}, bf16[256,512]{1,0:T(8,128)(2,1)S(1)}, u32[]{:S(2)}, u32[]{:S(2)}) collective-permute-start(bf16[256,512]{1,0:T(8,128)(2,1)S(1)} %get-tuple-element.53), channel_id=1, source_target_pairs={{0,8},{8,0},{16,24},{24,16},{32,40},{40,32},{48,56},{56,48},{64,72... | collective-permute-start | bytes 786440 | tf_op jit(solution)/shard_map/ppermute | solution.py:351
  79.9 5.0 %collective-permute-start.24 = (bf16[3,256,128]{2,1,0:T(8,128)(2,1)S(1)}, bf16[3,256,128]{2,1,0:T(8,128)(2,1)S(1)}, u32[]{:S(2)}, u32[]{:S(2)}) collective-permute-start(bf16[3,256,128]{2,1,0:T(8,128)(2,1)S(1)} %get-tuple-element.45), channel_id=1, source_target_pairs={{0,8},{8,0},{16,24},{24,16},{32,40},{40,32},{48,56},{56,48},{64,72... | collective-permute-start | bytes 589832 | tf_op jit(solution)/shard_map/ppermute | solution.py:351
  80.2 9.7 %collective-permute-start.23 = (bf16[256,128]{1,0:T(8,128)(2,1)S(1)}, bf16[256,128]{1,0:T(8,128)(2,1)S(1)}, u32[]{:S(2)}, u32[]{:S(2)}) collective-permute-start(bf16[256,128]{1,0:T(8,128)(2,1)S(1)} %get-tuple-element.43), channel_id=1, source_target_pairs={{0,128},{8,136},{16,144},{24,152},{32,160},{40,168},{48,176},{56,1... | collective-permute-start | bytes 196616 | tf_op jit(solution)/shard_map/ppermute | solution.py:359
  84.8 15.9 %copy-start.4 = (bf16[4096,128]{1,0:T(8,128)(2,1)S(1)}, bf16[4096,128]{1,0:T(8,128)(2,1)}, u32[]{:S(2)}) copy-start(bf16[4096,128]{1,0:T(8,128)(2,1)} %refs_12_.3) | copy-start | bytes 3145732
  84.9 15.9 %copy-start.6 = (bf16[4096,128]{1,0:T(8,128)(2,1)S(1)}, bf16[4096,128]{1,0:T(8,128)(2,1)}, u32[]{:S(2)}) copy-start(bf16[4096,128]{1,0:T(8,128)(2,1)} %refs_13_.1) | copy-start | bytes 3145732
  84.9 16.0 %copy-start.12 = (f32[4096]{0:T(1024)S(1)}, f32[4096]{0:T(1024)}, u32[]{:S(2)}) copy-start(f32[4096]{0:T(1024)} %param.11) | copy-start | bytes 49156
  85.4 8.1 %collective-permute-start.25 = (bf16[2,256,128]{2,1,0:T(8,128)(2,1)S(1)}, bf16[2,256,128]{2,1,0:T(8,128)(2,1)S(1)}, u32[]{:S(2)}, u32[]{:S(2)}) collective-permute-start(bf16[2,256,128]{2,1,0:T(8,128)(2,1)S(1)} %get-tuple-element.46), channel_id=1, source_target_pairs={{0,224},{8,40},{16,240},{24,56},{32,0},{40,72},{48,16},{56,88},{64... | collective-permute-start | bytes 393224 | tf_op jit(solution)/shard_map/ppermute | solution.py:363
  86.1 7.5 %collective-permute-start.26 = (bf16[2,256,128]{2,1,0:T(8,128)(2,1)S(1)}, bf16[2,256,128]{2,1,0:T(8,128)(2,1)S(1)}, u32[]{:S(2)}, u32[]{:S(2)}) collective-permute-start(bf16[2,256,128]{2,1,0:T(8,128)(2,1)S(1)} %get-tuple-element.47), channel_id=1, source_target_pairs={{0,192},{8,72},{16,208},{24,88},{32,224},{40,104},{48,240},{56,120... | collective-permute-start | bytes 393224 | tf_op jit(solution)/shard_map/ppermute | solution.py:363
  86.6 12.0 %collective-permute-start.27 = (bf16[2,256,128]{2,1,0:T(8,128)(2,1)S(1)}, bf16[2,256,128]{2,1,0:T(8,128)(2,1)S(1)}, u32[]{:S(2)}, u32[]{:S(2)}) collective-permute-start(bf16[2,256,128]{2,1,0:T(8,128)(2,1)S(1)} %get-tuple-element.48), channel_id=1, source_target_pairs={{0,160},{8,104},{16,176},{24,120},{32,192},{40,136},{48,208},{56,1... | collective-permute-start | bytes 393224 | tf_op jit(solution)/shard_map/ppermute | solution.py:363
  89.9 9.3 %collective-permute-start.30 = (bf16[128,512]{1,0:T(8,128)(2,1)S(1)}, bf16[128,512]{1,0:T(8,128)(2,1)S(1)}, u32[]{:S(2)}, u32[]{:S(2)}) collective-permute-start(bf16[128,512]{1,0:T(8,128)(2,1)S(1)} %get-tuple-element.55), channel_id=1, source_target_pairs={{0,16},{8,24},{16,0},{24,8},{32,48},{40,56},{48,32},{56,40},{64,80... | collective-permute-start | bytes 393224 | tf_op jit(solution)/shard_map/ppermute | solution.py:351
  99.2 1.6 %collective-permute-start.28 = (bf16[256,128]{1,0:T(8,128)(2,1)S(1)}, bf16[256,128]{1,0:T(8,128)(2,1)S(1)}, u32[]{:S(2)}, u32[]{:S(2)}) collective-permute-start(bf16[256,128]{1,0:T(8,128)(2,1)S(1)} %get-tuple-element.51), channel_id=1, source_target_pairs={{0,8},{8,0},{16,24},{24,16},{32,40},{40,32},{48,56},{56,48},{64,72... | collective-permute-start | bytes 196616 | tf_op jit(solution)/shard_map/ppermute | solution.py:351
  100.8 20.9 %copy-start.10 = (bf16[128,512]{1,0:T(8,128)(2,1)S(1)}, bf16[128,512]{1,0:T(8,128)(2,1)}, u32[]{:S(2)}) copy-start(bf16[128,512]{1,0:T(8,128)(2,1)} %refs_8_.1) | copy-start | bytes 393220
  102.3 7.1 %collective-permute-start.31 = (bf16[144,512]{1,0:T(8,128)(2,1)S(1)}, bf16[144,512]{1,0:T(8,128)(2,1)S(1)}, u32[]{:S(2)}, u32[]{:S(2)}) collective-permute-start(bf16[144,512]{1,0:T(8,128)(2,1)S(1)} %get-tuple-element.58), channel_id=1, source_target_pairs={{0,1},{1,0},{2,3},{3,2},{4,5},{5,4},{6,7},{7,6},{8,9},{9,8},{10,11... | collective-permute-start | bytes 442376 | tf_op jit(solution)/shard_map/ppermute | solution.py:347
  102.9 6.7 %collective-permute-start.32 = (bf16[144,512]{1,0:T(8,128)(2,1)S(1)}, bf16[144,512]{1,0:T(8,128)(2,1)S(1)}, u32[]{:S(2)}, u32[]{:S(2)}) collective-permute-start(bf16[144,512]{1,0:T(8,128)(2,1)S(1)} %get-tuple-element.59), channel_id=1, source_target_pairs={{0,2},{1,3},{2,0},{3,1},{4,6},{5,7},{6,4},{7,5},{8,10},{9,11},{10,... | collective-permute-start | bytes 442376 | tf_op jit(solution)/shard_map/ppermute | solution.py:347
  104.1 15.0 %collective-permute-start.33 = (bf16[144,512]{1,0:T(8,128)(2,1)S(1)}, bf16[144,512]{1,0:T(8,128)(2,1)S(1)}, u32[]{:S(2)}, u32[]{:S(2)}) collective-permute-start(bf16[144,512]{1,0:T(8,128)(2,1)S(1)} %get-tuple-element.60), channel_id=1, source_target_pairs={{0,4},{1,5},{2,6},{3,7},{4,0},{5,1},{6,2},{7,3},{8,12},{9,13},{10,... | collective-permute-start | bytes 442376 | tf_op jit(solution)/shard_map/ppermute | solution.py:347
  104.5 14.6 %collective-permute-start.34 = (bf16[144,512]{1,0:T(8,128)(2,1)S(1)}, bf16[144,512]{1,0:T(8,128)(2,1)S(1)}, u32[]{:S(2)}, u32[]{:S(2)}) collective-permute-start(bf16[144,512]{1,0:T(8,128)(2,1)S(1)} %get-tuple-element.61), channel_id=1, source_target_pairs={{0,5},{1,4},{2,7},{3,6},{4,1},{5,0},{6,3},{7,2},{8,13},{9,12},{10,... | collective-permute-start | bytes 442376 | tf_op jit(solution)/shard_map/ppermute | solution.py:347
  108.1 11.0 %collective-permute-start.35 = (bf16[144,512]{1,0:T(8,128)(2,1)S(1)}, bf16[144,512]{1,0:T(8,128)(2,1)S(1)}, u32[]{:S(2)}, u32[]{:S(2)}) collective-permute-start(bf16[144,512]{1,0:T(8,128)(2,1)S(1)} %get-tuple-element.62), channel_id=1, source_target_pairs={{0,3},{1,2},{2,1},{3,0},{4,7},{5,6},{6,5},{7,4},{8,11},{9,10},{10,... | collective-permute-start | bytes 442376 | tf_op jit(solution)/shard_map/ppermute | solution.py:347
  109.4 12.2 %collective-permute-start.36 = (bf16[144,512]{1,0:T(8,128)(2,1)S(1)}, bf16[144,512]{1,0:T(8,128)(2,1)S(1)}, u32[]{:S(2)}, u32[]{:S(2)}) collective-permute-start(bf16[144,512]{1,0:T(8,128)(2,1)S(1)} %get-tuple-element.63), channel_id=1, source_target_pairs={{0,6},{1,7},{2,4},{3,5},{4,2},{5,3},{6,0},{7,1},{8,14},{9,15},{10,... | collective-permute-start | bytes 442376 | tf_op jit(solution)/shard_map/ppermute | solution.py:347
  109.6 12.0 %collective-permute-start.37 = (bf16[144,512]{1,0:T(8,128)(2,1)S(1)}, bf16[144,512]{1,0:T(8,128)(2,1)S(1)}, u32[]{:S(2)}, u32[]{:S(2)}) collective-permute-start(bf16[144,512]{1,0:T(8,128)(2,1)S(1)} %get-tuple-element.64), channel_id=1, source_target_pairs={{0,7},{1,6},{2,5},{3,4},{4,3},{5,2},{6,1},{7,0},{8,15},{9,14},{10,... | collective-permute-start | bytes 442376 | tf_op jit(solution)/shard_map/ppermute | solution.py:347
